TPU v7x, 128 devices: a whole 4x4x4 slice. The times are simulated.
128 devices in a mesh: dp: 8 (over y, z_hi), dap: 16 (over x, z_lo, core).
Axes of the slice: x: 4, y: 4, z: 4 (z_hi: 2, z_lo: 2; z = z_hi * 2 + z_lo), core: 2. Of those that a mesh axis runs over, the one named last changes fastest.
Arguments:
- homolog_features: bfloat16 [8, 192, 192, 64], P('dp', None, 'dap'), may hold values from -6 to 6
- edge_features: bfloat16 [8, 192, 192, 128], P('dp', 'dap'), may hold values from -6 to 6
- adjoint_edges: bfloat16 [8, 192, 192, 128], P('dp', 'dap'), may hold values from -6 to 6
- homolog_scaling_factor: float32 [64], replicated, may hold values from 0.1 to 1.9
- tensor_mapping_matrix: bfloat16 [64, 64], replicated, may hold values from -0.75 to 0.75
- tensor_final_matrix: bfloat16 [1024, 128], replicated, may hold values from -2.5 to 2.5
- tensor_final_offset: float32 [128], replicated, may hold values from -3 to 3
- edge_scaling_factor: float32 [128], replicated, may hold values from 0.1 to 1.9
- trilateral_entry_matrix: bfloat16 [128, 512], replicated, may hold values from -0.5 to 0.5
- final_sigmoid_matrix: bfloat16 [128, 128], replicated, may hold values from -0.5 to 0.5
- central_scaling_factor: float32 [128], replicated, may hold values from 0.1 to 1.9
- trilateral_final_matrix: bfloat16 [128, 128], replicated, may hold values from -0.5 to 0.5
Outputs:
- pair_out: bfloat16 [8, 192, 192, 128], P('dp', 'dap')
- pair_input_gradient: bfloat16 [8, 192, 192, 128], P('dp', 'dap')
- homolog_sensitivity: bfloat16 [8, 192, 192, 64], P('dp', None, 'dap')
- opm_gain_grad: float32 [64], replicated
- opm_proj_grad: float32 [64, 64], replicated
- opm_out_grad: float32 [1024, 128], replicated
- opm_bias_grad: float32 [128], replicated
- tri_gain_grad: float32 [128], replicated
- tri_in_grad: float32 [128, 512], replicated
- tri_gate_grad: float32 [128, 128], replicated
- mid_gain_grad: float32 [128], replicated
- tri_out_grad: float32 [128, 128], replicated
All inputs are finite; a program needn't handle non-finite values.
Results may differ from a plain program's by a relative error of at most 0.025.
Values may be sent and summed in bfloat16 or wider, within the bound.
No kernel may reach another device: no remote copies, remote signals or barrier semaphores. Data moves between devices by JAX's collectives and lax.ppermute only.
A program may use at most 192 MiB of HBM per device.

v0:
```python
import jax
import jax.numpy as jnp
from jax import lax
from jax.sharding import PartitionSpec as P

EPSILON = 1e-05


def layer_norm_forward(values):
    centred = values - jnp.mean(values, -1, keepdims=True)
    inverse = lax.rsqrt(jnp.mean(centred * centred, -1, keepdims=True) + EPSILON)
    return (centred * inverse, inverse)


def standardize_adjoint(grad_hat, normed, inverse):
    first = jnp.mean(grad_hat, -1, keepdims=True)
    second = jnp.mean(grad_hat * normed, -1, keepdims=True)
    return (grad_hat - first - normed * second) * inverse


def trilateral_contraction(form, left, right):
    return jnp.einsum(form, left, right, preferred_element_type=jnp.float32)


def local(
    homolog_features,
    edge_features,
    adjoint_edges,
    homolog_scaling_factor,
    tensor_mapping_matrix,
    tensor_final_matrix,
    tensor_final_offset,
    edge_scaling_factor,
    trilateral_entry_matrix,
    final_sigmoid_matrix,
    central_scaling_factor,
    trilateral_final_matrix,
):
    homolog_lines = homolog_features[0]
    opm_half = tensor_mapping_matrix.shape[1] // 2
    width = trilateral_final_matrix.shape[0]
    sequence_depth = homolog_lines.shape[0]
    local_rows = edge_features.shape[1]
    length = edge_features.shape[2]
    homolog_standardized, homolog_reciprocal_spread = layer_norm_forward(
        homolog_lines.astype(jnp.float32)
    )
    alignment_normalized = (homolog_standardized * homolog_scaling_factor).astype(jnp.bfloat16)
    projected_pairs = trilateral_contraction(
        "zft,tr->zfr", alignment_normalized, tensor_mapping_matrix
    ).astype(jnp.bfloat16)
    left_projection_rows = projected_pairs[..., :opm_half]
    right_projection_rows = projected_pairs[..., opm_half:]
    crop_fragment = lax.all_gather(right_projection_rows, "dap", axis=1, tiled=True)
    outer_product_block = (
        trilateral_contraction("xeb,xdc->edbc", left_projection_rows, crop_fragment)
        / sequence_depth
    ).astype(jnp.bfloat16)
    outer_product_block = outer_product_block.reshape(
        local_rows, crop_fragment.shape[1], opm_half * opm_half
    )
    outer_term = trilateral_contraction("ijf,fd->ijd", outer_product_block, tensor_final_matrix)
    pair_mid = edge_features[0].astype(jnp.float32) + (outer_term + tensor_final_offset)
    pair_hat, pair_inv = layer_norm_forward(pair_mid)
    pair_normed = (pair_hat * edge_scaling_factor).astype(jnp.bfloat16)
    raw = trilateral_contraction("kid,de->kie", pair_normed, trilateral_entry_matrix)
    left_sig = jax.nn.sigmoid(raw[..., :width])
    right_sig = jax.nn.sigmoid(raw[..., 2 * width : 3 * width])
    left_value = raw[..., width : 2 * width]
    right_value = raw[..., 3 * width :]
    left_edge = (left_sig * left_value).astype(jnp.bfloat16)
    right_edge = (right_sig * right_value).astype(jnp.bfloat16)
    columns = lax.all_to_all(
        jnp.concatenate([left_edge, right_edge], -1), "dap", split_axis=1, concat_axis=0, tiled=True
    )
    left_cols = columns[..., :width]
    right_cols = columns[..., width:]
    right_whole = lax.all_gather(right_cols, "dap", axis=1, tiled=True)
    mixed = trilateral_contraction("kic,kjc->ijc", left_cols, right_whole)
    mixed_hat, mixed_inv = layer_norm_forward(mixed)
    mixed_normed = (mixed_hat * central_scaling_factor).astype(jnp.bfloat16)
    gate = jax.nn.sigmoid(trilateral_contraction("ijd,de->ije", pair_normed, final_sigmoid_matrix))
    update = trilateral_contraction("ijc,cd->ijd", mixed_normed, trilateral_final_matrix)
    pair_new = pair_mid + gate * update
    pair_result_state = pair_new.astype(jnp.bfloat16)
    upstream = adjoint_edges[0].astype(jnp.float32)
    grad_update = (upstream * gate).astype(jnp.bfloat16)
    grad_gate = (upstream * update * gate * (1.0 - gate)).astype(jnp.bfloat16)
    triangle_output_gradient = trilateral_contraction("ijc,ijd->cd", mixed_normed, grad_update)
    triangle_gate_gradient = trilateral_contraction("ijc,ijd->cd", pair_normed, grad_gate)
    grad_mixed_normed = trilateral_contraction("ijd,cd->ijc", grad_update, trilateral_final_matrix)
    middle_gain_gradient = jnp.sum(grad_mixed_normed * mixed_hat, (0, 1))
    grad_mixed = standardize_adjoint(
        grad_mixed_normed * central_scaling_factor, mixed_hat, mixed_inv
    ).astype(jnp.bfloat16)
    left_back = trilateral_contraction("ijc,kjc->kic", grad_mixed, right_whole)
    grad_left = lax.all_to_all(
        left_back.astype(jnp.bfloat16), "dap", split_axis=0, concat_axis=1, tiled=True
    ).astype(left_back.dtype)
    grad_right = lax.psum_scatter(
        trilateral_contraction("ijc,kic->kjc", grad_mixed, left_cols).astype(jnp.bfloat16),
        "dap",
        scatter_dimension=0,
        tiled=True,
    ).astype(jnp.float32)
    grad_raw = jnp.concatenate(
        [
            grad_left * left_value * left_sig * (1.0 - left_sig),
            grad_left * left_sig,
            grad_right * right_value * right_sig * (1.0 - right_sig),
            grad_right * right_sig,
        ],
        -1,
    ).astype(jnp.bfloat16)
    triangle_input_gradient = trilateral_contraction("kid,kie->de", pair_normed, grad_raw)
    grad_normed = trilateral_contraction(
        "kie,de->kid", grad_raw, trilateral_entry_matrix
    ) + trilateral_contraction("kie,de->kid", grad_gate, final_sigmoid_matrix)
    triangle_gain_gradient = jnp.sum(grad_normed * pair_hat, (0, 1))
    grad_mid = upstream + standardize_adjoint(grad_normed * edge_scaling_factor, pair_hat, pair_inv)
    pair_input_gradient = grad_mid.astype(jnp.bfloat16)
    output_bias_gradient = jnp.sum(grad_mid, (0, 1))
    factor = 1.0 / (lax.axis_size("dp") * length)
    crop_fragment = lax.all_gather(right_projection_rows, "dap", axis=1, tiled=True)
    span = crop_fragment.shape[1]
    outer_product_block = (
        trilateral_contraction("xeb,xdc->edbc", left_projection_rows, crop_fragment)
        / sequence_depth
    ).astype(jnp.bfloat16)
    outer_product_block = outer_product_block.reshape(local_rows, span, opm_half * opm_half)
    weight_part = trilateral_contraction("ijf,ijd->fd", outer_product_block, pair_input_gradient)
    outer_product_gradient = trilateral_contraction(
        "ijd,fd->ijf", pair_input_gradient, tensor_final_matrix
    ).astype(jnp.bfloat16)
    outer_product_gradient = outer_product_gradient.reshape(local_rows, span, opm_half, opm_half)
    left_operand = (
        trilateral_contraction("yxet,vxt->vye", outer_product_gradient, crop_fragment)
        / sequence_depth
    )
    right_operand = (
        trilateral_contraction("ynmv,oym->onv", outer_product_gradient, left_projection_rows)
        / sequence_depth
    )
    right_projection_gradient = lax.psum_scatter(
        right_operand.astype(jnp.bfloat16), "dap", scatter_dimension=1, tiled=True
    ).astype(jnp.float32)
    mapping_sensitivity = jnp.concatenate([left_operand, right_projection_gradient], -1).astype(
        jnp.bfloat16
    )
    outer_projection_gradient = trilateral_contraction(
        "keb,kex->bx", alignment_normalized, mapping_sensitivity
    )
    standardized_homolog_adjoint = trilateral_contraction(
        "dvk,gk->dvg", mapping_sensitivity, tensor_mapping_matrix
    )
    tensor_scaling_sensitivity = jnp.sum(
        standardized_homolog_adjoint * homolog_standardized, (0, 1)
    )
    homolog_sensitivity = standardize_adjoint(
        standardized_homolog_adjoint * homolog_scaling_factor,
        homolog_standardized,
        homolog_reciprocal_spread,
    ).astype(jnp.bfloat16)
    totals = lax.psum(
        (
            tensor_scaling_sensitivity * factor,
            outer_projection_gradient * factor,
            weight_part * factor,
            output_bias_gradient * factor,
            triangle_gain_gradient * factor,
            triangle_input_gradient * factor,
            triangle_gate_gradient * factor,
            middle_gain_gradient * factor,
            triangle_output_gradient * factor,
        ),
        ("dp", "dap"),
    )
    return (
        pair_result_state[None],
        pair_input_gradient[None],
        homolog_sensitivity[None],
        totals[0],
        totals[1],
        totals[2],
        totals[3],
        totals[4],
        totals[5],
        totals[6],
        totals[7],
        totals[8],
    )


def solution(mesh):
    placed = (
        P("dp", None, "dap", None),
        P("dp", "dap", None, None),
        P("dp", "dap", None, None),
        P(),
        P(),
        P(),
        P(),
        P(),
        P(),
        P(),
        P(),
        P(),
    )
    return jax.shard_map(
        local,
        mesh=mesh,
        in_specs=placed,
        out_specs=(
            P("dp", "dap", None, None),
            P("dp", "dap", None, None),
            P("dp", None, "dap", None),
            P(),
            P(),
            P(),
            P(),
            P(),
            P(),
            P(),
            P(),
            P(),
        ),
        check_vma=False,
    )
```

profile of v0, /device:TPU:0, one launch (start us, length us, event | category | flops | bytes accessed | tf_op | source)
XLA Modules:
  0.0 625.9 jit_solution(7159629464105642007)
XLA Ops:
  7.2 1.1 convert_reduce_fusion
  8.4 1.1 fusion.64
  9.6 1.3 convolution_convert_fusion.2
  10.9 0.7 slice.32
  11.7 38.3 %all-gather.3.cloned.1.call-done = bf16[192,192,32]{0,2,1:T(8,128)(2,1)} async-done(((bf16[192,12,32]{0,2,1:T(8,128)(2,1)}), bf16[192,192,32]{0,2,1:T(8,128)(2,1)}) %all-gather.3.cloned.1.call-update) | async-done | bytes 2359312 | tf_op jit(solution)/shard_map/all_gather | solution.py:54
  50.0 10.8 %fusion = bf16[12,192,32,32]{2,3,0,1:T(8,128)(2,1)} fusion(bf16[192,192,32]{0,2,1:T(8,128)(2,1)} %all-gather.3.cloned.1.call-done, bf16[192,12,64]{0,2,1:T(8,128)(2,1)S(1)} %convolution_convert_fusion.2), kind=kOutput, calls=%fused_computation.1 | convolution fusion | flops 910688256 | bytes 7274496 | tf_op jit(solution)/shard_map/xeb,xdc->edbc/dot_general | solution.py:22
  60.8 21.6 %copy.79 = bf16[12,192,32,32]{1,3,2,0:T(8,128)(2,1)} copy(bf16[12,192,32,32]{2,3,0,1:T(8,128)(2,1)} %fusion) | data formatting | bytes 9437184 | tf_op jit(solution)/shard_map/convert_element_type | solution.py:58
  82.4 5.1 fusion.94
  87.5 0.8 multiply_reduce_fusion.6
  89.0 0.8 multiply_convert_fusion.8
  89.8 0.8 copy-done.13
  90.6 0.7 fusion.72
  92.0 1.5 copy-done.1
  93.6 0.7 copy.81
  94.4 26.1 %all_to_all.27 = bf16[12,192,256]{2,0,1:T(8,128)(2,1)S(1)} all-to-all(bf16[12,192,256]{2,0,1:T(8,128)(2,1)S(1)} %copy.81), channel_id=1, replica_groups=mesh['dp'=8,'dap'=16] {'dap'}, dimensions={1} | all-to-all | bytes 2359296 | tf_op jit(solution)/shard_map/all_to_all | solution.py:73
  120.6 1.2 all_to_all.23
  121.8 2.4 fusion.93
  125.0 1.0 copy-done.3
  126.3 2.1 copy.87
  128.5 2.0 copy.112
  130.5 50.1 %all-gather.5.cloned.1.call-done = bf16[192,192,128]{2,0,1:T(8,128)(2,1)} async-done(((bf16[192,12,128]{2,0,1:T(8,128)(2,1)}), bf16[192,192,128]{2,0,1:T(8,128)(2,1)}) %all-gather.5.cloned.1.call-update) | async-done | bytes 9437200 | tf_op jit(solution)/shard_map/all_gather | solution.py:78
  180.5 17.4 %copy.85 = bf16[192,192,128]{0,1,2:T(8,128)(2,1)} copy(bf16[192,192,128]{2,0,1:T(8,128)(2,1)} %all-gather.5.cloned.1.call-done) | data formatting | bytes 18874368 | tf_op jit(solution)/shard_map/all_gather | solution.py:78
  197.9 8.8 %bitcast_reduce_fusion = (f32[12,192]{1,0:T(8,128)}, f32[128,192,12]{1,2,0:T(8,128)S(1)}) fusion(bf16[192,192,128]{0,1,2:T(8,128)(2,1)} %copy.85, bf16[192,12,128]{0,1,2:T(8,128)(2,1)} %copy.112), kind=kOutput, calls=%fused_computation.15 | convolution fusion | flops 113538816 | bytes 11215872 | tf_op jit(solution)/shard_map/kic,kjc->ijc/dot_general | solution.py:22
  206.7 0.9 broadcast_multiply_fusion.4
  208.3 1.8 multiply_reduce_fusion
  210.2 1.7 multiply_convert_fusion.2
  211.9 1.0 copy-done.5
  212.9 6.5 %fusion.97 = bf16[128,192,192]{2,1,0:T(8,128)(2,1)} fusion(bf16[192,12,128]{0,1,2:T(8,128)(2,1)S(1)} %copy-done.7, bf16[12,192,128]{1,0,2:T(8,128)(2,1)S(1)} %get-tuple-element.42), kind=kOutput, calls=%fused_computation.142 | convolution fusion | flops 113246208 | bytes 10616832 | tf_op jit(solution)/shard_map/ijc,kic->kjc/dot_general | solution.py:22
  219.3 16.3 %copy.92 = bf16[128,192,192]{0,2,1:T(8,128)(2,1)} copy(bf16[128,192,192]{2,1,0:T(8,128)(2,1)} %fusion.97) | data formatting | bytes 18874368 | tf_op jit(solution)/shard_map/ijc,kic->kjc/dot_general | solution.py:22
  235.7 1.2 copy-done.6
  236.9 6.3 %fusion.16 = bf16[192,12,128]{0,1,2:T(8,128)(2,1)S(1)} fusion(bf16[192,192,128]{0,1,2:T(8,128)(2,1)} %copy.85, bf16[12,192,128]{1,0,2:T(8,128)(2,1)S(1)} %copy-done.6), kind=kOutput, calls=%fused_computation.36 | convolution fusion | flops 113541120 | bytes 10616832 | tf_op jit(solution)/shard_map/ijc,kjc->kic/dot_general | solution.py:22
  243.2 1.9 copy.89
  245.1 5.1 all-to-all-start.1
  250.5 2.6 copy.86
  253.2 2.6 fusion.35
  255.8 11.1 %all-to-all-done.1 = bf16[192,12,128]{2,1,0:T(8,128)(2,1)} async-done(((bf16[192,12,128]{2,1,0:T(8,128)(2,1)}), bf16[192,12,128]{2,1,0:T(8,128)(2,1)}, u32[]{:S(2)}, u32[]{:S(2)}) %all-to-all-start.1) | async-done | bytes 589856 | tf_op jit(solution)/shard_map/all_to_all | solution.py:97
  266.9 2.3 copy_convert_fusion
  269.2 2.4 reshape.109
  271.6 3.3 copy.91
  274.9 2.4 reshape.108
  277.3 73.7 %reduce-scatter.3.cloned.1.call-done = bf16[12,192,128]{2,1,0:T(8,128)(2,1)} async-done(((bf16[192,192,128]{2,1,0:T(8,128)(2,1)}), bf16[12,192,128]{2,1,0:T(8,128)(2,1)}) %reduce-scatter.3.cloned.1.call-update) | async-done | bytes 589840 | tf_op jit(solution)/shard_map/reduce_scatter | solution.py:100
  351.1 4.1 multiply_convert_fusion.5
  355.2 0.8 fusion.66
  356.7 1.6 multiply_reduce_fusion.4
  358.3 1.6 fusion.92
  359.9 0.8 copy-done.17
  360.7 3.6 convolution_convert_fusion
  364.3 8.0 %copy.93 = bf16[12,192,1024]{1,2,0:T(8,128)(2,1)} copy(bf16[12,192,1024]{2,1,0:T(8,128)(2,1)} %convolution_convert_fusion) | data formatting | bytes 9437184 | tf_op jit(solution)/shard_map/convert_element_type | solution.py:134
  372.3 9.7 %fusion.8 = f32[192,192,32]{1,0,2:T(8,128)} fusion(bf16[12,192,32,32]{1,3,2,0:T(8,128)(2,1)} %bitcast.191, bf16[192,12,64]{0,2,1:T(8,128)(2,1)S(1)} %copy-done.34), kind=kOutput, calls=%fused_computation.12 | convolution fusion | flops 905969664 | bytes 9633792 | tf_op jit(solution)/shard_map/ynmv,oym->onv/dot_general | solution.py:22
  382.1 7.2 %copy.97 = f32[192,192,32]{0,2,1:T(8,128)} copy(f32[192,192,32]{1,0,2:T(8,128)} %fusion.8) | data formatting | bytes 9437184 | tf_op jit(solution)/shard_map/ynmv,oym->onv/dot_general | solution.py:22
  389.3 5.4 multiply_convert_fusion.1
  395.8 2.2 fusion.49
  398.0 1.0 fusion.48
  399.0 3.1 fusion.47
  402.2 2.3 fusion.17
  404.5 15.0 %fusion.42 = bf16[192,12,32]{0,2,1:T(8,128)(2,1)S(1)} fusion(bf16[12,192,32,32]{1,3,2,0:T(8,128)(2,1)} %bitcast.192, bf16[192,192,32]{0,2,1:T(8,128)(2,1)} %all-gather.3.cloned.1.call-done), kind=kOutput, calls=%fused_computation.68 | convolution fusion | flops 906117120 | bytes 7225344 | tf_op jit(solution)/shard_map/yxet,vxt->vye/dot_general | solution.py:22
  419.5 43.5 %reduce-scatter.5.cloned.1.call-done = bf16[192,12,32]{0,2,1:T(8,128)(2,1)} async-done(((bf16[192,192,32]{0,2,1:T(8,128)(2,1)}), bf16[192,12,32]{0,2,1:T(8,128)(2,1)}) %reduce-scatter.5.cloned.1.call-update) | async-done | bytes 147472 | tf_op jit(solution)/shard_map/reduce_scatter | solution.py:144
  463.0 1.5 fusion.63
  464.9 65.7 %all-reduce = (f32[64]{0:T(128)}, f32[64,64]{1,0:T(8,128)}, f32[128]{0:T(128)}, f32[128]{0:T(128)}, f32[128]{0:T(128)}) all-reduce(f32[64]{0:T(128)S(1)} %broadcast_multiply_fusion.12, f32[64,64]{1,0:T(8,128)S(1)} %fusion.50, f32[128]{0:T(128)S(1)} %broadcast_multiply_fusion.11, ...), channel_id=1, replica_groups=mesh['dp'=8,'dap'=16] {'dp','dap'}, use_global_device_ids=true, to_apply=%region_15.0 | all-reduce | flops 4544 | bytes 36352 | tf_op jit(solution)/shard_map/psum | solution.py:164
  530.6 1.0 fusion.67
  531.6 83.7 %all-reduce.4.cloned.1.call-done = (f32[1024,128]{1,0:T(8,128)}, f32[128,512]{1,0:T(8,128)}, f32[128,128]{1,0:T(8,128)}, f32[128,128]{1,0:T(8,128)}) async-done(((f32[1024,128]{1,0:T(8,128)}, f32[128,512]{1,0:T(8,128)}, f32[128,128]{1,0:T(8,128)}, f32[128,128]{1,0:T(8,128)}), (f32[1024,128]{1,0:T(8,128)}, f32[128,512]{1,0:T(8,128)}, f32[128,128]{1,0:T(8,128)}, ...) | async-done | bytes 917520 | tf_op jit(solution)/shard_map/psum | solution.py:164
  615.3 1.9 copy.140
  617.2 0.7 copy.141
  618.6 0.6 copy.143
  (129 shorter events, 6.5 us)
Async XLA Ops:
  7.2 75.2 %copy-start = (bf16[1024,128]{1,0:T(8,128)(2,1)S(1)}, bf16[1024,128]{1,0:T(8,128)(2,1)}, u32[]{:S(2)}) copy-start(bf16[1024,128]{1,0:T(8,128)(2,1)} %param.17) | copy-start | bytes 786436
  7.2 42.8 %all-gather.3.cloned.1.call-start = ((), (), s32[]{:S(2)}) async-start(), calls=%async_computation.4 | async-start | bytes 3342336 | tf_op jit(solution)/shard_map/all_gather | solution.py:54
  8.4 1.2 copy-start.27
  9.5 1.4 copy-start.35
  10.9 49.9 %copy-start.33 = (bf16[192,12,64]{0,2,1:T(8,128)(2,1)}, bf16[192,12,64]{0,2,1:T(8,128)(2,1)S(1)}, u32[]{:S(2)}) copy-start(bf16[192,12,64]{0,2,1:T(8,128)(2,1)S(1)} %convolution_convert_fusion.2) | copy-start | bytes 884740
  11.7 168.8 %all-gather.5.cloned.1.call-start = ((), (), s32[]{:S(2)}) async-start(), calls=%async_computation.5 | async-start | bytes 10027008 | tf_op jit(solution)/shard_map/all_gather | solution.py:78
  60.8 21.6 %copy-start.19 = (bf16[1,12,192,128]{3,2,1,0:T(8,128)(2,1)S(1)}, bf16[1,12,192,128]{3,2,1,0:T(8,128)(2,1)}, u32[]{:S(2)}) copy-start(bf16[1,12,192,128]{3,2,1,0:T(8,128)(2,1)} %param.13) | copy-start | bytes 1769476
  60.8 21.6 %copy-start.44 = (f32[128]{0:T(128)S(1)}, f32[128]{0:T(128)}, u32[]{:S(2)}) copy-start(f32[128]{0:T(128)} %param.18) | copy-start | bytes 1540
  87.5 1.5 copy-start.41
  88.3 2.3 copy-start.31
  88.4 0.6 copy-start.24
  89.8 0.8 copy-start.13
  91.4 2.1 copy-start.1
  121.8 2.7 copy-start.14
  121.8 2.7 copy-start.39
  124.2 1.8 copy-start.8
  124.2 1.8 copy-start.29
  124.2 226.8 %reduce-scatter.3.cloned.1.call-start = ((), (), s32[]{:S(2)}) async-start(), calls=%async_computation.6 | async-start | bytes 10027008 | tf_op jit(solution)/shard_map/reduce_scatter | solution.py:100
  125.0 1.0 copy-start.3
  126.3 2.2 copy-start.16
  206.7 1.6 copy-start.2
  206.7 1.6 copy-start.43
  210.2 2.7 copy-start.7
  211.9 1.0 copy-start.5
  235.6 1.2 copy-start.6
  245.1 8.1 %copy-start.9 = (bf16[1,12,192,128]{3,2,1,0:T(8,128)(2,1)S(1)}, bf16[1,12,192,128]{3,2,1,0:T(8,128)(2,1)}, u32[]{:S(2)}) copy-start(bf16[1,12,192,128]{3,2,1,0:T(8,128)(2,1)} %param.14) | copy-start | bytes 1769476
  245.1 21.8 %all-to-all-start.1 = ((bf16[192,12,128]{2,1,0:T(8,128)(2,1)}), bf16[192,12,128]{2,1,0:T(8,128)(2,1)}, u32[]{:S(2)}, u32[]{:S(2)}) async-start(bf16[192,12,128]{2,1,0:T(8,128)(2,1)} %copy.89), calls=%async_computation.1 | async-start | bytes 1572864 | tf_op jit(solution)/shard_map/all_to_all | solution.py:97
  250.3 2.9 copy-start.4
  250.3 2.9 copy-start.30
  250.3 212.7 %reduce-scatter.5.cloned.1.call-start = ((), (), s32[]{:S(2)}) async-start(), calls=%async_computation.7 | async-start | bytes 3342336 | tf_op jit(solution)/shard_map/reduce_scatter | solution.py:144
  277.3 77.8 %copy-start.32 = (bf16[128,512]{1,0:T(8,128)(2,1)S(1)}, bf16[128,512]{1,0:T(8,128)(2,1)}, u32[]{:S(2)}) copy-start(bf16[128,512]{1,0:T(8,128)(2,1)} %param.20) | copy-start | bytes 393220
  355.1 0.9 copy-start.20
  355.1 1.0 copy-start.21
  355.1 1.2 copy-start.22
  355.1 1.3 copy-start.23
  355.2 1.5 copy-start.10
  355.2 1.5 copy-start.25
  355.2 1.5 copy-start.40
  355.2 1.5 copy-start.42
  359.9 0.8 copy-start.17
  364.3 8.0 %copy-start.34 = (bf16[192,12,64]{0,2,1:T(8,128)(2,1)S(1)}, bf16[192,12,64]{0,2,1:T(8,128)(2,1)}, u32[]{:S(2)}) copy-start(bf16[192,12,64]{0,2,1:T(8,128)(2,1)} %copy-done.33) | copy-start | bytes 884740
  394.7 0.7 copy-start.46
  394.7 1.1 copy-start.11
  394.8 3.3 copy-start.12
  394.8 220.5 %all-reduce.4.cloned.1.call-start = ((), (), s32[]{:S(2)}) async-start(), calls=%async_computation.8 | async-start | bytes 1835008 | tf_op jit(solution)/shard_map/psum | solution.py:164
  395.8 6.4 %slice-start = ((s8[6291456]{0:T(1024)(128)(4,1)}), s8[4194304]{0:T(1024)(128)(4,1)S(1)}, s32[]{:S(2)}) async-start(s8[6291456]{0:T(1024)(128)(4,1)} %bitcast.186), calls=%async_computation.9 | async-start | bytes 8388608
  399.0 3.2 slice-start.1
  399.0 3.2 copy-start.18
  404.5 58.5 %copy-start.15 = (bf16[1,192,12,64]{1,3,2,0:T(8,128)(2,1)S(1)}, bf16[1,192,12,64]{1,3,2,0:T(8,128)(2,1)}, u32[]{:S(2)}) copy-start(bf16[1,192,12,64]{1,3,2,0:T(8,128)(2,1)} %param.12) | copy-start | bytes 884740
  404.5 58.5 %copy-start.28 = (f32[192,12]{0,1:T(8,128)S(1)}, f32[192,12]{0,1:T(8,128)}, u32[]{:S(2)}) copy-start(f32[192,12]{0,1:T(8,128)} %copy-done.27) | copy-start | bytes 27652
  404.5 58.5 %copy-start.36 = (f32[192,12]{0,1:T(8,128)S(1)}, f32[192,12]{0,1:T(8,128)}, u32[]{:S(2)}) copy-start(f32[192,12]{0,1:T(8,128)} %copy-done.35) | copy-start | bytes 27652
  404.5 58.5 %copy-start.45 = (f32[64]{0:T(128)S(1)}, f32[64]{0:T(128)}, u32[]{:S(2)}) copy-start(f32[64]{0:T(128)} %param.15) | copy-start | bytes 772
  404.5 58.5 %copy-start.48 = (bf16[64,64]{1,0:T(8,128)(2,1)S(1)}, bf16[64,64]{1,0:T(8,128)(2,1)}, u32[]{:S(2)}) copy-start(bf16[64,64]{1,0:T(8,128)(2,1)} %param.16) | copy-start | bytes 24580
  463.0 1.6 copy-start.47
  615.3 1.9 copy-start.26
  615.3 2.6 copy-start.38
  615.3 3.3 copy-start.37
Sparse Core Ops, SparseCore 0:
  11.8 38.1 all-gather.2
  124.3 56.1 all-gather.4
  235.8 115.2 reduce-scatter.2
  394.9 68.0 reduce-scatter.4
  469.3 145.9 all-reduce.3
where the time goes:
time: 636 us; the launch traced here: 626 us
  waiting for transfers between devices  300 us (47%)
  local copies, waits for them, and re-layouts  105 us (17%)
  blocking collectives  91.8 us (14%)
  matrix products  84 us (13%)
  other arithmetic  23.8 us (4%)
  between operations  14.5 us (2%)
    dot_general x21, matrix products, trilateral_contraction(): return jnp.einsum(form, left, right, preferred_element_type=jnp.float32)  84 us
    psum x1, waiting for transfers between devices, local(): lax.psum((tensor_scaling_sensitivity * factor, outer_projection_gradient...  83.7 us
    reduce_scatter x1, waiting for transfers between devices, local(): lax.psum_scatter(trilateral_contraction('ijc,kic->kjc', grad_mixed, left_...  73.7 us
    psum x1, blocking collectives, local(): lax.psum((tensor_scaling_sensitivity * factor, outer_projection_gradient...  65.7 us
    all_gather x1, waiting for transfers between devices, local(): right_whole = lax.all_gather(right_cols, 'dap', axis=1, tiled=True)  50.1 us
    reduce_scatter x1, waiting for transfers between devices, local(): lax.psum_scatter(right_operand.astype(jnp.bfloat16), 'dap', scatter_dimen...  43.5 us
    all_gather x1, waiting for transfers between devices, local(): lax.all_gather(right_projection_rows, 'dap', axis=1, tiled=True)  38.3 us
    all_to_all x1, blocking collectives, local(): lax.all_to_all(jnp.concatenate([left_edge, right_edge], -1), 'dap', split...  26.1 us
  transfers between devices with their start and end apart: 6, of which 6 were waited for; matrix products, arithmetic and copies ran while one was open for 9% of the time, Pallas kernels for 0%

commit v1 on v0

v1 whole, which is shorter than its diff:
```python
import jax
import jax.numpy as jnp
from jax import lax
from jax.experimental import pallas as pl
from jax.experimental.pallas import tpu as pltpu
from jax.sharding import PartitionSpec as P

EPSILON = 1e-05
BF = jnp.bfloat16
F32 = jnp.float32
WIDE = 256


def nn(a, b):
    return lax.dot_general(a, b, (((1,), (0,)), ((), ())), preferred_element_type=F32)


def nt(a, b):
    return lax.dot_general(a, b, (((1,), (1,)), ((), ())), preferred_element_type=F32)


def tn(a, b):
    return lax.dot_general(a, b, (((0,), (0,)), ((), ())), preferred_element_type=F32)


def norm(v):
    centred = v - jnp.mean(v, 0, keepdims=True)
    inverse = lax.rsqrt(jnp.mean(centred * centred, 0, keepdims=True) + EPSILON)
    return centred * inverse, inverse


def norm_back(h, hat, inverse):
    first = jnp.mean(h, 0, keepdims=True)
    second = jnp.mean(h * hat, 0, keepdims=True)
    return (h - first - hat * second) * inverse


def sigmoid(v):
    return 1.0 / (1.0 + jnp.exp(-v))


def pad_rows(v, rows):
    return jnp.concatenate([v, jnp.zeros((rows - v.shape[0],) + v.shape[1:], v.dtype)], 0)


def flip(v):
    return pad_rows(v, WIDE).T


def low_half(v):
    lane = lax.broadcasted_iota(jnp.int32, v.shape, v.ndim - 1)
    return jnp.where(lane < 64, v, 0.0)


def pack(a, b):
    tail = low_half(a[:, 128:]) + pltpu.roll(low_half(b[:, 128:]), 64, 1)
    return a[:, :128], b[:, :128], tail


def unpack(t0, t1, t2):
    return (t0, low_half(t2)), (t1, low_half(pltpu.roll(t2, 64, 1)))


def call(kernel, outs, scratch, *operands, smem=0):
    specs = [pl.BlockSpec(memory_space=pltpu.SMEM)] * smem
    specs += [pl.BlockSpec(memory_space=pltpu.VMEM)] * (len(operands) - smem)
    return pl.pallas_call(
        kernel,
        out_shape=[jax.ShapeDtypeStruct(s, t) for s, t in outs],
        in_specs=specs,
        out_specs=[pl.BlockSpec(memory_space=pltpu.VMEM)] * len(outs),
        scratch_shapes=[pltpu.VMEM(s, t) for s, t in scratch],
        compiler_params=pltpu.CompilerParams(vmem_limit_bytes=50 * 1024 * 1024),
    )(*operands)


def project_kernel(x_ref, gain_ref, wt_ref, left_ref, lsend_ref, rsend_ref):
    pairs = x_ref.shape[0]
    width = wt_ref.shape[1]
    half = wt_ref.shape[0] // 2

    @pl.loop(0, pairs)
    def _(m):
        x = flip(x_ref[m].astype(F32))
        both = []
        for o in range(2):
            hat, _ = norm(x[o * width : (o + 1) * width])
            normed = (hat * gain_ref[...]).astype(BF)
            proj = nn(wt_ref[...], normed)
            both.append(proj)
            left_ref[2 * m + o] = proj[:half].astype(BF)
        for t, v in enumerate(pack(both[0][:half], both[1][:half])):
            lsend_ref[m, t] = v.astype(BF)
        for t, v in enumerate(pack(both[0][half:], both[1][half:])):
            rsend_ref[m, t] = v.astype(BF)


def outer_kernel(
    par_ref, own_ref, other_ref, left_ref, edge_ref, wt_ref, bias_ref, gain_ref, entry_ref,
    send_ref, mid_ref, normed_ref, right_ref, outer_ref, head, tail,
):
    chips, pairs, _, half, _ = own_ref.shape
    rows = left_ref.shape[0]
    length = edge_ref.shape[1]
    depth = 1.0 / length
    par = par_ref[0]
    for source, p in ((own_ref, par), (other_ref, 1 - par)):

        @pl.loop(0, chips)
        def _(chip):
            for m in range(pairs):
                t = source[chip, m].astype(F32)
                base = pl.multiple_of(((2 * chip + p) * rows + 2 * m) * half, half)
                for o, (a, b) in enumerate(unpack(t[0], t[1], t[2])):
                    head[pl.ds(base + o * half, half), :] = a
                    tail[pl.ds(base + o * half, half), :] = b

    left = left_ref[...].reshape(rows * half, WIDE)

    @pl.loop(0, half)
    def _(q):
        a = head[pl.ds(q, length, stride=half), :]
        b = tail[pl.ds(q, length, stride=half), :]
        r = pad_rows(jnp.concatenate([a, b], 1), WIDE).astype(BF)
        right_ref[q] = r
        o = (nt(left, r) * depth).astype(BF)
        at = pl.ds(pl.multiple_of(q * half, half), half)
        for i in range(rows):
            outer_ref[i, at, :] = o[i * half : (i + 1) * half]

    devices, _, _, sixteen, _ = send_ref.shape

    @pl.loop(0, pairs)
    def _(m):
        both = []
        for o in range(2):
            i = 2 * m + o
            mid = flip(edge_ref[i].astype(F32)) + (nn(wt_ref[...], outer_ref[i]) + bias_ref[...])
            mid_ref[i] = mid
            hat, _ = norm(mid)
            normed = (hat * gain_ref[...]).astype(BF)
            normed_ref[i] = normed
            raw = nn(entry_ref[...], normed)
            cut = raw.shape[0] // 2
            both.append(sigmoid(raw[:cut]) * raw[cut:])
        for t, v in enumerate(pack(*both)):
            send_ref[:, m, t] = v.reshape(devices, sixteen, 128).astype(BF)


def load_wide(head, tail, start, count, stride):
    a = head[pl.ds(start, count, stride=stride), :]
    b = tail[pl.ds(start, count, stride=stride), :]
    return jnp.concatenate([a, b], 1)


def store_wide(head, tail, start, count, stride, v):
    head[pl.ds(start, count, stride=stride), :] = v[:, :128]
    tail[pl.ds(start, count, stride=stride), :] = v[:, 128:]


def spread(source, head, tail):
    devices, pairs, _, high, _ = source.shape

    @pl.loop(0, devices)
    def _(d):
        for m in range(pairs):
            t = source[d, m].astype(F32)
            base = pl.multiple_of((d * pairs + m) * 2 * high, 2 * high)
            for o, (a, b) in enumerate(unpack(t[0], t[1], t[2])):
                head[pl.ds(base + o * high, high), :] = a
                tail[pl.ds(base + o * high, high), :] = b


def gather_up(head, tail, target):
    devices, pairs, _, high, _ = target.shape

    @pl.loop(0, devices)
    def _(d):
        for m in range(pairs):
            base = pl.multiple_of((d * pairs + m) * 2 * high, 2 * high)
            wide = [
                jnp.concatenate(
                    [head[pl.ds(base + o * high, high), :], tail[pl.ds(base + o * high, high), :]], 1
                )
                for o in range(2)
            ]
            for t, v in enumerate(pack(*wide)):
                target[d, m, t] = v.astype(BF)


def triangle_kernel(edges_ref, send_ref, left_ref, right_ref, head, tail, mhead, mtail):
    channels, length, _ = left_ref.shape
    spread(edges_ref, head, tail)
    for c in range(channels):
        a = load_wide(head, tail, c, length, 2 * channels).astype(BF)
        b = load_wide(head, tail, channels + c, length, 2 * channels).astype(BF)
        left_ref[c] = a
        right_ref[c] = b
        mixed = tn(a, b)[:length]
        store_wide(mhead, mtail, c, length, channels, mixed)
    gather_up(mhead, mtail, send_ref)


def triangle_back_kernel(grads_ref, left_ref, right_ref, send_ref, head, tail, mhead, mtail):
    channels, length, _ = left_ref.shape
    spread(grads_ref, mhead, mtail)
    for c in range(channels):
        g = pad_rows(load_wide(mhead, mtail, c, length, channels), WIDE).astype(BF)
        store_wide(head, tail, c, length, 2 * channels, nt(right_ref[c], g))
        store_wide(head, tail, channels + c, length, 2 * channels, nn(left_ref[c], g))
    gather_up(head, tail, send_ref)


def update_kernel(
    mixed_ref, mid_ref, normed_ref, adj_ref, cgain_ref, wf_ref, wft_ref, wgt_ref,
    out_ref, send_ref, ggate_ref, wfg_ref, wgg_ref, msum_ref, acc,
):
    devices, quads, _, sixteen, _ = mixed_ref.shape
    length = out_ref.shape[1]
    channels = wf_ref.shape[0]
    eight = channels // devices
    wfg_ref[...] = jnp.zeros_like(wfg_ref)
    wgg_ref[...] = jnp.zeros_like(wgg_ref)
    acc[...] = jnp.zeros_like(acc)

    @pl.loop(0, quads)
    def _(n):
        t = [mixed_ref[:, n, k].astype(F32).reshape(devices * sixteen, 128) for k in range(3)]
        packed = []
        for mo, (a, b) in enumerate(unpack(*t)):
            block = jnp.concatenate([a, b], 1).reshape(devices, 2, eight, WIDE)
            grads = []
            for o in range(2):
                i = 4 * n + 2 * mo + o
                mixed = block[:, o].reshape(channels, WIDE)
                hat, inverse = norm(mixed)
                mn = (hat * cgain_ref[...]).astype(BF)
                normed = normed_ref[i]
                gate = sigmoid(nn(wgt_ref[...], normed))
                update = nn(wft_ref[...], mn)
                new = mid_ref[i] + gate * update
                out_ref[i] = new.T[:length].astype(BF)
                up = flip(adj_ref[i].astype(F32))
                gu = (up * gate).astype(BF)
                gg = (up * update * gate * (1.0 - gate)).astype(BF)
                ggate_ref[i] = gg
                wfg_ref[...] += nt(mn, gu)
                wgg_ref[...] += nt(normed, gg)
                gmn = nn(wf_ref[...], gu)
                acc[...] += gmn * hat
                grads.append(
                    norm_back(gmn * cgain_ref[...], hat, inverse).reshape(devices, 1, eight, WIDE)
                )
            packed.append(jnp.concatenate(grads, 1).reshape(devices * sixteen, WIDE))
        for k, v in enumerate(pack(*packed)):
            send_ref[:, n, k] = v.reshape(devices, sixteen, 128).astype(BF)

    msum_ref[...] = jnp.sum(acc[...].T, 0, keepdims=True)


def edge_back_kernel(
    grads_ref, mid_ref, normed_ref, ggate_ref, adj_ref, gain_ref, entryt_ref, entry_ref, wg_ref,
    pgrad_ref, pgradt_ref, send_ref, win_ref, gsum_ref, bsum_ref, gacc, bacc, rows,
):
    devices, pairs, _, sixteen, _ = grads_ref.shape
    count, length, channels = pgrad_ref.shape
    win_ref[...] = jnp.zeros_like(win_ref)
    gacc[...] = jnp.zeros_like(gacc)
    bacc[...] = jnp.zeros_like(bacc)

    @pl.loop(0, pairs)
    def _(m):
        t = [grads_ref[:, m, k].astype(F32).reshape(devices * sixteen, 128) for k in range(3)]
        for o, (a, b) in enumerate(unpack(*t)):
            i = 2 * m + o
            grad = jnp.concatenate([a, b], 1)
            normed = normed_ref[i]
            raw = nn(entryt_ref[...], normed)
            cut = raw.shape[0] // 2
            sig = sigmoid(raw[:cut])
            gs = grad * sig
            graw = jnp.concatenate([gs * raw[cut:] * (1.0 - sig), gs], 0).astype(BF)
            win_ref[...] += nt(graw, normed)
            gpn = nn(entry_ref[...], graw) + nn(wg_ref[...], ggate_ref[i])
            hat, inverse = norm(mid_ref[i])
            gacc[...] += gpn * hat
            up = flip(adj_ref[i].astype(F32))
            gmid = up + norm_back(gpn * gain_ref[...], hat, inverse)
            bacc[...] += gmid
            pgradt_ref[i] = gmid.astype(BF)
            turned = gmid.T[:length]
            pgrad_ref[i] = turned.astype(BF)
            rows[pl.ds(i, length, stride=count), :] = turned

    send_ref[...] = rows[...].astype(BF)
    gsum_ref[...] = jnp.sum(gacc[...].T, 0, keepdims=True)
    bsum_ref[...] = jnp.sum(bacc[...].T, 0, keepdims=True)


def outer_back_kernel(
    pgradt_ref, right_ref, outer_ref, w_ref, grad_ref, wout_ref, stage,
):
    count, _, _ = pgradt_ref.shape
    half = right_ref.shape[0]
    length = 1.0 / 192
    group = stage.shape[2] // WIDE

    @pl.loop(0, count)
    def _(i):
        g = nn(w_ref[...], pgradt_ref[i]).astype(BF)
        at = pl.ds(pl.multiple_of(i * half, half), half)
        for q in range(half):
            stage[q // group, at, (q % group) * WIDE : (q % group + 1) * WIDE] = g[
                q * half : (q + 1) * half
            ]

    grad_ref[...] = jnp.zeros_like(grad_ref)

    @pl.loop(0, half // group)
    def _(k):
        r = right_ref[pl.ds(k * group, group)].reshape(group * WIDE, WIDE)
        grad_ref[...] += nn(stage[k], r)

    grad_ref[...] = grad_ref[...] * length
    wout_ref[...] = jnp.zeros_like(wout_ref)

    @pl.loop(0, count // 2)
    def _(m):
        a = jnp.concatenate([outer_ref[2 * m], outer_ref[2 * m + 1]], 1)
        b = jnp.concatenate([pgradt_ref[2 * m], pgradt_ref[2 * m + 1]], 1)
        wout_ref[...] += nt(a, b)


def column_kernel(
    pcol_ref, lgath_ref, w_ref, gleft_ref, x_ref, mgain_ref, wmap_ref,
    out_ref, wproj_ref, msum_ref, prow, head, tail, stage, lefts, gright, macc,
):
    devices, many, channels = pcol_ref.shape
    _, pairs, _, half, _ = lgath_ref.shape
    count = 2 * pairs
    length = devices * count
    group = stage.shape[2] // WIDE

    @pl.loop(0, devices)
    def _(d):
        prow[pl.ds(pl.multiple_of(d * many, 8), many), :] = pcol_ref[d].astype(F32)
        for m in range(pairs):
            t = lgath_ref[d, m].astype(F32)
            for o, (a, b) in enumerate(unpack(t[0], t[1], t[2])):
                base = pl.multiple_of(((2 * m + o) * devices + d) * half, half)
                head[pl.ds(base, half), :] = a
                tail[pl.ds(base, half), :] = b

    @pl.loop(0, count)
    def _(j):
        p = jnp.concatenate(
            [prow[pl.ds(j * count + i, devices, stride=many), :] for i in range(count)], 0
        )
        g = nt(w_ref[...], pad_rows(p, WIDE).astype(BF)).astype(BF)
        at = pl.ds(pl.multiple_of(j * half, half), half)
        for q in range(half):
            stage[q // group, at, (q % group) * WIDE : (q % group + 1) * WIDE] = g[
                q * half : (q + 1) * half
            ]

    @pl.loop(0, half)
    def _(q):
        lefts[q] = pad_rows(load_wide(head, tail, q, length, half), WIDE).astype(BF)

    gright[...] = jnp.zeros_like(gright)

    @pl.loop(0, half // group)
    def _(k):
        r = lefts[pl.ds(k * group, group)].reshape(group * WIDE, WIDE)
        gright[...] += nn(stage[k], r)

    width = wmap_ref.shape[0]
    wproj_ref[...] = jnp.zeros_like(wproj_ref)
    macc[...] = jnp.zeros_like(macc)

    @pl.loop(0, pairs)
    def _(m):
        x = flip(x_ref[m].astype(F32))
        both = []
        for o in range(2):
            hat, inverse = norm(x[o * width : (o + 1) * width])
            normed = (hat * mgain_ref[...]).astype(BF)
            at = pl.ds(pl.multiple_of((2 * m + o) * half, half), half)
            g = jnp.concatenate([gleft_ref[at, :], gright[at, :] * (1.0 / length)], 0).astype(BF)
            wproj_ref[...] += nt(normed, g)
            gn = nn(wmap_ref[...], g)
            macc[...] += gn * hat
            both.append(norm_back(gn * mgain_ref[...], hat, inverse))
        out_ref[m] = jnp.concatenate(both, 0).T[:length].astype(BF)

    total = macc[...]
    msum_ref[...] = jnp.sum(jnp.concatenate([total, jnp.zeros_like(total)], 0).T, 0, keepdims=True)


def exchange(v, axes="dap", groups=None):
    return lax.all_to_all(
        v, axes, split_axis=0, concat_axis=0, tiled=True, axis_index_groups=groups
    )


def local(
    homolog_features,
    edge_features,
    adjoint_edges,
    homolog_scaling_factor,
    tensor_mapping_matrix,
    tensor_final_matrix,
    tensor_final_offset,
    edge_scaling_factor,
    trilateral_entry_matrix,
    final_sigmoid_matrix,
    central_scaling_factor,
    trilateral_final_matrix,
):
    n = lax.axis_size("dap")
    everyone = n * lax.axis_size("dp")
    msa = homolog_features[0]
    depth, count, width = msa.shape
    length = edge_features.shape[2]
    pairs = count // 2
    half = tensor_mapping_matrix.shape[1] // 2
    channels = edge_features.shape[3]
    eight = channels // n
    edges = edge_features[0]
    adjoint = adjoint_edges[0]
    column = lambda v: v.reshape(-1, 1)

    x = msa.reshape(depth, pairs, 2 * width).transpose(1, 0, 2)
    left, left_send, right_send = call(
        project_kernel,
        [((count, half, WIDE), BF), ((pairs, 3, half, 128), BF), ((pairs, 3, half, 128), BF)],
        [],
        x, column(homolog_scaling_factor), tensor_mapping_matrix.T,
    )
    chips = n // 2
    groups = [list(range(0, n, 2)), list(range(1, n, 2))]
    own = exchange(
        jnp.broadcast_to(right_send, (chips,) + right_send.shape), groups=groups
    )
    other = lax.ppermute(own, "dap", [(i, i ^ 1) for i in range(n)])
    left_all = lax.all_gather(left_send, "dap", axis=0, tiled=False)
    parity = lax.rem(lax.axis_index("dap"), 2).astype(jnp.int32).reshape(1)

    qp = tensor_final_matrix.reshape(half, half, channels).transpose(1, 0, 2)
    qp = qp.reshape(half * half, channels)
    entry = trilateral_entry_matrix.reshape(channels, 2, 2, n, eight).transpose(0, 2, 3, 1, 4)
    entry = entry.reshape(channels, 4 * channels)
    edge_send, mid, normed, right, outer = call(
        outer_kernel,
        [
            ((n, pairs, 3, 2 * eight, 128), BF),
            ((count, channels, WIDE), F32),
            ((count, channels, WIDE), BF),
            ((half, WIDE, WIDE), BF),
            ((count, half * half, WIDE), BF),
        ],
        [((length * half, 128), F32)] * 2,
        parity, own, other, left, edges, qp.T, column(tensor_final_offset),
        column(edge_scaling_factor), entry.T, smem=1,
    )
    edge_cols = exchange(edge_send)
    mixed_send, left_cols, right_cols = call(
        triangle_kernel,
        [
            ((n, pairs // 2, 3, 2 * eight, 128), BF),
            ((eight, length, WIDE), BF),
            ((eight, length, WIDE), BF),
        ],
        [((length * 2 * eight, 128), F32)] * 2 + [((length * eight, 128), F32)] * 2,
        edge_cols,
    )
    mixed = exchange(mixed_send)
    square = ((channels, channels), F32)
    row = ((1, channels), F32)
    pair_out, grad_send, grad_gate, tri_out, tri_gate, mid_gain = call(
        update_kernel,
        [
            (edges.shape, BF),
            ((n, pairs // 2, 3, 2 * eight, 128), BF),
            ((count, channels, WIDE), BF),
            square, square, row,
        ],
        [((channels, WIDE), F32)],
        mixed, mid, normed, adjoint, column(central_scaling_factor),
        trilateral_final_matrix, trilateral_final_matrix.T, final_sigmoid_matrix.T,
    )
    grad_cols = exchange(grad_send)
    (back_send,) = call(
        triangle_back_kernel,
        [((n, pairs, 3, 2 * eight, 128), BF)],
        [((length * 2 * eight, 128), F32)] * 2 + [((length * eight, 128), F32)] * 2,
        grad_cols, left_cols, right_cols,
    )
    back = exchange(back_send)
    pgrad, pgradt, pgrad_send, tri_in, tri_gain, bias = call(
        edge_back_kernel,
        [
            (edges.shape, BF),
            ((count, channels, WIDE), BF),
            ((length * count, channels), BF),
            ((4 * channels, channels), F32),
            row, row,
        ],
        [((channels, WIDE), F32)] * 2 + [((length * count, channels), F32)],
        back, mid, normed, grad_gate, adjoint, column(edge_scaling_factor),
        entry.T, entry, final_sigmoid_matrix,
    )
    pgrad_cols = exchange(pgrad_send.reshape(n, count * count, channels))
    group = 4
    stage = ((half // group, count * half, group * WIDE), BF)
    grad_left, opm_out = call(
        outer_back_kernel,
        [((count * half, WIDE), F32), ((half * half, channels), F32)],
        [stage],
        pgradt, right, outer, qp,
    )
    sens, opm_proj, opm_gain = call(
        column_kernel,
        [((pairs, length, 2 * width), BF), ((width, 2 * half), F32), ((1, 2 * width), F32)],
        [
            ((length * count, channels), F32),
            ((length * half, 128), F32),
            ((length * half, 128), F32),
            stage,
            ((half, WIDE, WIDE), BF),
            ((count * half, WIDE), F32),
            ((width, WIDE), F32),
        ],
        pgrad_cols, left_all, tensor_final_matrix, grad_left, x,
        column(homolog_scaling_factor), tensor_mapping_matrix,
    )
    sensitivity = sens.transpose(1, 0, 2).reshape(depth, count, width)

    factor = 1.0 / (lax.axis_size("dp") * length)
    parts = [opm_out, tri_in, tri_gate, tri_out, opm_proj.reshape(-1, 128)]
    parts += [mid_gain, tri_gain, bias, opm_gain]
    used = sum(p.shape[0] for p in parts)
    each = -(-used // (16 * everyone)) * 16
    parts.append(jnp.zeros((each * everyone - used, 128), F32))
    mine = exchange(
        jnp.concatenate(parts, 0).astype(BF).reshape(everyone, each, 128), ("dp", "dap")
    )
    mine = (jnp.sum(mine.astype(F32), 0) * factor).astype(BF)
    total = exchange(jnp.broadcast_to(mine, (everyone, each, 128)), ("dp", "dap"))
    total = total.reshape(everyone * each, 128).astype(F32)
    found = []
    at = 0
    for p in parts[:-1]:
        found.append(total[at : at + p.shape[0]])
        at += p.shape[0]
    opm_out, tri_in, tri_gate, tri_out, opm_proj, mid_gain, tri_gain, bias, opm_gain = found
    opm_out = opm_out.reshape(half, half, channels).transpose(1, 0, 2).reshape(-1, channels)
    tri_in = tri_in.reshape(2, n, 2, eight, channels).transpose(4, 2, 0, 1, 3)
    return (
        pair_out[None],
        pgrad[None],
        sensitivity[None],
        opm_gain[0, :width],
        opm_proj.reshape(width, 2 * half),
        opm_out,
        bias[0],
        tri_gain[0],
        tri_in.reshape(channels, 4 * channels),
        tri_gate,
        mid_gain[0],
        tri_out,
    )


def solution(mesh):
    placed = (
        P("dp", None, "dap", None),
        P("dp", "dap", None, None),
        P("dp", "dap", None, None),
    ) + (P(),) * 9
    return jax.shard_map(
        local,
        mesh=mesh,
        in_specs=placed,
        out_specs=(
            P("dp", "dap", None, None),
            P("dp", "dap", None, None),
            P("dp", None, "dap", None),
        )
        + (P(),) * 9,
        check_vma=False,
    )
```

time: 636 us -> 259 us (0.41); the launches traced: 626 us -> 257 us
  waiting for transfers between devices: 300 us -> 43.7 us
  local copies, waits for them, and re-layouts: 105 us -> 16.1 us
  Pallas kernels: 0 us -> 84.4 us
  matrix products: 84 us -> 0 us
  other arithmetic: 23.8 us -> 0.29 us
  blocking collectives: 91.8 us -> 81.6 us
  starting transfers between devices: 6.14 us -> 16.3 us
    reduce_scatter x2 -> x0, waiting for transfers between devices: 117 us -> none  [the longest x1 73.7 us: local(): lax.psum_scatter(trilateral_contraction('ijc,kic->kjc', grad_mixed, left_...]
    all_gather x2 -> x1, waiting for transfers between devices: 88.4 us -> 0.02 us  [local(): left_all = lax.all_gather(left_send, 'dap', axis=0, tiled=False)]
    pallas_call x0 -> x8, Pallas kernels: none -> 84.4 us  [call(): pl.pallas_call(kernel, out_shape=[jax.ShapeDtypeStruct(s, t) for s, t in...]
    dot_general x21 -> x0, matrix products: 84 us -> none  [trilateral_contraction(): return jnp.einsum(form, left, right, preferred_element_type=jnp.float32)]
    psum x1 -> x0, waiting for transfers between devices: 83.7 us -> none  [local(): lax.psum((tensor_scaling_sensitivity * factor, outer_projection_gradient...]
    psum x1 -> x0, blocking collectives: 65.7 us -> none  [local(): lax.psum((tensor_scaling_sensitivity * factor, outer_projection_gradient...]
    all_to_all x1 -> x4, blocking collectives: 26.1 us -> 81.6 us  [exchange(): lax.all_to_all(v, axes, split_axis=0, concat_axis=0, tiled=True, axis_ind...]
    convert_element_type x7 -> x0, local copies, waits for them, and re-layouts: 42.3 us -> none  [the longest x1 21.6 us: local(): outer_product_block = (trilateral_contraction('xeb,xdc->edbc', left_proje...]
  transfers between devices with their start and end apart: 6 -> 6, of which waited for: 6 -> 4; matrix products, arithmetic and copies ran while one was open for 9% -> 1% of each run, Pallas kernels for 0% -> 24%
where the time goes in v1:
time: 259 us; the launch traced here: 257 us
  Pallas kernels  84.4 us (33%)
  blocking collectives  81.6 us (32%)
  waiting for transfers between devices  43.7 us (17%)
  starting transfers between devices  16.3 us (6%)
  local copies, waits for them, and re-layouts  16.1 us (6%)
  between operations  14.4 us (6%)
    pallas_call x8, Pallas kernels, call(): pl.pallas_call(kernel, out_shape=[jax.ShapeDtypeStruct(s, t) for s, t in...  84.4 us
    all_to_all x4, blocking collectives, exchange(): lax.all_to_all(v, axes, split_axis=0, concat_axis=0, tiled=True, axis_ind...  81.6 us
    all_to_all x4, waiting for transfers between devices, exchange(): lax.all_to_all(v, axes, split_axis=0, concat_axis=0, tiled=True, axis_ind...  41.3 us
    all_to_all x4, starting transfers between devices, exchange(): lax.all_to_all(v, axes, split_axis=0, concat_axis=0, tiled=True, axis_ind...  16.3 us
    unnamed x41, local copies, waits for them, and re-layouts  7.19 us
  transfers between devices with their start and end apart: 6, of which 4 were waited for; matrix products, arithmetic and copies ran while one was open for 1% of the time, Pallas kernels for 24%

profile of v1, /device:TPU:0, one launch (start us, length us, event | category | flops | bytes accessed | tf_op | source)
XLA Modules:
  0.0 256.8 jit_solution(15545405202599040352)
XLA Ops:
  7.2 0.0 all-gather.3.cloned.1.call-start
  7.2 1.2 copy.77
  8.4 0.8 copy.79.gain_ref.mgain_ref
  9.2 0.8 copy.78
  10.0 2.8 %shard_map.211 = (bf16[12,32,256]{2,1,0:T(8,128)(2,1)S(1)}, bf16[6,3,32,128]{3,2,1,0:T(8,128)(2,1)}, bf16[6,3,32,128]{3,2,1,0:T(8,128)(2,1)S(1)}) custom-call(bf16[6,192,128]{2,1,0:T(8,128)(2,1)S(1)} %bitcast.50, f32[64,1]{1,0:T(8,128)S(1)} %copy.79.gain_ref.mgain_ref, bf16[64,64]{1,0:T(8,128)(2,1)S(1)} %bitcast.64), custom_call_target="tpu_custom_call" | custom-call | tf_op jit(solution)/shard_map/pallas_call | solution.py:67
  12.8 0.2 broadcast_in_dim.15
  13.0 0.0 copy-start.14
  13.0 0.0 copy-start.1
  13.0 22.7 %all_to_all.40.own_ref = bf16[8,6,3,32,128]{4,3,2,1,0:T(8,128)(2,1)} all-to-all(bf16[8,6,3,32,128]{4,3,2,1,0:T(8,128)(2,1)S(1)} %broadcast_in_dim.15), channel_id=1, replica_groups={{0,2,4,6,8,10,12,14},{1,3,5,7,9,11,13,15},{16,18,20,22,24,26,28,30},{17..., dimensions={0} | all-to-all | bytes 2359296 | tf_op jit(solution)/shard_map/all_to_all | solution.py:401
  35.7 0.0 collective-permute-start
  35.8 0.0 all-gather.3.cloned.1.call-update
  35.8 0.0 copy-done.14
  35.8 0.1 copy.81
  36.0 0.1 copy.80
  36.1 0.1 copy.83.wt_ref
  36.2 0.2 copy-done.15
  36.4 0.1 copy.85.gain_ref
  36.5 0.0 copy-done.16
  36.5 0.1 copy.84.bias_ref
  36.6 2.3 collective-permute-done.other_ref
  38.9 25.5 %shard_map.212 = (bf16[16,6,3,16,128]{4,3,2,1,0:T(8,128)(2,1)S(1)}, f32[12,128,256]{2,1,0:T(8,128)}, bf16[12,128,256]{2,1,0:T(8,128)(2,1)S(1)}, bf16[32,256,256]{2,1,0:T(8,128)(2,1)}, bf16[12,1024,256]{2,1,0:T(8,128)(2,1)}) custom-call(s32[1]{0:T(128)} %bitcast.par_ref, bf16[8,6,3,32,128]{4,3,2,1,0:T(8,128)(2,1)} %all_to_all.40.own_ref, ...), custom_call_target="tpu_custom_call" | custom-call | tf_op jit(solution)/shard_map/pallas_call | solution.py:67
  64.4 20.5 %all_to_all.41.edges_ref = bf16[16,6,3,16,128]{4,3,2,1,0:T(8,128)(2,1)S(1)} all-to-all(bf16[16,6,3,16,128]{4,3,2,1,0:T(8,128)(2,1)S(1)} %get-tuple-element.42), channel_id=1, replica_groups=mesh['dp'=8,'dap'=16] {'dap'}, dimensions={0} | all-to-all | bytes 2359296 | tf_op jit(solution)/shard_map/all_to_all | solution.py:401
  84.9 3.8 %shard_map.213 = (bf16[16,3,3,16,128]{4,3,2,1,0:T(8,128)(2,1)S(1)}, bf16[8,192,256]{2,1,0:T(8,128)(2,1)S(1)}, bf16[8,192,256]{2,1,0:T(8,128)(2,1)S(1)}) custom-call(bf16[16,6,3,16,128]{4,3,2,1,0:T(8,128)(2,1)S(1)} %all_to_all.41.edges_ref), custom_call_target="tpu_custom_call" | custom-call | tf_op jit(solution)/shard_map/pallas_call | solution.py:67
  88.7 0.9 copy-done.5
  89.6 0.9 copy-done.7
  90.5 0.8 copy-done.9
  91.4 3.6 %all-to-all-start.2 = ((bf16[16,3,3,16,128]{4,3,2,1,0:T(8,128)(2,1)}), bf16[16,3,3,16,128]{4,3,2,1,0:T(8,128)(2,1)S(1)}, u32[]{:S(2)}, u32[]{:S(2)}) async-start(bf16[16,3,3,16,128]{4,3,2,1,0:T(8,128)(2,1)} %copy-done.9), calls=%async_computation.2 | async-start | bytes 1179648 | tf_op jit(solution)/shard_map/all_to_all | solution.py:401
  95.0 0.1 copy.88.cgain_ref
  95.1 0.1 copy.86
  95.2 0.0 copy-done.12
  95.2 0.1 copy.87
  95.3 11.2 %all-to-all-done.2.mixed_ref = bf16[16,3,3,16,128]{4,3,2,1,0:T(8,128)(2,1)S(1)} async-done(((bf16[16,3,3,16,128]{4,3,2,1,0:T(8,128)(2,1)}), bf16[16,3,3,16,128]{4,3,2,1,0:T(8,128)(2,1)S(1)}, u32[]{:S(2)}, u32[]{:S(2)}) %all-to-all-start.2) | async-done | bytes 589856 | tf_op jit(solution)/shard_map/all_to_all | solution.py:401
  106.5 6.3 %shard_map.214 = (bf16[12,192,128]{2,1,0:T(8,128)(2,1)}, bf16[16,3,3,16,128]{4,3,2,1,0:T(8,128)(2,1)S(1)}, bf16[12,128,256]{2,1,0:T(8,128)(2,1)S(1)}, f32[128,12...) custom-call(bf16[16,3,3,16,128]{4,3,2,1,0:T(8,128)(2,1)S(1)} %all-to-all-done.2.mixed_ref, ...), custom_call_target="tpu_custom_call" | custom-call | tf_op jit(solution)/shard_map/pallas_call | solution.py:67
  112.8 0.9 copy-done.2
  113.7 14.3 %all_to_all.42.grads_ref = bf16[16,3,3,16,128]{4,3,2,1,0:T(8,128)(2,1)S(1)} all-to-all(bf16[16,3,3,16,128]{4,3,2,1,0:T(8,128)(2,1)S(1)} %get-tuple-element.47), channel_id=1, replica_groups=mesh['dp'=8,'dap'=16] {'dap'}, dimensions={0} | all-to-all | bytes 1179648 | tf_op jit(solution)/shard_map/all_to_all | solution.py:401
  128.0 0.0 copy-done.6
  128.0 5.1 %shard_map.215 = bf16[16,6,3,16,128]{4,3,2,1,0:T(8,128)(2,1)} custom-call(bf16[16,3,3,16,128]{4,3,2,1,0:T(8,128)(2,1)S(1)} %all_to_all.42.grads_ref, bf16[8,192,256]{2,1,0:T(8,128)(2,1)S(1)} %copy-done.6, bf16[8,192,256]{2,1,0:T(8,128)(2,1)S(1)} %copy-done.8), custom_call_target="tpu_custom_call" | custom-call | tf_op jit(solution)/shard_map/pallas_call | solution.py:67
  133.1 4.4 %all-to-all-start.4 = ((bf16[16,6,3,16,128]{4,3,2,1,0:T(8,128)(2,1)}), bf16[16,6,3,16,128]{4,3,2,1,0:T(8,128)(2,1)}, u32[]{:S(2)}, u32[]{:S(2)}) async-start(bf16[16,6,3,16,128]{4,3,2,1,0:T(8,128)(2,1)} %shard_map.215), calls=%async_computation.4 | async-start | bytes 2359296 | tf_op jit(solution)/shard_map/all_to_all | solution.py:401
  137.5 0.1 copy.90.entry_ref
  137.6 17.8 %all-to-all-done.4.grads_ref = bf16[16,6,3,16,128]{4,3,2,1,0:T(8,128)(2,1)} async-done(((bf16[16,6,3,16,128]{4,3,2,1,0:T(8,128)(2,1)}), bf16[16,6,3,16,128]{4,3,2,1,0:T(8,128)(2,1)}, u32[]{:S(2)}, u32[]{:S(2)}) %all-to-all-start.4) | async-done | bytes 1179680 | tf_op jit(solution)/shard_map/all_to_all | solution.py:401
  155.4 8.8 %shard_map.216 = (bf16[12,192,128]{2,1,0:T(8,128)(2,1)}, bf16[12,128,256]{2,1,0:T(8,128)(2,1)S(1)}, bf16[2304,128]{1,0:T(8,128)(2,1)}, f32[512,128]{1,0:T(8,128)...) custom-call(bf16[16,6,3,16,128]{4,3,2,1,0:T(8,128)(2,1)} %all-to-all-done.4.grads_ref, ...), custom_call_target="tpu_custom_call" | custom-call | tf_op jit(solution)/shard_map/pallas_call | solution.py:67
  164.2 0.9 copy-done.3
  165.0 3.7 %all-to-all-start.5 = ((bf16[16,144,128]{2,1,0:T(8,128)(2,1)}), bf16[16,144,128]{2,1,0:T(8,128)(2,1)S(1)}, u32[]{:S(2)}, u32[]{:S(2)}) async-start(bf16[16,144,128]{2,1,0:T(8,128)(2,1)} %bitcast.23), calls=%async_computation.5 | async-start | bytes 1179648 | tf_op jit(solution)/shard_map/all_to_all | solution.py:401
  168.8 13.1 %shard_map.217 = (f32[384,256]{1,0:T(8,128)S(1)}, f32[1024,128]{1,0:T(8,128)S(1)}) custom-call(bf16[12,128,256]{2,1,0:T(8,128)(2,1)S(1)} %copy-done.4, bf16[32,256,256]{2,1,0:T(8,128)(2,1)} %get-tuple-element.55.right_ref, bf16[12,1024,256]{2,1,0:T(8,128)(2,1)} %get-tuple-element.56.outer_ref, bf16[1024,128]{1,0:T(8,128)(2,1)S(1)} %bitcast.55), custom_call_target="tpu_custom_call" | custom-call | tf_op jit(solution)/shard_map/pallas_call | solution.py:67
  181.9 0.0 copy-start.13
  182.0 0.0 all-gather.3.cloned.1.call-done
  182.0 0.0 all-to-all-done.5.pcol_ref
  182.0 0.6 copy-done.13
  182.6 19.0 %shard_map.218 = (bf16[6,192,128]{2,1,0:T(8,128)(2,1)S(1)}, f32[64,64]{1,0:T(8,128)S(1)}, f32[1,128]{1,0:T(1,128)S(1)}) custom-call(bf16[16,144,128]{2,1,0:T(8,128)(2,1)S(1)} %all-to-all-done.5.pcol_ref, bf16[16,6,3,32,128]{4,3,2,1,0:T(8,128)(2,1)} %bitcast.65, bf16[1024,128]{1,0:T(8,128)(2,1)S(1)} %copy-done.1, f32[384,256]{1,0:T(8,128)S(1)} %get-tuple-element.57.gleft_ref, ...), custom_call_target="tpu_custom_call" | custom-call | tf_op jit(solution)/shard_map/pallas_call | solution.py:67
  201.7 0.1 reshape.98
  201.8 0.6 concatenate.4
  202.4 24.1 %all_to_all.43 = bf16[128,16,128]{2,1,0:T(8,128)(2,1)S(1)} all-to-all(bf16[128,16,128]{2,1,0:T(8,128)(2,1)S(1)} %bitcast.66), channel_id=1, replica_groups=mesh['dp'=8,'dap'=16] {'dp','dap'}, dimensions={0} | all-to-all | bytes 1048576 | tf_op jit(solution)/shard_map/all_to_all | solution.py:401
  226.5 0.1 convert_reduce_fusion
  226.6 0.9 broadcast_in_dim.19
  227.5 4.6 %all-to-all-start.7 = ((bf16[128,16,128]{2,1,0:T(8,128)(2,1)}), bf16[128,16,128]{2,1,0:T(8,128)(2,1)S(1)}, u32[]{:S(2)}, u32[]{:S(2)}) async-start(bf16[128,16,128]{2,1,0:T(8,128)(2,1)} %broadcast_in_dim.19), calls=%async_computation.7 | async-start | bytes 1048576 | tf_op jit(solution)/shard_map/all_to_all | solution.py:401
  232.1 0.9 copy.92
  233.0 12.4 %all-to-all-done.7 = bf16[128,16,128]{2,1,0:T(8,128)(2,1)S(1)} async-done(((bf16[128,16,128]{2,1,0:T(8,128)(2,1)}), bf16[128,16,128]{2,1,0:T(8,128)(2,1)S(1)}, u32[]{:S(2)}, u32[]{:S(2)}) %all-to-all-start.7) | async-done | bytes 524320 | tf_op jit(solution)/shard_map/all_to_all | solution.py:401
  245.5 0.1 convert_element_type.20
  245.5 0.5 slice_bitcast_fusion
  246.1 0.5 slice_bitcast_fusion.3
  246.6 1.1 copy.93
  247.8 0.8 copy.95
  248.6 0.7 reshape.99
  249.3 0.7 fusion
  (38 shorter events, 0.2 us)
Async XLA Ops:
  7.2 174.8 %all-gather.3.cloned.1.call-start = ((), (), s32[]{:S(2)}) async-start(), calls=%async_computation.8 | async-start | bytes 2506752 | tf_op jit(solution)/shard_map/all_gather | solution.py:446
  13.0 22.8 %copy-start.14 = (bf16[128,512]{1,0:T(8,128)(2,1)S(1)}, bf16[128,512]{1,0:T(8,128)(2,1)}, u32[]{:S(2)}) copy-start(bf16[128,512]{1,0:T(8,128)(2,1)} %param.20) | copy-start | bytes 393220
  13.0 23.0 %copy-start.1 = (bf16[1024,128]{1,0:T(8,128)(2,1)S(1)}, bf16[1024,128]{1,0:T(8,128)(2,1)}, u32[]{:S(2)}) copy-start(bf16[1024,128]{1,0:T(8,128)(2,1)} %w_ref.1) | copy-start | bytes 786436
  35.7 0.7 copy-start.15
  35.7 0.8 copy-start.16
  35.7 3.2 %copy-start.10 = (bf16[1,12,192,128]{3,2,1,0:T(8,128)(2,1)S(1)}, bf16[1,12,192,128]{3,2,1,0:T(8,128)(2,1)}, u32[]{:S(2)}) copy-start(bf16[1,12,192,128]{3,2,1,0:T(8,128)(2,1)} %param.13) | copy-start | bytes 1769476
  35.7 3.2 %collective-permute-start = (bf16[8,6,3,32,128]{4,3,2,1,0:T(8,128)(2,1)}, bf16[8,6,3,32,128]{4,3,2,1,0:T(8,128)(2,1)}, u32[]{:S(2)}, u32[]{:S(2)}) collective-permute-start(bf16[8,6,3,32,128]{4,3,2,1,0:T(8,128)(2,1)} %all_to_all.40.own_ref), channel_id=1, source_target_pairs={{0,1},{1,0},{2,3},{3,2},{4,5},{5,4},{6,7},{7,6},{8,9},{9,8},{10,11... | collective-permute-start | bytes 3538952 | tf_op jit(solution)/shard_map/ppermute | solution.py:445
  84.9 10.1 %copy-start.17 = (f32[128]{0:T(128)S(1)}, f32[128]{0:T(128)}, u32[]{:S(2)}) copy-start(f32[128]{0:T(128)} %param.22) | copy-start | bytes 1540
  84.9 10.2 %copy-start.11 = (bf16[128,128]{1,0:T(8,128)(2,1)S(1)}, bf16[128,128]{1,0:T(8,128)(2,1)}, u32[]{:S(2)}) copy-start(bf16[128,128]{1,0:T(8,128)(2,1)} %wf_ref.1) | copy-start | bytes 98308
  84.9 10.3 %copy-start.12 = (bf16[128,128]{1,0:T(8,128)(2,1)S(1)}, bf16[128,128]{1,0:T(8,128)(2,1)}, u32[]{:S(2)}) copy-start(bf16[128,128]{1,0:T(8,128)(2,1)} %wg_ref.1) | copy-start | bytes 98308
  84.9 21.6 %copy-start = (bf16[1,12,192,128]{3,2,1,0:T(8,128)(2,1)S(1)}, bf16[1,12,192,128]{3,2,1,0:T(8,128)(2,1)}, u32[]{:S(2)}) copy-start(bf16[1,12,192,128]{3,2,1,0:T(8,128)(2,1)} %param.14) | copy-start | bytes 1769476
  88.7 0.9 copy-start.5
  89.6 0.9 copy-start.7
  90.5 0.8 copy-start.9
  91.4 15.1 %all-to-all-start.2 = ((bf16[16,3,3,16,128]{4,3,2,1,0:T(8,128)(2,1)}), bf16[16,3,3,16,128]{4,3,2,1,0:T(8,128)(2,1)S(1)}, u32[]{:S(2)}, u32[]{:S(2)}) async-start(bf16[16,3,3,16,128]{4,3,2,1,0:T(8,128)(2,1)} %copy-done.9), calls=%async_computation.2 | async-start | bytes 1179648 | tf_op jit(solution)/shard_map/all_to_all | solution.py:401
  106.5 21.5 %copy-start.8 = (bf16[8,192,256]{2,1,0:T(8,128)(2,1)S(1)}, bf16[8,192,256]{2,1,0:T(8,128)(2,1)}, u32[]{:S(2)}) copy-start(bf16[8,192,256]{2,1,0:T(8,128)(2,1)} %copy-done.7) | copy-start | bytes 2359300
  112.8 0.9 copy-start.2
  113.7 14.3 %copy-start.6 = (bf16[8,192,256]{2,1,0:T(8,128)(2,1)S(1)}, bf16[8,192,256]{2,1,0:T(8,128)(2,1)}, u32[]{:S(2)}) copy-start(bf16[8,192,256]{2,1,0:T(8,128)(2,1)} %copy-done.5) | copy-start | bytes 2359300
  133.1 22.3 %all-to-all-start.4 = ((bf16[16,6,3,16,128]{4,3,2,1,0:T(8,128)(2,1)}), bf16[16,6,3,16,128]{4,3,2,1,0:T(8,128)(2,1)}, u32[]{:S(2)}, u32[]{:S(2)}) async-start(bf16[16,6,3,16,128]{4,3,2,1,0:T(8,128)(2,1)} %shard_map.215), calls=%async_computation.4 | async-start | bytes 2359296 | tf_op jit(solution)/shard_map/all_to_all | solution.py:401
  164.2 0.9 copy-start.3
  165.0 3.8 %copy-start.4 = (bf16[12,128,256]{2,1,0:T(8,128)(2,1)S(1)}, bf16[12,128,256]{2,1,0:T(8,128)(2,1)}, u32[]{:S(2)}) copy-start(bf16[12,128,256]{2,1,0:T(8,128)(2,1)} %copy-done.3) | copy-start | bytes 2359300
  165.0 17.0 %all-to-all-start.5 = ((bf16[16,144,128]{2,1,0:T(8,128)(2,1)}), bf16[16,144,128]{2,1,0:T(8,128)(2,1)S(1)}, u32[]{:S(2)}, u32[]{:S(2)}) async-start(bf16[16,144,128]{2,1,0:T(8,128)(2,1)} %bitcast.23), calls=%async_computation.5 | async-start | bytes 1179648 | tf_op jit(solution)/shard_map/all_to_all | solution.py:401
  181.9 0.7 copy-start.13
  227.5 18.0 %all-to-all-start.7 = ((bf16[128,16,128]{2,1,0:T(8,128)(2,1)}), bf16[128,16,128]{2,1,0:T(8,128)(2,1)S(1)}, u32[]{:S(2)}, u32[]{:S(2)}) async-start(bf16[128,16,128]{2,1,0:T(8,128)(2,1)} %broadcast_in_dim.19), calls=%async_computation.7 | async-start | bytes 1048576 | tf_op jit(solution)/shard_map/all_to_all | solution.py:401
Sparse Core Ops, SparseCore 0:
  35.9 35.0 all-gather.2

commit v2 on v1

v2 whole, which is shorter than its diff:
```python
import jax
import jax.numpy as jnp
from jax import lax
from jax.experimental import pallas as pl
from jax.experimental.pallas import tpu as pltpu
from jax.sharding import PartitionSpec as P

EPSILON = 1e-05
BF = jnp.bfloat16
F32 = jnp.float32
WIDE = 256


def nn(a, b):
    return lax.dot_general(a, b, (((1,), (0,)), ((), ())), preferred_element_type=F32)


def nt(a, b):
    return lax.dot_general(a, b, (((1,), (1,)), ((), ())), preferred_element_type=F32)


def tn(a, b):
    return lax.dot_general(a, b, (((0,), (0,)), ((), ())), preferred_element_type=F32)


def norm(v):
    centred = v - jnp.mean(v, 0, keepdims=True)
    inverse = lax.rsqrt(jnp.mean(centred * centred, 0, keepdims=True) + EPSILON)
    return centred * inverse, inverse


def norm_back(h, hat, inverse):
    first = jnp.mean(h, 0, keepdims=True)
    second = jnp.mean(h * hat, 0, keepdims=True)
    return (h - first - hat * second) * inverse


def sigmoid(v):
    return 1.0 / (1.0 + jnp.exp(-v))


def pad_rows(v, rows):
    return jnp.concatenate([v, jnp.zeros((rows - v.shape[0],) + v.shape[1:], v.dtype)], 0)


def flip(v):
    return pad_rows(v, WIDE).T


def low_half(v):
    lane = lax.broadcasted_iota(jnp.int32, v.shape, v.ndim - 1)
    return jnp.where(lane < 64, v, 0.0)


def pack(a, b):
    tail = low_half(a[:, 128:]) + pltpu.roll(low_half(b[:, 128:]), 64, 1)
    return a[:, :128], b[:, :128], tail


def unpack(t0, t1, t2):
    return (t0, low_half(t2)), (t1, low_half(pltpu.roll(t2, 64, 1)))


def as_column(row_ref):
    n = row_ref.shape[1]
    a = lax.broadcasted_iota(jnp.int32, (n, n), 0)
    b = lax.broadcasted_iota(jnp.int32, (n, n), 1)
    return jnp.sum(jnp.where(a == b, row_ref[...], 0.0), 1, keepdims=True)


def as_row(column):
    n = column.shape[0]
    a = lax.broadcasted_iota(jnp.int32, (n, n), 0)
    b = lax.broadcasted_iota(jnp.int32, (n, n), 1)
    return jnp.sum(jnp.where(a == b, column, 0.0), 0, keepdims=True)


def call(kernel, outs, scratch, *operands, smem=0, away=0, copies=0):
    specs = [pl.BlockSpec(memory_space=pltpu.SMEM)] * smem
    specs += [pl.BlockSpec(memory_space=pltpu.VMEM)] * (len(operands) - smem)
    room = [pltpu.VMEM(s, t) for s, t in scratch]
    if copies:
        room.append(pltpu.SemaphoreType.DMA((copies,)))
    return pl.pallas_call(
        kernel,
        out_shape=[jax.ShapeDtypeStruct(s, t) for s, t in outs],
        in_specs=specs,
        out_specs=[pl.BlockSpec(memory_space=pltpu.VMEM)] * (len(outs) - away)
        + [pl.BlockSpec(memory_space=pl.ANY)] * away,
        scratch_shapes=room,
        compiler_params=pltpu.CompilerParams(vmem_limit_bytes=50 * 1024 * 1024),
    )(*operands)


def project_kernel(x_ref, gain_ref, w_ref, left_ref, lsend_ref, rsend_ref):
    pairs = x_ref.shape[0]
    width = w_ref.shape[0]
    half = w_ref.shape[1] // 2
    gain = as_column(gain_ref)

    @pl.loop(0, pairs)
    def _(m):
        x = flip(x_ref[m].astype(F32))
        both = []
        for o in range(2):
            hat, _ = norm(x[o * width : (o + 1) * width])
            proj = tn(w_ref[...], (hat * gain).astype(BF))
            both.append(proj)
            left_ref[2 * m + o] = proj[:half].astype(BF)
        for t, v in enumerate(pack(both[0][:half], both[1][:half])):
            lsend_ref[m, t] = v.astype(BF)
        for t, v in enumerate(pack(both[0][half:], both[1][half:])):
            rsend_ref[m, t] = v.astype(BF)


def load_wide(head, tail, start, count, stride):
    a = head[pl.ds(start, count, stride=stride), :]
    b = tail[pl.ds(start, count, stride=stride), :]
    return jnp.concatenate([a, b], 1)


def store_wide(head, tail, start, count, stride, v):
    head[pl.ds(start, count, stride=stride), :] = v[:, :128]
    tail[pl.ds(start, count, stride=stride), :] = v[:, 128:]


def spread_projections(source, first, step, pitch, head, tail):
    pairs, _, half, _ = source.shape
    for m in range(pairs):
        t = source[m].astype(F32)
        for o, (a, b) in enumerate(unpack(t[0], t[1], t[2])):
            at = pl.ds((first + step * (2 * m + o)) * pitch, half)
            head[at, :] = a
            tail[at, :] = b


def outer_kernel(
    par_ref, own_ref, other_ref, left_ref, edge_ref, wt_ref, bias_ref, gain_ref, entry_ref,
    send_ref, mid_ref, normed_ref, right_out, outer_out,
    head, tail, right_ref, outer_ref, sems,
):
    chips, pairs, _, half, _ = own_ref.shape
    rows = left_ref.shape[0]
    length = edge_ref.shape[1]
    depth = 1.0 / length
    pitch = half + 1
    par = par_ref[0]
    for source, p in ((own_ref, par), (other_ref, 1 - par)):

        @pl.loop(0, chips)
        def _(chip):
            spread_projections(source.at[chip], (2 * chip + p) * rows, 1, pitch, head, tail)

    left = left_ref[...].reshape(rows * half, WIDE)

    @pl.loop(0, half, unroll=4)
    def _(q):
        r = pad_rows(load_wide(head, tail, q, length, pitch), WIDE).astype(BF)
        right_ref[q] = r
        o = (nt(left, r) * depth).astype(BF)
        at = pl.ds(pl.multiple_of(q * half, half), half)
        for i in range(rows):
            outer_ref[i, at, :] = o[i * half : (i + 1) * half]

    copies = [
        pltpu.make_async_copy(right_ref, right_out, sems.at[0]),
        pltpu.make_async_copy(outer_ref, outer_out, sems.at[1]),
    ]
    for c in copies:
        c.start()
    devices, _, _, sixteen, _ = send_ref.shape
    bias = as_column(bias_ref)
    gain = as_column(gain_ref)

    @pl.loop(0, pairs)
    def _(m):
        both = []
        for o in range(2):
            i = 2 * m + o
            mid = flip(edge_ref[i].astype(F32)) + (nn(wt_ref[...], outer_ref[i]) + bias)
            mid_ref[i] = mid
            hat, _ = norm(mid)
            normed = (hat * gain).astype(BF)
            normed_ref[i] = normed
            raw = nn(entry_ref[...], normed)
            cut = raw.shape[0] // 2
            both.append(sigmoid(raw[:cut]) * raw[cut:])
        for t, v in enumerate(pack(*both)):
            send_ref[:, m, t] = v.reshape(devices, sixteen, 128).astype(BF)

    for c in copies:
        c.wait()


def gate_kernel(normed_ref, adj_ref, wg_ref, gate_ref, up_ref):
    @pl.loop(0, normed_ref.shape[0])
    def _(i):
        gate_ref[i] = sigmoid(tn(wg_ref[...], normed_ref[i]))
        up_ref[i] = flip(adj_ref[i].astype(F32)).astype(BF)


def spread(source, half, head, tail):
    devices, pairs, _, high, _ = source.shape
    many = high // half

    @pl.loop(0, devices)
    def _(d):
        for m in range(pairs):
            t = source[d, m].astype(F32)
            for o, (a, b) in enumerate(unpack(t[0], t[1], t[2])):
                for g in range(many):
                    at = pl.ds((((d * pairs + m) * 2 + o) * many + g) * (half + 1), half)
                    head[at, :] = a[g * half : (g + 1) * half]
                    tail[at, :] = b[g * half : (g + 1) * half]


def gather_up(half, head, tail, target):
    devices, pairs, _, high, _ = target.shape
    many = high // half

    @pl.loop(0, devices)
    def _(d):
        for m in range(pairs):
            wide = []
            for o in range(2):
                got = []
                for g in range(many):
                    at = pl.ds((((d * pairs + m) * 2 + o) * many + g) * (half + 1), half)
                    got.append(jnp.concatenate([head[at, :], tail[at, :]], 1))
                wide.append(jnp.concatenate(got, 0))
            for t, v in enumerate(pack(*wide)):
                target[d, m, t] = v.astype(BF)


def triangle_kernel(edges_ref, send_ref, left_ref, right_ref, head, tail, mhead, mtail):
    channels, length, _ = left_ref.shape
    spread(edges_ref, 2 * channels, head, tail)
    for c in range(channels):
        a = load_wide(head, tail, c, length, 2 * channels + 1).astype(BF)
        b = load_wide(head, tail, channels + c, length, 2 * channels + 1).astype(BF)
        left_ref[c] = a
        right_ref[c] = b
        mixed = tn(a, b)[:length]
        store_wide(mhead, mtail, c, length, channels + 1, mixed)
    gather_up(channels, mhead, mtail, send_ref)


def triangle_back_kernel(grads_ref, left_ref, right_ref, send_ref, head, tail, mhead, mtail):
    channels, length, _ = left_ref.shape
    spread(grads_ref, channels, mhead, mtail)
    for c in range(channels):
        g = pad_rows(load_wide(mhead, mtail, c, length, channels + 1), WIDE).astype(BF)
        store_wide(head, tail, c, length, 2 * channels + 1, nt(right_ref[c], g))
        store_wide(head, tail, channels + c, length, 2 * channels + 1, nn(left_ref[c], g))
    gather_up(2 * channels, head, tail, send_ref)


def mixed_rows(mixed_ref, n):
    devices, _, _, sixteen, _ = mixed_ref.shape
    eight = sixteen // 2
    t = [mixed_ref[:, n, k].astype(F32).reshape(devices * sixteen, 128) for k in range(3)]
    out = []
    for a, b in unpack(*t):
        block = jnp.concatenate([a, b], 1).reshape(devices, 2, eight, WIDE)
        out += [block[:, o].reshape(devices * eight, WIDE) for o in range(2)]
    return out


def update_kernel(mixed_ref, gate_ref, up_ref, cgain_ref, wf_ref, send_ref):
    devices, quads, _, sixteen, _ = mixed_ref.shape
    cgain = as_column(cgain_ref)

    @pl.loop(0, quads)
    def _(n):
        grads = []
        for k, mixed in enumerate(mixed_rows(mixed_ref, n)):
            i = 4 * n + k
            hat, inverse = norm(mixed)
            gu = (up_ref[i].astype(F32) * gate_ref[i]).astype(BF)
            gmn = nn(wf_ref[...], gu)
            back = norm_back(gmn * cgain, hat, inverse)
            grads.append(back.reshape(devices, 1, sixteen // 2, WIDE))
        packed = [
            jnp.concatenate(grads[2 * o : 2 * o + 2], 1).reshape(devices * sixteen, WIDE)
            for o in range(2)
        ]
        for k, v in enumerate(pack(*packed)):
            send_ref[:, n, k] = v.reshape(devices, sixteen, 128).astype(BF)


def result_kernel(
    mixed_ref, mid_ref, normed_ref, gate_ref, up_ref, cgain_ref, wf_ref,
    out_ref, ggate_ref, wfg_ref, wgg_ref, msum_ref, acc,
):
    _, quads, _, _, _ = mixed_ref.shape
    length = out_ref.shape[1]
    wfg_ref[...] = jnp.zeros_like(wfg_ref)
    wgg_ref[...] = jnp.zeros_like(wgg_ref)
    acc[...] = jnp.zeros_like(acc)
    cgain = as_column(cgain_ref)

    @pl.loop(0, quads)
    def _(n):
        for k, mixed in enumerate(mixed_rows(mixed_ref, n)):
            i = 4 * n + k
            hat, _ = norm(mixed)
            mn = (hat * cgain).astype(BF)
            gate = gate_ref[i]
            update = tn(wf_ref[...], mn)
            new = mid_ref[i] + gate * update
            out_ref[i] = new.T[:length].astype(BF)
            upgate = up_ref[i].astype(F32) * gate
            gu = upgate.astype(BF)
            gg = (upgate * update * (1.0 - gate)).astype(BF)
            ggate_ref[i] = gg
            wfg_ref[...] += nt(mn, gu)
            wgg_ref[...] += nt(normed_ref[i], gg)
            acc[...] += nn(wf_ref[...], gu) * hat

    msum_ref[...] = jnp.sum(acc[...].T, 0, keepdims=True)


def edge_back_kernel(
    grads_ref, mid_ref, normed_ref, ggate_ref, up_ref, gain_ref, entryt_ref, entry_ref, wg_ref,
    pgrad_ref, pgradt_ref, send_ref, win_ref, gsum_ref, bsum_ref, gacc, bacc, rows,
):
    devices, pairs, _, sixteen, _ = grads_ref.shape
    count, length, channels = pgrad_ref.shape
    win_ref[...] = jnp.zeros_like(win_ref)
    gacc[...] = jnp.zeros_like(gacc)
    bacc[...] = jnp.zeros_like(bacc)
    gain = as_column(gain_ref)

    @pl.loop(0, pairs)
    def _(m):
        t = [grads_ref[:, m, k].astype(F32).reshape(devices * sixteen, 128) for k in range(3)]
        for o, (a, b) in enumerate(unpack(*t)):
            i = 2 * m + o
            grad = jnp.concatenate([a, b], 1)
            normed = normed_ref[i]
            raw = nn(entryt_ref[...], normed)
            cut = raw.shape[0] // 2
            sig = sigmoid(raw[:cut])
            gs = grad * sig
            graw = jnp.concatenate([gs * raw[cut:] * (1.0 - sig), gs], 0).astype(BF)
            win_ref[...] += nt(graw, normed)
            gpn = nn(entry_ref[...], graw) + nn(wg_ref[...], ggate_ref[i])
            hat, inverse = norm(mid_ref[i])
            gacc[...] += gpn * hat
            gmid = up_ref[i].astype(F32) + norm_back(gpn * gain, hat, inverse)
            bacc[...] += gmid
            pgradt_ref[i] = gmid.astype(BF)
            turned = gmid.T[:length]
            pgrad_ref[i] = turned.astype(BF)
            rows[pl.ds(i, length, stride=count), :] = turned

    send_ref[...] = rows[...].astype(BF)
    gsum_ref[...] = jnp.sum(gacc[...].T, 0, keepdims=True)
    bsum_ref[...] = jnp.sum(bacc[...].T, 0, keepdims=True)


def prepare_kernel(par_ref, own_ref, other_ref, x_ref, left_ref, hat_ref, inv_ref, head, tail):
    chips, pairs, _, half, _ = own_ref.shape
    length = left_ref.shape[1] * 3 // 4
    devices = 2 * chips
    pitch = half + 1
    par = par_ref[0]
    for source, p in ((own_ref, par), (other_ref, 1 - par)):

        @pl.loop(0, chips)
        def _(chip):
            spread_projections(source.at[chip], 2 * chip + p, devices, pitch, head, tail)

    @pl.loop(0, half, unroll=2)
    def _(q):
        left_ref[q] = pad_rows(load_wide(head, tail, q, length, pitch), WIDE).astype(BF)

    width = hat_ref.shape[1]

    @pl.loop(0, pairs)
    def _(m):
        x = flip(x_ref[m].astype(F32))
        for o in range(2):
            hat, inverse = norm(x[o * width : (o + 1) * width])
            hat_ref[2 * m + o] = hat
            inv_ref[2 * m + o] = inverse


def put(stage, i, g):
    half = g.shape[0] // (stage.shape[0] * (stage.shape[2] // WIDE))
    group = stage.shape[2] // WIDE
    at = pl.ds(pl.multiple_of(i * half, half), half)
    for q in range(g.shape[0] // half):
        lanes = slice((q % group) * WIDE, (q % group + 1) * WIDE)
        stage[q // group, at, lanes] = g[q * half : (q + 1) * half]


def contract(stage, projections, total):
    group = stage.shape[2] // WIDE
    total[...] = jnp.zeros_like(total)

    @pl.loop(0, stage.shape[0], unroll=2)
    def _(k):
        r = projections[pl.ds(k * group, group)].reshape(group * WIDE, WIDE)
        total[...] += nn(stage[k], r)


def squeeze(v):
    n = v.shape[0] // 4
    out = v[:n]
    for k in range(1, 4):
        out = out + pltpu.roll(v[k * n : (k + 1) * n], 32 * k, 1)
    return out


def outer_back_kernel(
    pgradt_ref, right_ref, outer_ref, w_ref, hat_ref, grad_ref, wout_ref, cross_ref,
    stage, wacc, cacc,
):
    count, _, _ = pgradt_ref.shape
    half = right_ref.shape[0]
    depth = 1.0 / (right_ref.shape[1] * 3 // 4)

    wacc[...] = jnp.zeros_like(wacc)

    @pl.loop(0, count // 2)
    def _(m):
        a = jnp.concatenate([outer_ref[2 * m], outer_ref[2 * m + 1]], 1)
        b = jnp.concatenate([pgradt_ref[2 * m], pgradt_ref[2 * m + 1]], 1)
        wacc[...] += nt(a, b)

    for q in range(half):
        wout_ref[pl.ds(q, half, stride=half), :] = wacc[q * half : (q + 1) * half, :]

    @pl.loop(0, count, unroll=2)
    def _(i):
        put(stage, i, nn(w_ref[...], pgradt_ref[i]).astype(BF))

    contract(stage, right_ref, grad_ref)
    grad_ref[...] = grad_ref[...] * depth
    cacc[...] = jnp.zeros_like(cacc)

    @pl.loop(0, count)
    def _(i):
        g = grad_ref[pl.ds(pl.multiple_of(i * half, half), half), :].astype(BF)
        cacc[...] += nt(hat_ref[i].astype(BF), pad_rows(g, 128))

    cross_ref[...] = squeeze(cacc[...])


def column_kernel(
    pcol_ref, left_ref, w_ref, gleft_ref, hat_ref, inv_ref, mgain_ref, wmap_ref,
    out_ref, cross_ref, prow, stage, gright, cacc,
):
    devices, many, channels = pcol_ref.shape
    half = left_ref.shape[0]
    count = gleft_ref.shape[0] // half
    length = devices * count
    pairs = count // 2

    @pl.loop(0, devices)
    def _(d):
        prow[pl.ds(d * (many + 1), many), :] = pcol_ref[d].astype(F32)

    @pl.loop(0, count, unroll=2)
    def _(j):
        p = jnp.concatenate(
            [prow[pl.ds(j * count + i, devices, stride=many + 1), :] for i in range(count)], 0
        )
        put(stage, j, nt(w_ref[...], pad_rows(p, WIDE).astype(BF)).astype(BF))

    contract(stage, left_ref, gright)
    gain = as_column(mgain_ref)
    cacc[...] = jnp.zeros_like(cacc)

    @pl.loop(0, pairs)
    def _(m):
        both = []
        for o in range(2):
            i = 2 * m + o
            hat = hat_ref[i]
            at = pl.ds(pl.multiple_of(i * half, half), half)
            right = (gright[at, :] * (1.0 / length)).astype(BF)
            cacc[...] += nt(hat.astype(BF), pad_rows(right, 128))
            g = jnp.concatenate([gleft_ref[at, :].astype(BF), right], 0)
            both.append(norm_back(nn(wmap_ref[...], g) * gain, hat, inv_ref[i]))
        out_ref[m] = jnp.concatenate(both, 0).T[:length].astype(BF)

    cross_ref[...] = squeeze(cacc[...])


def unsqueeze(v):
    lane = lax.broadcasted_iota(jnp.int32, v.shape, 1)
    got = [v if k == 0 else pltpu.roll(v, 128 - 32 * k, 1) for k in range(4)]
    return jnp.concatenate([jnp.where(lane < 32, g, 0.0) for g in got], 0)


def finish_kernel(
    factor, all_ref, gain_ref, wmap_ref,
    mgain_out, proj_out, wout_out, bias_out, pgain_out, win_out, wgg_out, cgain_out, wfg_out,
    rows, flat,
):
    everyone, each, _ = all_ref.shape
    own = each - 16
    eight = 8

    @pl.loop(0, everyone)
    def _(d):
        rows[pl.ds(pl.multiple_of(d * own, 16), own), :] = all_ref[d, :own].astype(F32) * factor

    many = wout_out.shape[0]
    wout_out[...] = rows[:many, :]
    at = many
    channels = wgg_out.shape[0]
    devices = channels // eight
    for k in range(4):
        lr, gv = k // 2, k % 2
        for d in range(devices):
            start = at + gv * 2 * channels + d * 2 * eight + lr * eight
            flat[d * eight : (d + 1) * eight, :] = rows[start : start + eight, :]
        win_out[:, k * channels : (k + 1) * channels] = flat[...].T
    at += 4 * channels
    wgg_out[...] = rows[at : at + channels, :]
    at += channels
    wfg_out[...] = rows[at : at + channels, :]
    at += channels
    left = unsqueeze(rows[at : at + 16, :])
    at += 16
    cgain_out[...] = rows[at : at + 1, :]
    pgain_out[...] = rows[at + 1 : at + 2, :]
    bias_out[...] = rows[at + 2 : at + 3, :]
    right = unsqueeze(jnp.sum(all_ref[:, own:].astype(F32), 0) * factor)
    width = proj_out.shape[0]
    cross = (left + pltpu.roll(right, 32, 1))[:, :width]
    proj_out[...] = cross * as_column(gain_ref)
    mgain_out[...] = as_row(jnp.sum(cross * wmap_ref[...].astype(F32), 1, keepdims=True))


def exchange(v, axes="dap", groups=None):
    return lax.all_to_all(
        v, axes, split_axis=0, concat_axis=0, tiled=True, axis_index_groups=groups
    )


def local(
    homolog_features,
    edge_features,
    adjoint_edges,
    homolog_scaling_factor,
    tensor_mapping_matrix,
    tensor_final_matrix,
    tensor_final_offset,
    edge_scaling_factor,
    trilateral_entry_matrix,
    final_sigmoid_matrix,
    central_scaling_factor,
    trilateral_final_matrix,
):
    n = lax.axis_size("dap")
    everyone = n * lax.axis_size("dp")
    msa = homolog_features[0]
    depth, count, width = msa.shape
    length = edge_features.shape[2]
    pairs = count // 2
    half = tensor_mapping_matrix.shape[1] // 2
    channels = edge_features.shape[3]
    eight = channels // n
    edges = edge_features[0]
    adjoint = adjoint_edges[0]
    line = lambda v: v.reshape(1, -1)
    msa_gain = line(homolog_scaling_factor)

    x = msa.reshape(depth, pairs, 2 * width).transpose(1, 0, 2)
    left, left_send, right_send = call(
        project_kernel,
        [((count, half, WIDE), BF), ((pairs, 3, half, 128), BF), ((pairs, 3, half, 128), BF)],
        [],
        x, msa_gain, tensor_mapping_matrix,
    )
    chips = n // 2
    groups = [list(range(0, n, 2)), list(range(1, n, 2))]

    def everywhere(v):
        own = exchange(jnp.broadcast_to(v, (chips,) + v.shape), groups=groups)
        return own, lax.ppermute(own, "dap", [(i, i ^ 1) for i in range(n)])

    own, other = everywhere(right_send)
    left_send, other = lax.optimization_barrier((left_send, other))
    left_own, left_other = everywhere(left_send)
    parity = lax.rem(lax.axis_index("dap"), 2).astype(jnp.int32).reshape(1)

    qp = tensor_final_matrix.reshape(half, half, channels).transpose(1, 0, 2)
    qp = qp.reshape(half * half, channels)
    entry = trilateral_entry_matrix.reshape(channels, 2, 2, n, eight).transpose(0, 2, 3, 1, 4)
    entry = entry.reshape(channels, 4 * channels)
    wide = ((count, channels, WIDE), BF)
    wide32 = ((count, channels, WIDE), F32)
    every = ((half, WIDE, WIDE), BF)
    outers = ((count, half * half, WIDE), BF)
    spare = [((length * (half + 1), 128), F32)] * 2
    edge_send, mid, normed, right, outer = call(
        outer_kernel,
        [((n, pairs, 3, 2 * eight, 128), BF), wide32, wide, every, outers],
        spare + [every, outers],
        parity, own, other, left, edges, qp.T, line(tensor_final_offset),
        line(edge_scaling_factor), entry.T, smem=1, away=2, copies=2,
    )
    edge_cols = exchange(edge_send)
    gate, up = call(gate_kernel, [wide32, wide], [], normed, adjoint, final_sigmoid_matrix)
    rooms = [((length * (2 * eight + 1), 128), F32)] * 2
    rooms += [((length * (eight + 1), 128), F32)] * 2
    mixed_send, left_cols, right_cols = call(
        triangle_kernel,
        [((n, pairs // 2, 3, 2 * eight, 128), BF)] + [((eight, length, WIDE), BF)] * 2,
        rooms,
        edge_cols,
    )
    mixed = exchange(mixed_send)
    square = ((channels, channels), F32)
    row = ((1, channels), F32)
    (grad_send,) = call(
        update_kernel,
        [((n, pairs // 2, 3, 2 * eight, 128), BF)],
        [],
        mixed, gate, up, line(central_scaling_factor), trilateral_final_matrix,
    )
    grad_cols = exchange(grad_send)
    pair_out, grad_gate, tri_out, tri_gate, mid_gain = call(
        result_kernel,
        [(edges.shape, BF), wide, square, square, row],
        [((channels, WIDE), F32)],
        mixed, mid, normed, gate, up, line(central_scaling_factor), trilateral_final_matrix,
    )
    (back_send,) = call(
        triangle_back_kernel,
        [((n, pairs, 3, 2 * eight, 128), BF)],
        rooms,
        grad_cols, left_cols, right_cols,
    )
    back = exchange(back_send)
    left_own, left_other, back_send = lax.optimization_barrier((left_own, left_other, back_send))
    lefts, hat, inverse = call(
        prepare_kernel,
        [every, ((count, width, WIDE), F32), ((count, 1, WIDE), F32)],
        spare,
        parity, left_own, left_other, x, smem=1,
    )
    pgrad, pgradt, pgrad_send, tri_in, tri_gain, bias = call(
        edge_back_kernel,
        [
            (edges.shape, BF), wide, ((length * count, channels), BF),
            ((4 * channels, channels), F32), row, row,
        ],
        [((channels, WIDE), F32)] * 2 + [((length * count, channels), F32)],
        back, mid, normed, grad_gate, up, line(edge_scaling_factor),
        entry.T, entry, final_sigmoid_matrix,
    )
    pgrad_cols = exchange(pgrad_send.reshape(n, count * count, channels))
    group = 4
    stage = ((half // group, count * half, group * WIDE), BF)
    grads = ((count * half, WIDE), F32)
    cross = ((width // 4, 128), F32)
    full = ((half * half, channels), F32)
    grad_left, opm_out, cross_left = call(
        outer_back_kernel,
        [grads, full, cross],
        [stage, full, ((width, 128), F32)],
        pgradt, right, outer, qp, hat,
    )
    parts = [opm_out, tri_in, tri_gate, tri_out, cross_left, mid_gain, tri_gain, bias]
    used = sum(p.shape[0] for p in parts)
    each = -(-used // (16 * everyone)) * 16
    parts.append(jnp.zeros((each * everyone - used, 128), F32))
    mine = exchange(
        jnp.concatenate(parts, 0).astype(BF).reshape(everyone, each, 128), ("dp", "dap")
    )
    sens, cross_right = call(
        column_kernel,
        [((pairs, length, 2 * width), BF), cross],
        [((devices_rows(n, count), channels), F32), stage, grads, ((width, 128), F32)],
        pgrad_cols, lefts, tensor_final_matrix, grad_left, hat, inverse,
        msa_gain, tensor_mapping_matrix,
    )
    sensitivity = sens.transpose(1, 0, 2).reshape(depth, count, width)
    mine = jnp.sum(mine.astype(F32), 0)
    mine = jnp.concatenate([mine, cross_right], 0).astype(BF)
    total = exchange(jnp.broadcast_to(mine, (everyone, each + 16, 128)), ("dp", "dap"))
    factor = 1.0 / (lax.axis_size("dp") * length)
    last = call(
        lambda *refs: finish_kernel(factor, *refs),
        [
            ((1, width), F32), ((width, 2 * half), F32), full, row, row,
            ((channels, 4 * channels), F32), square, row, square,
        ],
        [((everyone * each, 128), F32), ((channels, 128), F32)],
        total, msa_gain, tensor_mapping_matrix,
    )
    last = [v.reshape(-1) if v.shape[0] == 1 else v for v in last]
    return (pair_out[None], pgrad[None], sensitivity[None], *last)


def devices_rows(devices, count):
    return devices * (count * count + 1)


def solution(mesh):
    placed = (
        P("dp", None, "dap", None),
        P("dp", "dap", None, None),
        P("dp", "dap", None, None),
    ) + (P(),) * 9
    return jax.shard_map(
        local,
        mesh=mesh,
        in_specs=placed,
        out_specs=(
            P("dp", "dap", None, None),
            P("dp", "dap", None, None),
            P("dp", None, "dap", None),
        )
        + (P(),) * 9,
        check_vma=False,
    )
```

time: 259 us -> 253 us (0.977)
  waiting for transfers between devices: 43.7 us -> 61.1 us
  between operations: 14.4 us -> 1.1 us
  Pallas kernels: 84.4 us -> 74.6 us
  starting transfers between devices: 16.3 us -> 21.4 us
  local copies, waits for them, and re-layouts: 16.1 us -> 12.2 us
    all_to_all x4 -> x5, waiting for transfers between devices: 41.3 us -> 58.6 us  [exchange(): lax.all_to_all(v, axes, split_axis=0, concat_axis=0, tiled=True, axis_ind...]
    pallas_call x8 -> x12, Pallas kernels: 84.4 us -> 74.6 us  [call(): pl.pallas_call(kernel, out_shape=[jax.ShapeDtypeStruct(s, t) for s, t in...]
    all_to_all x4 -> x5, starting transfers between devices: 16.3 us -> 21 us  [exchange(): lax.all_to_all(v, axes, split_axis=0, concat_axis=0, tiled=True, axis_ind...]
    unnamed x41 -> x59, local copies, waits for them, and re-layouts: 7.19 us -> 6.44 us
  transfers between devices with their start and end apart: 6 -> 7, of which waited for: 4 -> 6; matrix products, arithmetic and copies ran while one was open for 1% -> 1% of each run, Pallas kernels for 24% -> 8%
where the time goes in v2:
time: 253 us; the launch traced here: 251 us
  blocking collectives  80 us (32%)
  Pallas kernels  74.6 us (29%)
  waiting for transfers between devices  61.1 us (24%)
  starting transfers between devices  21.4 us (8%)
  local copies, waits for them, and re-layouts  12.2 us (5%)
    all_to_all x4, blocking collectives, exchange(): lax.all_to_all(v, axes, split_axis=0, concat_axis=0, tiled=True, axis_ind...  80 us
    pallas_call x12, Pallas kernels, call(): pl.pallas_call(kernel, out_shape=[jax.ShapeDtypeStruct(s, t) for s, t in...  74.6 us
    all_to_all x5, waiting for transfers between devices, exchange(): lax.all_to_all(v, axes, split_axis=0, concat_axis=0, tiled=True, axis_ind...  58.6 us
    all_to_all x5, starting transfers between devices, exchange(): lax.all_to_all(v, axes, split_axis=0, concat_axis=0, tiled=True, axis_ind...  21 us
    unnamed x59, local copies, waits for them, and re-layouts  6.44 us
  transfers between devices with their start and end apart: 7, of which 6 were waited for; matrix products, arithmetic and copies ran while one was open for 1% of the time, Pallas kernels for 8%

profile of v2, /device:TPU:0, one launch (start us, length us, event | category | flops | bytes accessed | tf_op | source)
XLA Modules:
  0.0 250.7 jit_solution(1035464386900170938)
XLA Ops:
  0.6 1.2 copy.29
  1.9 0.0 copy-start.17
  1.9 0.7 copy-done.17
  2.6 0.7 copy-done.22
  3.2 2.2 shard_map.211
  5.4 0.2 broadcast_in_dim.18
  5.6 0.0 copy-start.9
  5.6 0.0 copy-start.28
  5.6 22.6 %all_to_all.45.own_ref = bf16[8,6,3,32,128]{4,3,2,1,0:T(8,128)(2,1)S(1)} all-to-all(bf16[8,6,3,32,128]{4,3,2,1,0:T(8,128)(2,1)S(1)} %broadcast_in_dim.18), channel_id=1, replica_groups={{0,2,4,6,8,10,12,14},{1,3,5,7,9,11,13,15},{16,18,20,22,24,26,28,30},{17..., dimensions={0} | all-to-all | bytes 2359296 | tf_op jit(solution)/shard_map/all_to_all | solution.py:540
  28.3 0.1 collective-permute-start
  28.4 0.1 copy.30
  28.5 0.0 copy-start.4
  28.5 0.1 copy.33.wt_ref
  28.7 0.1 copy.31
  28.8 0.0 copy-start.7
  28.8 2.5 collective-permute-done.other_ref
  31.4 14.5 %shard_map.212 = (bf16[16,6,3,16,128]{4,3,2,1,0:T(8,128)(2,1)S(1)}, f32[12,128,256]{2,1,0:T(8,128)}, bf16[12,128,256]{2,1,0:T(8,128)(2,1)S(1)}, bf16[32,256,256]{2,1,0:T(8,128)(2,1)}, bf16[12,1024,256]{2,1,0:T(8,128)(2,1)}) custom-call(s32[1]{0:T(128)} %bitcast.par_ref, bf16[8,6,3,32,128]{4,3,2,1,0:T(8,128)(2,1)} %copy-done.27, ...), custom_call_target="tpu_custom_call" | custom-call | tf_op jit(solution)/shard_map/pallas_call | solution.py:84
  45.9 20.5 %all_to_all.46.edges_ref = bf16[16,6,3,16,128]{4,3,2,1,0:T(8,128)(2,1)S(1)} all-to-all(bf16[16,6,3,16,128]{4,3,2,1,0:T(8,128)(2,1)S(1)} %get-tuple-element.61), channel_id=1, replica_groups=mesh['dp'=8,'dap'=16] {'dap'}, dimensions={0} | all-to-all | bytes 2359296 | tf_op jit(solution)/shard_map/all_to_all | solution.py:540
  66.4 3.1 %shard_map.213 = (bf16[16,3,3,16,128]{4,3,2,1,0:T(8,128)(2,1)S(1)}, bf16[8,192,256]{2,1,0:T(8,128)(2,1)S(1)}, bf16[8,192,256]{2,1,0:T(8,128)(2,1)S(1)}) custom-call(bf16[16,6,3,16,128]{4,3,2,1,0:T(8,128)(2,1)S(1)} %all_to_all.46.edges_ref), custom_call_target="tpu_custom_call" | custom-call | tf_op jit(solution)/shard_map/pallas_call | solution.py:84
  69.5 0.9 copy-done.11
  70.4 0.9 copy-done.13
  71.3 14.8 %all_to_all.47.mixed_ref = bf16[16,3,3,16,128]{4,3,2,1,0:T(8,128)(2,1)} all-to-all(bf16[16,3,3,16,128]{4,3,2,1,0:T(8,128)(2,1)S(1)} %get-tuple-element.62), channel_id=1, replica_groups=mesh['dp'=8,'dap'=16] {'dap'}, dimensions={0} | all-to-all | bytes 1179648 | tf_op jit(solution)/shard_map/all_to_all | solution.py:540
  86.1 1.3 broadcast_in_dim.21
  87.4 4.4 %all-to-all-start.6 = ((bf16[8,6,3,32,128]{4,3,2,1,0:T(8,128)(2,1)}), bf16[8,6,3,32,128]{4,3,2,1,0:T(8,128)(2,1)}, u32[]{:S(2)}, u32[]{:S(2)}) async-start(bf16[8,6,3,32,128]{4,3,2,1,0:T(8,128)(2,1)} %broadcast_in_dim.21), calls=%async_computation.6 | async-start | bytes 2359296 | tf_op jit(solution)/shard_map/all_to_all | solution.py:540
  91.8 0.0 copy-start.16
  91.8 1.1 copy-done.16
  93.0 2.7 %shard_map.214 = (f32[12,128,256]{2,1,0:T(8,128)S(1)}, bf16[12,128,256]{2,1,0:T(8,128)(2,1)S(1)}) custom-call(bf16[12,128,256]{2,1,0:T(8,128)(2,1)S(1)} %get-tuple-element.64.normed_ref, bf16[12,192,128]{2,1,0:T(8,128)(2,1)S(1)} %bitcast.40, bf16[128,128]{1,0:T(8,128)(2,1)S(1)} %copy-done.20), custom_call_target="tpu_custom_call" | custom-call | tf_op jit(solution)/shard_map/pallas_call | solution.py:84
  95.7 0.0 copy-start.1
  95.7 0.0 copy-start
  95.7 0.0 copy-done.19
  95.7 0.0 copy-done.25
  95.7 0.0 copy-done.2
  95.7 1.5 shard_map.216
  97.2 0.0 copy-start.6
  97.3 0.8 copy-done.6
  98.1 12.9 %all-to-all-done.6.own_ref = bf16[8,6,3,32,128]{4,3,2,1,0:T(8,128)(2,1)} async-done(((bf16[8,6,3,32,128]{4,3,2,1,0:T(8,128)(2,1)}), bf16[8,6,3,32,128]{4,3,2,1,0:T(8,128)(2,1)}, u32[]{:S(2)}, u32[]{:S(2)}) %all-to-all-start.6) | async-done | bytes 1179680 | tf_op jit(solution)/shard_map/all_to_all | solution.py:540
  110.9 3.7 %all-to-all-start.3 = ((bf16[16,3,3,16,128]{4,3,2,1,0:T(8,128)(2,1)}), bf16[16,3,3,16,128]{4,3,2,1,0:T(8,128)(2,1)S(1)}, u32[]{:S(2)}, u32[]{:S(2)}) async-start(bf16[16,3,3,16,128]{4,3,2,1,0:T(8,128)(2,1)} %copy-done.6), calls=%async_computation.3 | async-start | bytes 1179648 | tf_op jit(solution)/shard_map/all_to_all | solution.py:540
  114.6 0.3 collective-permute-start.1
  114.9 11.2 %all-to-all-done.3.grads_ref = bf16[16,3,3,16,128]{4,3,2,1,0:T(8,128)(2,1)S(1)} async-done(((bf16[16,3,3,16,128]{4,3,2,1,0:T(8,128)(2,1)}), bf16[16,3,3,16,128]{4,3,2,1,0:T(8,128)(2,1)S(1)}, u32[]{:S(2)}, u32[]{:S(2)}) %all-to-all-start.3) | async-done | bytes 589856 | tf_op jit(solution)/shard_map/all_to_all | solution.py:540
  126.2 1.1 copy-done.14
  127.3 4.1 %shard_map.217 = bf16[16,6,3,16,128]{4,3,2,1,0:T(8,128)(2,1)} custom-call(bf16[16,3,3,16,128]{4,3,2,1,0:T(8,128)(2,1)S(1)} %all-to-all-done.3.grads_ref, bf16[8,192,256]{2,1,0:T(8,128)(2,1)S(1)} %copy-done.12, bf16[8,192,256]{2,1,0:T(8,128)(2,1)S(1)} %copy-done.14), custom_call_target="tpu_custom_call" | custom-call | tf_op jit(solution)/shard_map/pallas_call | solution.py:84
  131.5 4.5 %all-to-all-start.4 = ((bf16[16,6,3,16,128]{4,3,2,1,0:T(8,128)(2,1)}), bf16[16,6,3,16,128]{4,3,2,1,0:T(8,128)(2,1)}, u32[]{:S(2)}, u32[]{:S(2)}) async-start(bf16[16,6,3,16,128]{4,3,2,1,0:T(8,128)(2,1)} %shard_map.217), calls=%async_computation.4 | async-start | bytes 2359296 | tf_op jit(solution)/shard_map/all_to_all | solution.py:540
  136.0 0.1 copy.34.entry_ref
  136.1 5.8 %shard_map.215 = (bf16[12,192,128]{2,1,0:T(8,128)(2,1)}, bf16[12,128,256]{2,1,0:T(8,128)(2,1)S(1)}, f32[128,128]{1,0:T(8,128)S(1)}, f32[128,128]{1,0:T(8,128)S(1)}, f32[1,128]{1,0:T(1,128)S(1)}) custom-call(bf16[16,3,3,16,128]{4,3,2,1,0:T(8,128)(2,1)S(1)} %copy-done.3, f32[12,128,256]{2,1,0:T(8,128)} %get-tuple-element.63.mid_ref, ...), custom_call_target="tpu_custom_call" | custom-call | tf_op jit(solution)/shard_map/pallas_call | solution.py:84
  142.0 0.0 copy-start.21
  142.0 0.0 collective-permute-done.1.other_ref
  142.0 6.3 %shard_map.219 = (bf16[32,256,256]{2,1,0:T(8,128)(2,1)}, f32[12,64,256]{2,1,0:T(8,128)S(1)}, f32[12,1,256]{2,1,0:T(1,128)S(1)}) custom-call(s32[1]{0:T(128)} %bitcast.par_ref, bf16[8,6,3,32,128]{4,3,2,1,0:T(8,128)(2,1)} %all-to-all-done.6.own_ref, bf16[8,6,3,32,128]{4,3,2,1,0:T(8,128)(2,1)} %collective-permute-done.1.other_ref, bf16[6,192,128]{2,1,0:T(8,128)(2,1)S(1)} %bitcast.32), custom_call_target="tpu_custom_call" | custom-call | tf_op jit(solution)/shard_map/pallas_call | solution.py:84
  148.3 5.6 %all-to-all-done.4.grads_ref = bf16[16,6,3,16,128]{4,3,2,1,0:T(8,128)(2,1)} async-done(((bf16[16,6,3,16,128]{4,3,2,1,0:T(8,128)(2,1)}), bf16[16,6,3,16,128]{4,3,2,1,0:T(8,128)(2,1)}, u32[]{:S(2)}, u32[]{:S(2)}) %all-to-all-start.4) | async-done | bytes 1179680 | tf_op jit(solution)/shard_map/all_to_all | solution.py:540
  153.9 8.9 %shard_map.218 = (bf16[12,192,128]{2,1,0:T(8,128)(2,1)}, bf16[12,128,256]{2,1,0:T(8,128)(2,1)S(1)}, bf16[2304,128]{1,0:T(8,128)(2,1)}, f32[512,128]{1,0:T(8,128)...) custom-call(bf16[16,6,3,16,128]{4,3,2,1,0:T(8,128)(2,1)} %all-to-all-done.4.grads_ref, ...), custom_call_target="tpu_custom_call" | custom-call | tf_op jit(solution)/shard_map/pallas_call | solution.py:84
  162.8 14.0 %shard_map.220 = (f32[384,256]{1,0:T(8,128)S(1)}, f32[1024,128]{1,0:T(8,128)S(1)}, f32[16,128]{1,0:T(8,128)S(1)}) custom-call(bf16[12,128,256]{2,1,0:T(8,128)(2,1)S(1)} %get-tuple-element.77.pgradt_ref, bf16[32,256,256]{2,1,0:T(8,128)(2,1)} %get-tuple-element.78.right_ref, bf16[12,1024,256]{2,1,0:T(8,128)(2,1)} %get-tuple-element.79.outer_ref, ...), custom_call_target="tpu_custom_call" | custom-call | tf_op jit(solution)/shard_map/pallas_call | solution.py:84
  177.0 0.6 concatenate.8
  177.6 0.0 copy-start.10
  177.6 0.0 copy-start.18
  177.6 0.0 copy-start.23
  177.6 22.1 %all_to_all.48 = bf16[128,16,128]{2,1,0:T(8,128)(2,1)S(1)} all-to-all(bf16[128,16,128]{2,1,0:T(8,128)(2,1)S(1)} %bitcast.50), channel_id=1, replica_groups=mesh['dp'=8,'dap'=16] {'dp','dap'}, dimensions={0} | all-to-all | bytes 1048576 | tf_op jit(solution)/shard_map/all_to_all | solution.py:540
  199.6 3.8 %all-to-all-start.5 = ((bf16[16,144,128]{2,1,0:T(8,128)(2,1)}), bf16[16,144,128]{2,1,0:T(8,128)(2,1)S(1)}, u32[]{:S(2)}, u32[]{:S(2)}) async-start(bf16[16,144,128]{2,1,0:T(8,128)(2,1)} %bitcast.20), calls=%async_computation.5 | async-start | bytes 1179648 | tf_op jit(solution)/shard_map/all_to_all | solution.py:540
  203.4 0.1 reduce
  203.6 11.2 %all-to-all-done.5.pcol_ref = bf16[16,144,128]{2,1,0:T(8,128)(2,1)S(1)} async-done(((bf16[16,144,128]{2,1,0:T(8,128)(2,1)}), bf16[16,144,128]{2,1,0:T(8,128)(2,1)S(1)}, u32[]{:S(2)}, u32[]{:S(2)}) %all-to-all-start.5) | async-done | bytes 589856 | tf_op jit(solution)/shard_map/all_to_all | solution.py:540
  214.8 9.3 %shard_map.221 = (bf16[6,192,128]{2,1,0:T(8,128)(2,1)S(1)}, f32[16,128]{1,0:T(8,128)S(1)}) custom-call(bf16[16,144,128]{2,1,0:T(8,128)(2,1)S(1)} %all-to-all-done.5.pcol_ref, bf16[32,256,256]{2,1,0:T(8,128)(2,1)} %get-tuple-element.76.left_ref, bf16[1024,128]{1,0:T(8,128)(2,1)S(1)} %copy-done.10, f32[384,256]{1,0:T(8,128)S(1)} %get-tuple-element.81.gleft_ref, ...), custom_call_target="tpu_custom_call" | custom-call | tf_op jit(solution)/shard_map/pallas_call | solution.py:84
  224.1 1.1 broadcast_in_dim.23
  225.3 4.6 %all-to-all-start.8 = ((bf16[128,32,128]{2,1,0:T(8,128)(2,1)}), bf16[128,32,128]{2,1,0:T(8,128)(2,1)S(1)}, u32[]{:S(2)}, u32[]{:S(2)}) async-start(bf16[128,32,128]{2,1,0:T(8,128)(2,1)} %broadcast_in_dim.23), calls=%async_computation.8 | async-start | bytes 2097152 | tf_op jit(solution)/shard_map/all_to_all | solution.py:540
  229.9 0.9 copy.35
  230.8 17.7 %all-to-all-done.8.refs_0_ = bf16[128,32,128]{2,1,0:T(8,128)(2,1)S(1)} async-done(((bf16[128,32,128]{2,1,0:T(8,128)(2,1)}), bf16[128,32,128]{2,1,0:T(8,128)(2,1)S(1)}, u32[]{:S(2)}, u32[]{:S(2)}) %all-to-all-start.8) | async-done | bytes 1048608 | tf_op jit(solution)/shard_map/all_to_all | solution.py:540
  248.6 2.1 shard_map.222
  (47 shorter events, 0.2 us)
Async XLA Ops:
  1.9 0.7 copy-start.17
  2.6 0.7 copy-start.22
  5.6 22.8 %copy-start.9 = (bf16[1024,128]{1,0:T(8,128)(2,1)S(1)}, bf16[1024,128]{1,0:T(8,128)(2,1)}, u32[]{:S(2)}) copy-start(bf16[1024,128]{1,0:T(8,128)(2,1)} %w_ref.3) | copy-start | bytes 786436
  5.6 23.1 %copy-start.28 = (bf16[128,512]{1,0:T(8,128)(2,1)S(1)}, bf16[128,512]{1,0:T(8,128)(2,1)}, u32[]{:S(2)}) copy-start(bf16[128,512]{1,0:T(8,128)(2,1)} %param.20) | copy-start | bytes 393220
  28.3 3.1 %copy-start.27 = (bf16[8,6,3,32,128]{4,3,2,1,0:T(8,128)(2,1)}, bf16[8,6,3,32,128]{4,3,2,1,0:T(8,128)(2,1)S(1)}, u32[]{:S(2)}) copy-start(bf16[8,6,3,32,128]{4,3,2,1,0:T(8,128)(2,1)S(1)} %all_to_all.45.own_ref) | copy-start | bytes 3538948
  28.3 3.1 %copy-start.15 = (bf16[1,12,192,128]{3,2,1,0:T(8,128)(2,1)S(1)}, bf16[1,12,192,128]{3,2,1,0:T(8,128)(2,1)}, u32[]{:S(2)}) copy-start(bf16[1,12,192,128]{3,2,1,0:T(8,128)(2,1)} %param.13) | copy-start | bytes 1769476
  28.3 3.1 %copy-start.24 = (f32[128]{0:T(128)S(1)}, f32[128]{0:T(128)}, u32[]{:S(2)}) copy-start(f32[128]{0:T(128)} %param.19) | copy-start | bytes 1540
  28.3 3.1 %copy-start.26 = (f32[128]{0:T(128)S(1)}, f32[128]{0:T(128)}, u32[]{:S(2)}) copy-start(f32[128]{0:T(128)} %param.18) | copy-start | bytes 1540
  28.3 3.1 %collective-permute-start = (bf16[8,6,3,32,128]{4,3,2,1,0:T(8,128)(2,1)S(1)}, bf16[8,6,3,32,128]{4,3,2,1,0:T(8,128)(2,1)}, u32[]{:S(2)}, u32[]{:S(2)}) collective-permute-start(bf16[8,6,3,32,128]{4,3,2,1,0:T(8,128)(2,1)S(1)} %all_to_all.45.own_ref), channel_id=1, source_target_pairs={{0,1},{1,0},{2,3},{3,2},{4,5},{5,4},{6,7},{7,6},{8,9},{9,8},{10,11... | collective-permute-start | bytes 3538952 | tf_op jit(solution)/shard_map/ppermute | solution.py:585
  28.5 2.8 %copy-start.4 = (bf16[32,32,128]{2,0,1:T(8,128)(2,1)}, bf16[32,32,128]{2,0,1:T(8,128)(2,1)S(1)}, u32[]{:S(2)}) copy-start(bf16[32,32,128]{2,0,1:T(8,128)(2,1)S(1)} %copy.30) | copy-start | bytes 786436
  28.8 17.1 %copy-start.7 = (bf16[128,2,16,2,8]{0,4,3,2,1:T(8,128)(2,1)}, bf16[128,2,16,2,8]{0,4,3,2,1:T(8,128)(2,1)S(1)}, u32[]{:S(2)}) copy-start(bf16[128,2,16,2,8]{0,4,3,2,1:T(8,128)(2,1)S(1)} %copy.32) | copy-start | bytes 393220
  69.5 0.9 copy-start.11
  70.4 0.9 copy-start.13
  87.4 4.4 %copy-start.20 = (bf16[128,128]{1,0:T(8,128)(2,1)S(1)}, bf16[128,128]{1,0:T(8,128)(2,1)}, u32[]{:S(2)}) copy-start(bf16[128,128]{1,0:T(8,128)(2,1)} %wg_ref.3) | copy-start | bytes 98308
  87.4 8.3 %copy-start.19 = (bf16[128,128]{1,0:T(8,128)(2,1)S(1)}, bf16[128,128]{1,0:T(8,128)(2,1)}, u32[]{:S(2)}) copy-start(bf16[128,128]{1,0:T(8,128)(2,1)} %wf_ref.3) | copy-start | bytes 98308
  87.4 8.3 %copy-start.25 = (f32[128]{0:T(128)S(1)}, f32[128]{0:T(128)}, u32[]{:S(2)}) copy-start(f32[128]{0:T(128)} %param.22) | copy-start | bytes 1540
  87.4 23.5 %all-to-all-start.6 = ((bf16[8,6,3,32,128]{4,3,2,1,0:T(8,128)(2,1)}), bf16[8,6,3,32,128]{4,3,2,1,0:T(8,128)(2,1)}, u32[]{:S(2)}, u32[]{:S(2)}) async-start(bf16[8,6,3,32,128]{4,3,2,1,0:T(8,128)(2,1)} %broadcast_in_dim.21), calls=%async_computation.6 | async-start | bytes 2359296 | tf_op jit(solution)/shard_map/all_to_all | solution.py:540
  91.8 3.9 %copy-start.2 = (bf16[16,3,3,16,128]{4,3,2,1,0:T(8,128)(2,1)S(1)}, bf16[16,3,3,16,128]{4,3,2,1,0:T(8,128)(2,1)}, u32[]{:S(2)}) copy-start(bf16[16,3,3,16,128]{4,3,2,1,0:T(8,128)(2,1)} %all_to_all.47.mixed_ref) | copy-start | bytes 1769476
  91.8 1.1 copy-start.16
  95.7 1.6 copy-start.1
  95.7 40.4 %copy-start = (bf16[12,128,256]{2,1,0:T(8,128)(2,1)}, bf16[12,128,256]{2,1,0:T(8,128)(2,1)S(1)}, u32[]{:S(2)}) copy-start(bf16[12,128,256]{2,1,0:T(8,128)(2,1)S(1)} %get-tuple-element.66.up_ref) | copy-start | bytes 2359300
  97.2 0.8 copy-start.6
  110.9 15.3 %copy-start.12 = (bf16[8,192,256]{2,1,0:T(8,128)(2,1)S(1)}, bf16[8,192,256]{2,1,0:T(8,128)(2,1)}, u32[]{:S(2)}) copy-start(bf16[8,192,256]{2,1,0:T(8,128)(2,1)} %copy-done.11) | copy-start | bytes 2359300
  110.9 15.2 %all-to-all-start.3 = ((bf16[16,3,3,16,128]{4,3,2,1,0:T(8,128)(2,1)}), bf16[16,3,3,16,128]{4,3,2,1,0:T(8,128)(2,1)S(1)}, u32[]{:S(2)}, u32[]{:S(2)}) async-start(bf16[16,3,3,16,128]{4,3,2,1,0:T(8,128)(2,1)} %copy-done.6), calls=%async_computation.3 | async-start | bytes 1179648 | tf_op jit(solution)/shard_map/all_to_all | solution.py:540
  114.6 27.3 %collective-permute-start.1 = (bf16[8,6,3,32,128]{4,3,2,1,0:T(8,128)(2,1)}, bf16[8,6,3,32,128]{4,3,2,1,0:T(8,128)(2,1)}, u32[]{:S(2)}, u32[]{:S(2)}) collective-permute-start(bf16[8,6,3,32,128]{4,3,2,1,0:T(8,128)(2,1)} %all-to-all-done.6.own_ref), channel_id=1, source_target_pairs={{0,1},{1,0},{2,3},{3,2},{4,5},{5,4},{6,7},{7,6},{8,9},{9,8},{10,11... | collective-permute-start | bytes 3538952 | tf_op jit(solution)/shard_map/ppermute | solution.py:585
  126.2 1.1 copy-start.14
  131.4 4.5 %copy-start.8 = (bf16[128,2,16,2,8]{0,4,3,2,1:T(8,128)(2,1)S(1)}, bf16[128,2,16,2,8]{0,4,3,2,1:T(8,128)(2,1)}, u32[]{:S(2)}) copy-start(bf16[128,2,16,2,8]{0,4,3,2,1:T(8,128)(2,1)} %copy-done.7) | copy-start | bytes 393220
  131.5 4.7 %copy-start.3 = (bf16[16,3,3,16,128]{4,3,2,1,0:T(8,128)(2,1)S(1)}, bf16[16,3,3,16,128]{4,3,2,1,0:T(8,128)(2,1)}, u32[]{:S(2)}) copy-start(bf16[16,3,3,16,128]{4,3,2,1,0:T(8,128)(2,1)} %all_to_all.47.mixed_ref) | copy-start | bytes 1769476
  131.5 22.4 %all-to-all-start.4 = ((bf16[16,6,3,16,128]{4,3,2,1,0:T(8,128)(2,1)}), bf16[16,6,3,16,128]{4,3,2,1,0:T(8,128)(2,1)}, u32[]{:S(2)}, u32[]{:S(2)}) async-start(bf16[16,6,3,16,128]{4,3,2,1,0:T(8,128)(2,1)} %shard_map.217), calls=%async_computation.4 | async-start | bytes 2359296 | tf_op jit(solution)/shard_map/all_to_all | solution.py:540
  142.0 11.9 %copy-start.21 = (bf16[128,128]{1,0:T(8,128)(2,1)S(1)}, bf16[128,128]{1,0:T(8,128)(2,1)}, u32[]{:S(2)}) copy-start(bf16[128,128]{1,0:T(8,128)(2,1)} %wg_ref.3) | copy-start | bytes 98308
  153.9 8.9 %copy-start.5 = (bf16[32,32,128]{2,0,1:T(8,128)(2,1)S(1)}, bf16[32,32,128]{2,0,1:T(8,128)(2,1)}, u32[]{:S(2)}) copy-start(bf16[32,32,128]{2,0,1:T(8,128)(2,1)} %copy-done.4) | copy-start | bytes 786436
  177.6 37.2 %copy-start.10 = (bf16[1024,128]{1,0:T(8,128)(2,1)S(1)}, bf16[1024,128]{1,0:T(8,128)(2,1)}, u32[]{:S(2)}) copy-start(bf16[1024,128]{1,0:T(8,128)(2,1)} %w_ref.3) | copy-start | bytes 786436
  177.6 37.2 %copy-start.18 = (bf16[64,64]{1,0:T(8,128)(2,1)S(1)}, bf16[64,64]{1,0:T(8,128)(2,1)}, u32[]{:S(2)}) copy-start(bf16[64,64]{1,0:T(8,128)(2,1)} %refs_2_.1) | copy-start | bytes 24580
  177.6 37.2 %copy-start.23 = (f32[64]{0:T(128)S(1)}, f32[64]{0:T(128)}, u32[]{:S(2)}) copy-start(f32[64]{0:T(128)} %param.15) | copy-start | bytes 772
  199.6 15.1 %all-to-all-start.5 = ((bf16[16,144,128]{2,1,0:T(8,128)(2,1)}), bf16[16,144,128]{2,1,0:T(8,128)(2,1)S(1)}, u32[]{:S(2)}, u32[]{:S(2)}) async-start(bf16[16,144,128]{2,1,0:T(8,128)(2,1)} %bitcast.20), calls=%async_computation.5 | async-start | bytes 1179648 | tf_op jit(solution)/shard_map/all_to_all | solution.py:540
  225.3 23.3 %all-to-all-start.8 = ((bf16[128,32,128]{2,1,0:T(8,128)(2,1)}), bf16[128,32,128]{2,1,0:T(8,128)(2,1)S(1)}, u32[]{:S(2)}, u32[]{:S(2)}) async-start(bf16[128,32,128]{2,1,0:T(8,128)(2,1)} %broadcast_in_dim.23), calls=%async_computation.8 | async-start | bytes 2097152 | tf_op jit(solution)/shard_map/all_to_all | solution.py:540

commit v3 on v2

--- a/solution.py
+++ b/solution.py
@@ -75,30 +75,33 @@
     return jnp.sum(jnp.where(a == b, column, 0.0), 0, keepdims=True)
 
 
-def call(kernel, outs, scratch, *operands, smem=0, away=0, copies=0):
+def call(us, kernel, outs, scratch, *operands, smem=0, away=0, sems=None):
     specs = [pl.BlockSpec(memory_space=pltpu.SMEM)] * smem
     specs += [pl.BlockSpec(memory_space=pltpu.VMEM)] * (len(operands) - smem)
     room = [pltpu.VMEM(s, t) for s, t in scratch]
-    if copies:
-        room.append(pltpu.SemaphoreType.DMA((copies,)))
+    if away:
+        room.append(pltpu.SemaphoreType.DMA(sems or (away,)))
     return pl.pallas_call(
         kernel,
         out_shape=[jax.ShapeDtypeStruct(s, t) for s, t in outs],
         in_specs=specs,
         out_specs=[pl.BlockSpec(memory_space=pltpu.VMEM)] * (len(outs) - away)
-        + [pl.BlockSpec(memory_space=pl.ANY)] * away,
+        + [pl.BlockSpec(memory_space=pltpu.HBM)] * away,
         scratch_shapes=room,
         compiler_params=pltpu.CompilerParams(vmem_limit_bytes=50 * 1024 * 1024),
+        cost_estimate=pl.CostEstimate(flops=us * 10**9, bytes_accessed=0, transcendentals=0),
     )(*operands)
 
 
-def project_kernel(x_ref, gain_ref, w_ref, left_ref, lsend_ref, rsend_ref):
+def project_kernel(
+    x_ref, gain_ref, w_ref, left_ref, rsend_out, lsend_out, rsend_ref, lsend_ref, sems
+):
     pairs = x_ref.shape[0]
     width = w_ref.shape[0]
     half = w_ref.shape[1] // 2
     gain = as_column(gain_ref)
 
-    @pl.loop(0, pairs)
+    @pl.loop(0, pairs, unroll=3)
     def _(m):
         x = flip(x_ref[m].astype(F32))
         both = []
@@ -112,6 +115,15 @@
         for t, v in enumerate(pack(both[0][half:], both[1][half:])):
             rsend_ref[m, t] = v.astype(BF)
 
+    copies = []
+    for k in range(rsend_out.shape[0]):
+        copies.append(pltpu.make_async_copy(rsend_ref, rsend_out.at[k], sems.at[0, k]))
+        copies.append(pltpu.make_async_copy(lsend_ref, lsend_out.at[k], sems.at[1, k]))
+    for c in copies:
+        c.start()
+    for c in copies:
+        c.wait()
+
 
 def load_wide(head, tail, start, count, stride):
     a = head[pl.ds(start, count, stride=stride), :]
@@ -172,7 +184,7 @@
     bias = as_column(bias_ref)
     gain = as_column(gain_ref)
 
-    @pl.loop(0, pairs)
+    @pl.loop(0, pairs, unroll=3)
     def _(m):
         both = []
         for o in range(2):
@@ -232,7 +244,9 @@
                 target[d, m, t] = v.astype(BF)
 
 
-def triangle_kernel(edges_ref, send_ref, left_ref, right_ref, head, tail, mhead, mtail):
+def triangle_kernel(
+    edges_ref, send_ref, left_out, right_out, head, tail, mhead, mtail, left_ref, right_ref, sems
+):
     channels, length, _ = left_ref.shape
     spread(edges_ref, 2 * channels, head, tail)
     for c in range(channels):
@@ -242,7 +256,15 @@
         right_ref[c] = b
         mixed = tn(a, b)[:length]
         store_wide(mhead, mtail, c, length, channels + 1, mixed)
+    copies = [
+        pltpu.make_async_copy(left_ref, left_out, sems.at[0]),
+        pltpu.make_async_copy(right_ref, right_out, sems.at[1]),
+    ]
+    for c in copies:
+        c.start()
     gather_up(channels, mhead, mtail, send_ref)
+    for c in copies:
+        c.wait()
 
 
 def triangle_back_kernel(grads_ref, left_ref, right_ref, send_ref, head, tail, mhead, mtail):
@@ -270,7 +292,7 @@
     devices, quads, _, sixteen, _ = mixed_ref.shape
     cgain = as_column(cgain_ref)
 
-    @pl.loop(0, quads)
+    @pl.loop(0, quads, unroll=3)
     def _(n):
         grads = []
         for k, mixed in enumerate(mixed_rows(mixed_ref, n)):
@@ -331,7 +353,7 @@
     bacc[...] = jnp.zeros_like(bacc)
     gain = as_column(gain_ref)
 
-    @pl.loop(0, pairs)
+    @pl.loop(0, pairs, unroll=3)
     def _(m):
         t = [grads_ref[:, m, k].astype(F32).reshape(devices * sixteen, 128) for k in range(3)]
         for o, (a, b) in enumerate(unpack(*t)):
@@ -405,32 +427,40 @@
         total[...] += nn(stage[k], r)
 
 
-def squeeze(v):
-    n = v.shape[0] // 4
-    out = v[:n]
-    for k in range(1, 4):
-        out = out + pltpu.roll(v[k * n : (k + 1) * n], 32 * k, 1)
-    return out
-
-
-def outer_back_kernel(
-    pgradt_ref, right_ref, outer_ref, w_ref, hat_ref, grad_ref, wout_ref, cross_ref,
-    stage, wacc, cacc,
-):
-    count, _, _ = pgradt_ref.shape
-    half = right_ref.shape[0]
-    depth = 1.0 / (right_ref.shape[1] * 3 // 4)
-
+def weight_kernel(
+    pgradt_ref, outer_ref, win_ref, wgg_ref, wfg_ref, cgain_ref, pgain_ref, bias_ref,
+    out_ref, wacc, wout,
+):
+    count = pgradt_ref.shape[0]
+    many = wacc.shape[0]
+    half = out_ref.shape[1] // 4
     wacc[...] = jnp.zeros_like(wacc)
 
-    @pl.loop(0, count // 2)
+    @pl.loop(0, count // 2, unroll=2)
     def _(m):
         a = jnp.concatenate([outer_ref[2 * m], outer_ref[2 * m + 1]], 1)
         b = jnp.concatenate([pgradt_ref[2 * m], pgradt_ref[2 * m + 1]], 1)
         wacc[...] += nt(a, b)
 
     for q in range(half):
-        wout_ref[pl.ds(q, half, stride=half), :] = wacc[q * half : (q + 1) * half, :]
+        wout[pl.ds(q, half, stride=half + 1), :] = wacc[q * half : (q + 1) * half, :]
+    for p in range(half):
+        out_ref[p * half : (p + 1) * half, :] = wout[
+            p * (half + 1) : p * (half + 1) + half, :
+        ].astype(BF)
+    at = many
+    for ref in (win_ref, wgg_ref, wfg_ref):
+        out_ref[at : at + ref.shape[0], :] = ref[...].astype(BF)
+        at += ref.shape[0]
+    rest = [cgain_ref[...], pgain_ref[...], bias_ref[...], jnp.zeros((13, 128), F32)]
+    out_ref[at : at + 16, :] = jnp.concatenate(rest, 0).astype(BF)
+    at += 16
+    out_ref[at:, :] = jnp.zeros((out_ref.shape[0] - at, 128), BF)
+
+
+def outer_back_kernel(pgradt_ref, right_ref, w_ref, grad_ref, stage):
+    count, _, _ = pgradt_ref.shape
+    depth = 1.0 / (right_ref.shape[1] * 3 // 4)
 
     @pl.loop(0, count, unroll=2)
     def _(i):
@@ -438,14 +468,6 @@
 
     contract(stage, right_ref, grad_ref)
     grad_ref[...] = grad_ref[...] * depth
-    cacc[...] = jnp.zeros_like(cacc)
-
-    @pl.loop(0, count)
-    def _(i):
-        g = grad_ref[pl.ds(pl.multiple_of(i * half, half), half), :].astype(BF)
-        cacc[...] += nt(hat_ref[i].astype(BF), pad_rows(g, 128))
-
-    cross_ref[...] = squeeze(cacc[...])
 
 
 def column_kernel(
@@ -473,7 +495,7 @@
     gain = as_column(mgain_ref)
     cacc[...] = jnp.zeros_like(cacc)
 
-    @pl.loop(0, pairs)
+    @pl.loop(0, pairs, unroll=3)
     def _(m):
         both = []
         for o in range(2):
@@ -481,18 +503,13 @@
             hat = hat_ref[i]
             at = pl.ds(pl.multiple_of(i * half, half), half)
             right = (gright[at, :] * (1.0 / length)).astype(BF)
-            cacc[...] += nt(hat.astype(BF), pad_rows(right, 128))
             g = jnp.concatenate([gleft_ref[at, :].astype(BF), right], 0)
+            cacc[...] += nt(hat.astype(BF), pad_rows(g, 128))
             both.append(norm_back(nn(wmap_ref[...], g) * gain, hat, inv_ref[i]))
         out_ref[m] = jnp.concatenate(both, 0).T[:length].astype(BF)
 
-    cross_ref[...] = squeeze(cacc[...])
-
-
-def unsqueeze(v):
-    lane = lax.broadcasted_iota(jnp.int32, v.shape, 1)
-    got = [v if k == 0 else pltpu.roll(v, 128 - 32 * k, 1) for k in range(4)]
-    return jnp.concatenate([jnp.where(lane < 32, g, 0.0) for g in got], 0)
+    rows = cross_ref.shape[0]
+    cross_ref[...] = (cacc[:rows, :] + pltpu.roll(cacc[rows:, :], 64, 1)).astype(BF)
 
 
 def finish_kernel(
@@ -501,7 +518,8 @@
     rows, flat,
 ):
     everyone, each, _ = all_ref.shape
-    own = each - 16
+    width = proj_out.shape[0]
+    own = each - width // 2
     eight = 8
 
     @pl.loop(0, everyone)
@@ -524,14 +542,11 @@
     at += channels
     wfg_out[...] = rows[at : at + channels, :]
     at += channels
-    left = unsqueeze(rows[at : at + 16, :])
-    at += 16
     cgain_out[...] = rows[at : at + 1, :]
     pgain_out[...] = rows[at + 1 : at + 2, :]
     bias_out[...] = rows[at + 2 : at + 3, :]
-    right = unsqueeze(jnp.sum(all_ref[:, own:].astype(F32), 0) * factor)
-    width = proj_out.shape[0]
-    cross = (left + pltpu.roll(right, 32, 1))[:, :width]
+    cross = jnp.sum(all_ref[:, own:].astype(F32), 0) * factor
+    cross = jnp.concatenate([cross, pltpu.roll(cross, 64, 1)], 0)[:, :width]
     proj_out[...] = cross * as_column(gain_ref)
     mgain_out[...] = as_row(jnp.sum(cross * wmap_ref[...].astype(F32), 1, keepdims=True))
 
@@ -557,7 +572,6 @@
     trilateral_final_matrix,
 ):
     n = lax.axis_size("dap")
-    everyone = n * lax.axis_size("dp")
     msa = homolog_features[0]
     depth, count, width = msa.shape
     length = edge_features.shape[2]
@@ -571,22 +585,24 @@
     msa_gain = line(homolog_scaling_factor)
 
     x = msa.reshape(depth, pairs, 2 * width).transpose(1, 0, 2)
-    left, left_send, right_send = call(
+    chips = n // 2
+    left, right_send, left_send = call(
+        2,
         project_kernel,
-        [((count, half, WIDE), BF), ((pairs, 3, half, 128), BF), ((pairs, 3, half, 128), BF)],
-        [],
+        [((count, half, WIDE), BF)] + [((chips, pairs, 3, half, 128), BF)] * 2,
+        [((pairs, 3, half, 128), BF)] * 2,
         x, msa_gain, tensor_mapping_matrix,
-    )
-    chips = n // 2
+        away=2, sems=(2, chips),
+    )
     groups = [list(range(0, n, 2)), list(range(1, n, 2))]
 
-    def everywhere(v):
-        own = exchange(jnp.broadcast_to(v, (chips,) + v.shape), groups=groups)
-        return own, lax.ppermute(own, "dap", [(i, i ^ 1) for i in range(n)])
-
-    own, other = everywhere(right_send)
+    def sibling(v):
+        return lax.ppermute(v, "dap", [(i, i ^ 1) for i in range(n)])
+
+    own = exchange(right_send, groups=groups)
+    other = sibling(own)
     left_send, other = lax.optimization_barrier((left_send, other))
-    left_own, left_other = everywhere(left_send)
+    left_own = exchange(left_send, groups=groups)
     parity = lax.rem(lax.axis_index("dap"), 2).astype(jnp.int32).reshape(1)
 
     qp = tensor_final_matrix.reshape(half, half, channels).transpose(1, 0, 2)
@@ -599,26 +615,33 @@
     outers = ((count, half * half, WIDE), BF)
     spare = [((length * (half + 1), 128), F32)] * 2
     edge_send, mid, normed, right, outer = call(
+        14,
         outer_kernel,
         [((n, pairs, 3, 2 * eight, 128), BF), wide32, wide, every, outers],
         spare + [every, outers],
         parity, own, other, left, edges, qp.T, line(tensor_final_offset),
-        line(edge_scaling_factor), entry.T, smem=1, away=2, copies=2,
-    )
+        line(edge_scaling_factor), entry.T, smem=1, away=2,
+    )
+    edge_send, left_own = lax.optimization_barrier((edge_send, left_own))
     edge_cols = exchange(edge_send)
-    gate, up = call(gate_kernel, [wide32, wide], [], normed, adjoint, final_sigmoid_matrix)
+    left_other = sibling(left_own)
+    gate, up = call(3, gate_kernel, [wide32, wide], [], normed, adjoint, final_sigmoid_matrix)
     rooms = [((length * (2 * eight + 1), 128), F32)] * 2
     rooms += [((length * (eight + 1), 128), F32)] * 2
     mixed_send, left_cols, right_cols = call(
+        3,
         triangle_kernel,
         [((n, pairs // 2, 3, 2 * eight, 128), BF)] + [((eight, length, WIDE), BF)] * 2,
-        rooms,
+        rooms + [((eight, length, WIDE), BF)] * 2,
         edge_cols,
-    )
+        away=2,
+    )
+    mixed_send, gate, up = lax.optimization_barrier((mixed_send, gate, up))
     mixed = exchange(mixed_send)
     square = ((channels, channels), F32)
     row = ((1, channels), F32)
     (grad_send,) = call(
+        2,
         update_kernel,
         [((n, pairs // 2, 3, 2 * eight, 128), BF)],
         [],
@@ -626,12 +649,14 @@
     )
     grad_cols = exchange(grad_send)
     pair_out, grad_gate, tri_out, tri_gate, mid_gain = call(
+        6,
         result_kernel,
         [(edges.shape, BF), wide, square, square, row],
         [((channels, WIDE), F32)],
         mixed, mid, normed, gate, up, line(central_scaling_factor), trilateral_final_matrix,
     )
     (back_send,) = call(
+        4,
         triangle_back_kernel,
         [((n, pairs, 3, 2 * eight, 128), BF)],
         rooms,
@@ -640,12 +665,14 @@
     back = exchange(back_send)
     left_own, left_other, back_send = lax.optimization_barrier((left_own, left_other, back_send))
     lefts, hat, inverse = call(
+        6,
         prepare_kernel,
         [every, ((count, width, WIDE), F32), ((count, 1, WIDE), F32)],
         spare,
         parity, left_own, left_other, x, smem=1,
     )
     pgrad, pgradt, pgrad_send, tri_in, tri_gain, bias = call(
+        9,
         edge_back_kernel,
         [
             (edges.shape, BF), wide, ((length * count, channels), BF),
@@ -659,22 +686,22 @@
     group = 4
     stage = ((half // group, count * half, group * WIDE), BF)
     grads = ((count * half, WIDE), F32)
-    cross = ((width // 4, 128), F32)
+    cross = ((width // 2, 128), BF)
     full = ((half * half, channels), F32)
-    grad_left, opm_out, cross_left = call(
-        outer_back_kernel,
-        [grads, full, cross],
-        [stage, full, ((width, 128), F32)],
-        pgradt, right, outer, qp, hat,
-    )
-    parts = [opm_out, tri_in, tri_gate, tri_out, cross_left, mid_gain, tri_gain, bias]
-    used = sum(p.shape[0] for p in parts)
-    each = -(-used // (16 * everyone)) * 16
-    parts.append(jnp.zeros((each * everyone - used, 128), F32))
-    mine = exchange(
-        jnp.concatenate(parts, 0).astype(BF).reshape(everyone, each, 128), ("dp", "dap")
-    )
-    sens, cross_right = call(
+    used = half * half + 6 * channels + 3
+    each = -(-used // (16 * n)) * 16
+    (weights,) = call(
+        6,
+        weight_kernel,
+        [((each * n, channels), BF)],
+        [full, ((half * (half + 1), channels), F32)],
+        pgradt, outer, tri_in, tri_gate, tri_out, mid_gain, tri_gain, bias,
+    )
+    (grad_left,) = call(7, outer_back_kernel, [grads], [stage], pgradt, right, qp)
+    weights, pgrad_cols = lax.optimization_barrier((weights, pgrad_cols))
+    mine = exchange(weights.reshape(n, each, channels))
+    sens, cross = call(
+        9,
         column_kernel,
         [((pairs, length, 2 * width), BF), cross],
         [((devices_rows(n, count), channels), F32), stage, grads, ((width, 128), F32)],
@@ -682,17 +709,20 @@
         msa_gain, tensor_mapping_matrix,
     )
     sensitivity = sens.transpose(1, 0, 2).reshape(depth, count, width)
-    mine = jnp.sum(mine.astype(F32), 0)
-    mine = jnp.concatenate([mine, cross_right], 0).astype(BF)
-    total = exchange(jnp.broadcast_to(mine, (everyone, each + 16, 128)), ("dp", "dap"))
-    factor = 1.0 / (lax.axis_size("dp") * length)
+    crops = lax.axis_size("dp")
+    mine = jnp.concatenate([jnp.sum(mine.astype(F32), 0).astype(BF), cross], 0)
+    mine = exchange(jnp.broadcast_to(mine, (crops,) + mine.shape), "dp")
+    mine = jnp.sum(mine.astype(F32), 0).astype(BF)
+    total = exchange(jnp.broadcast_to(mine, (n,) + mine.shape))
+    factor = 1.0 / (crops * length)
     last = call(
+        2,
         lambda *refs: finish_kernel(factor, *refs),
         [
             ((1, width), F32), ((width, 2 * half), F32), full, row, row,
             ((channels, 4 * channels), F32), square, row, square,
         ],
-        [((everyone * each, 128), F32), ((channels, 128), F32)],
+        [((n * each, 128), F32), ((channels, 128), F32)],
         total, msa_gain, tensor_mapping_matrix,
     )
     last = [v.reshape(-1) if v.shape[0] == 1 else v for v in last]

time: 253 us -> 224 us (0.89)
  blocking collectives: 80 us -> 54 us
  waiting for transfers between devices: 61.1 us -> 44.2 us
  local copies, waits for them, and re-layouts: 12.2 us -> 22.4 us
  starting transfers between devices: 21.4 us -> 30.8 us
  Pallas kernels: 74.6 us -> 70 us
    all_to_all x4 -> x3, blocking collectives: 80 us -> 54 us  [exchange(): lax.all_to_all(v, axes, split_axis=0, concat_axis=0, tiled=True, axis_ind...]
    all_to_all x5 -> x7, waiting for transfers between devices: 58.6 us -> 41.6 us  [exchange(): lax.all_to_all(v, axes, split_axis=0, concat_axis=0, tiled=True, axis_ind...]
    unnamed x59 -> x79, local copies, waits for them, and re-layouts: 6.44 us -> 18.9 us
    all_to_all x5 -> x7, starting transfers between devices: 21 us -> 30.5 us  [exchange(): lax.all_to_all(v, axes, split_axis=0, concat_axis=0, tiled=True, axis_ind...]
    pallas_call x12 -> x13, Pallas kernels: 74.6 us -> 70 us  [call(): pl.pallas_call(kernel, out_shape=[jax.ShapeDtypeStruct(s, t) for s, t in...]
  transfers between devices with their start and end apart: 7 -> 9, of which waited for: 6 -> 7; matrix products, arithmetic and copies ran while one was open for 1% -> 1% of each run, Pallas kernels for 8% -> 23%
where the time goes in v3:
time: 224 us; the launch traced here: 223 us
  Pallas kernels  70 us (31%)
  blocking collectives  54 us (24%)
  waiting for transfers between devices  44.2 us (20%)
  starting transfers between devices  30.8 us (14%)
  local copies, waits for them, and re-layouts  22.4 us (10%)
    pallas_call x13, Pallas kernels, call(): pl.pallas_call(kernel, out_shape=[jax.ShapeDtypeStruct(s, t) for s, t in...  70 us
    all_to_all x3, blocking collectives, exchange(): lax.all_to_all(v, axes, split_axis=0, concat_axis=0, tiled=True, axis_ind...  54 us
    all_to_all x7, waiting for transfers between devices, exchange(): lax.all_to_all(v, axes, split_axis=0, concat_axis=0, tiled=True, axis_ind...  41.6 us
    all_to_all x7, starting transfers between devices, exchange(): lax.all_to_all(v, axes, split_axis=0, concat_axis=0, tiled=True, axis_ind...  30.5 us
    unnamed x79, local copies, waits for them, and re-layouts  18.9 us
  transfers between devices with their start and end apart: 9, of which 7 were waited for; matrix products, arithmetic and copies ran while one was open for 1% of the time, Pallas kernels for 23%

profile of v3, /device:TPU:0, one launch (start us, length us, event | category | flops | bytes accessed | tf_op | source)
XLA Modules:
  0.0 222.6 jit_solution(8028942102281085745)
XLA Ops:
  0.6 1.2 copy.36
  1.9 0.7 copy-done.5
  2.6 0.7 copy-done.10
  3.2 3.3 %shard_map.211 = (bf16[12,32,256]{2,1,0:T(8,128)(2,1)S(1)}, bf16[8,6,3,32,128]{4,3,2,1,0:T(8,128)(2,1)S(1)}, bf16[8,6,3,32,128]{4,3,2,1,0:T(8,128)(2,1)}) custom-call(bf16[6,192,128]{2,1,0:T(8,128)(2,1)S(1)} %bitcast.36, f32[1,64]{1,0:T(1,128)S(1)} %bitcast.47, bf16[64,64]{1,0:T(8,128)(2,1)S(1)} %copy-done.5), custom_call_target="tpu_custom_call" | custom-call | flops 2000000000 | tf_op jit(solution)/shard_map/pallas_call | solution.py:84
  6.5 0.0 copy-start.38
  6.5 0.0 copy-start
  6.6 22.6 %all_to_all.50.own_ref = bf16[8,6,3,32,128]{4,3,2,1,0:T(8,128)(2,1)S(1)} all-to-all(bf16[8,6,3,32,128]{4,3,2,1,0:T(8,128)(2,1)S(1)} %get-tuple-element.61), channel_id=1, replica_groups={{0,2,4,6,8,10,12,14},{1,3,5,7,9,11,13,15},{16,18,20,22,24,26,28,30},{17..., dimensions={0} | all-to-all | bytes 2359296 | tf_op jit(solution)/shard_map/all_to_all | solution.py:555
  29.2 0.1 copy.38
  29.4 0.1 copy.37
  29.5 0.1 copy.40.wt_ref
  29.6 2.5 %collective-permute-done.other_ref = bf16[8,6,3,32,128]{4,3,2,1,0:T(8,128)(2,1)} collective-permute-done((bf16[8,6,3,32,128]{4,3,2,1,0:T(8,128)(2,1)S(1)}, bf16[8,6,3,32,128]{4,3,2,1,0:T(8,128)(2,1)}, u32[]{:S(2)}, u32[]{:S(2)}) %collective-permute-start) | collective-permute-done | bytes 1179680 | tf_op jit(solution)/shard_map/ppermute | solution.py:600
  32.2 3.7 %all-to-all-start.1 = ((bf16[8,6,3,32,128]{4,3,2,1,0:T(8,128)(2,1)}), bf16[8,6,3,32,128]{4,3,2,1,0:T(8,128)(2,1)S(1)}, u32[]{:S(2)}, u32[]{:S(2)}) async-start(bf16[8,6,3,32,128]{4,3,2,1,0:T(8,128)(2,1)} %get-tuple-element.66), calls=%async_computation.1 | async-start | bytes 2359296 | tf_op jit(solution)/shard_map/all_to_all | solution.py:555
  35.9 12.0 %shard_map.212 = (bf16[16,6,3,16,128]{4,3,2,1,0:T(8,128)(2,1)}, f32[12,128,256]{2,1,0:T(8,128)}, bf16[12,128,256]{2,1,0:T(8,128)(2,1)S(1)}, bf16[32,256,256]{2,1,0:T(8,128)(2,1)}, bf16[12,1024,256]{2,1,0:T(8,128)(2,1)}) custom-call(s32[1]{0:T(128)} %bitcast.par_ref, bf16[8,6,3,32,128]{4,3,2,1,0:T(8,128)(2,1)} %copy-done.37, ...), custom_call_target="tpu_custom_call" | custom-call | flops 14000000000 | tf_op jit(solution)/shard_map/pallas_call | solution.py:84
  48.0 0.9 copy-done.17
  48.9 6.1 %all-to-all-done.1.own_ref = bf16[8,6,3,32,128]{4,3,2,1,0:T(8,128)(2,1)S(1)} async-done(((bf16[8,6,3,32,128]{4,3,2,1,0:T(8,128)(2,1)}), bf16[8,6,3,32,128]{4,3,2,1,0:T(8,128)(2,1)S(1)}, u32[]{:S(2)}, u32[]{:S(2)}) %all-to-all-start.1) | async-done | bytes 1179680 | tf_op jit(solution)/shard_map/all_to_all | solution.py:555
  55.0 3.8 %all-to-all-start.2 = ((bf16[16,6,3,16,128]{4,3,2,1,0:T(8,128)(2,1)}), bf16[16,6,3,16,128]{4,3,2,1,0:T(8,128)(2,1)S(1)}, u32[]{:S(2)}, u32[]{:S(2)}) async-start(bf16[16,6,3,16,128]{4,3,2,1,0:T(8,128)(2,1)} %get-tuple-element.67), calls=%async_computation.2 | async-start | bytes 2359296 | tf_op jit(solution)/shard_map/all_to_all | solution.py:555
  58.8 0.0 copy-start.2
  58.8 1.1 copy-done.2
  59.9 1.1 copy-done.18
  61.0 2.7 %shard_map.214 = (f32[12,128,256]{2,1,0:T(8,128)S(1)}, bf16[12,128,256]{2,1,0:T(8,128)(2,1)S(1)}) custom-call(bf16[12,128,256]{2,1,0:T(8,128)(2,1)S(1)} %copy-done.18, bf16[12,192,128]{2,1,0:T(8,128)(2,1)S(1)} %bitcast.41, bf16[128,128]{1,0:T(8,128)(2,1)S(1)} %copy-done.4), custom_call_target="tpu_custom_call" | custom-call | flops 3000000000 | tf_op jit(solution)/shard_map/pallas_call | solution.py:84
  63.8 1.2 copy-done.12
  64.9 0.9 copy-done.14
  65.8 10.9 %all-to-all-done.2.edges_ref = bf16[16,6,3,16,128]{4,3,2,1,0:T(8,128)(2,1)S(1)} async-done(((bf16[16,6,3,16,128]{4,3,2,1,0:T(8,128)(2,1)}), bf16[16,6,3,16,128]{4,3,2,1,0:T(8,128)(2,1)S(1)}, u32[]{:S(2)}, u32[]{:S(2)}) %all-to-all-start.2) | async-done | bytes 1179680 | tf_op jit(solution)/shard_map/all_to_all | solution.py:555
  76.7 3.2 %shard_map.213 = (bf16[16,3,3,16,128]{4,3,2,1,0:T(8,128)(2,1)S(1)}, bf16[8,192,256]{2,1,0:T(8,128)(2,1)S(1)}, bf16[8,192,256]{2,1,0:T(8,128)(2,1)S(1)}) custom-call(bf16[16,6,3,16,128]{4,3,2,1,0:T(8,128)(2,1)S(1)} %all-to-all-done.2.edges_ref), custom_call_target="tpu_custom_call" | custom-call | flops 3000000000 | tf_op jit(solution)/shard_map/pallas_call | solution.py:84
  79.9 0.9 copy-done.21
  80.8 14.9 %all_to_all.51.mixed_ref = bf16[16,3,3,16,128]{4,3,2,1,0:T(8,128)(2,1)S(1)} all-to-all(bf16[16,3,3,16,128]{4,3,2,1,0:T(8,128)(2,1)S(1)} %get-tuple-element.72), channel_id=1, replica_groups=mesh['dp'=8,'dap'=16] {'dap'}, dimensions={0} | all-to-all | bytes 1179648 | tf_op jit(solution)/shard_map/all_to_all | solution.py:555
  95.7 2.1 shard_map.216
  97.8 3.6 %all-to-all-start.4 = ((bf16[16,3,3,16,128]{4,3,2,1,0:T(8,128)(2,1)}), bf16[16,3,3,16,128]{4,3,2,1,0:T(8,128)(2,1)S(1)}, u32[]{:S(2)}, u32[]{:S(2)}) async-start(bf16[16,3,3,16,128]{4,3,2,1,0:T(8,128)(2,1)} %shard_map.216), calls=%async_computation.4 | async-start | bytes 1179648 | tf_op jit(solution)/shard_map/all_to_all | solution.py:555
  101.4 0.3 collective-permute-start.1
  101.7 0.1 copy.41.entry_ref
  101.8 11.1 %all-to-all-done.4.grads_ref = bf16[16,3,3,16,128]{4,3,2,1,0:T(8,128)(2,1)S(1)} async-done(((bf16[16,3,3,16,128]{4,3,2,1,0:T(8,128)(2,1)}), bf16[16,3,3,16,128]{4,3,2,1,0:T(8,128)(2,1)S(1)}, u32[]{:S(2)}, u32[]{:S(2)}) %all-to-all-start.4) | async-done | bytes 589856 | tf_op jit(solution)/shard_map/all_to_all | solution.py:555
  113.0 1.1 copy-done.22
  114.1 1.1 copy-done.24
  115.2 4.1 %shard_map.217 = bf16[16,6,3,16,128]{4,3,2,1,0:T(8,128)(2,1)} custom-call(bf16[16,3,3,16,128]{4,3,2,1,0:T(8,128)(2,1)S(1)} %all-to-all-done.4.grads_ref, bf16[8,192,256]{2,1,0:T(8,128)(2,1)S(1)} %copy-done.22, bf16[8,192,256]{2,1,0:T(8,128)(2,1)S(1)} %copy-done.24), custom_call_target="tpu_custom_call" | custom-call | flops 4000000000 | tf_op jit(solution)/shard_map/pallas_call | solution.py:84
  119.4 4.4 %all-to-all-start.5 = ((bf16[16,6,3,16,128]{4,3,2,1,0:T(8,128)(2,1)}), bf16[16,6,3,16,128]{4,3,2,1,0:T(8,128)(2,1)}, u32[]{:S(2)}, u32[]{:S(2)}) async-start(bf16[16,6,3,16,128]{4,3,2,1,0:T(8,128)(2,1)} %shard_map.217), calls=%async_computation.5 | async-start | bytes 2359296 | tf_op jit(solution)/shard_map/all_to_all | solution.py:555
  123.8 1.1 copy-done.16
  124.9 1.1 copy-done.19
  126.0 5.7 %shard_map.215 = (bf16[12,192,128]{2,1,0:T(8,128)(2,1)}, bf16[12,128,256]{2,1,0:T(8,128)(2,1)S(1)}, f32[128,128]{1,0:T(8,128)S(1)}, f32[128,128]{1,0:T(8,128)S(1)}, f32[1,128]{1,0:T(1,128)S(1)}) custom-call(bf16[16,3,3,16,128]{4,3,2,1,0:T(8,128)(2,1)S(1)} %all_to_all.51.mixed_ref, f32[12,128,256]{2,1,0:T(8,128)} %get-tuple-element.73.mid_ref, ...), custom_call_target="tpu_custom_call" | custom-call | flops 6000000000 | tf_op jit(solution)/shard_map/pallas_call | solution.py:84
  131.7 0.9 copy-done.27
  132.7 0.6 copy-done.33
  133.3 0.6 copy-done.35
  133.9 6.0 %shard_map.220 = (bf16[32,256,256]{2,1,0:T(8,128)(2,1)}, f32[12,64,256]{2,1,0:T(8,128)S(1)}, f32[12,1,256]{2,1,0:T(1,128)S(1)}) custom-call(s32[1]{0:T(128)} %bitcast.par_ref, bf16[8,6,3,32,128]{4,3,2,1,0:T(8,128)(2,1)S(1)} %all-to-all-done.1.own_ref, bf16[8,6,3,32,128]{4,3,2,1,0:T(8,128)(2,1)} %collective-permute-done.1.other_ref, ...), custom_call_target="tpu_custom_call" | custom-call | flops 6000000000 | tf_op jit(solution)/shard_map/pallas_call | solution.py:84
  139.9 0.9 copy-done.29
  140.8 0.9 all-to-all-done.5.grads_ref
  141.7 1.1 copy-done.28
  142.8 7.8 %shard_map.218 = (bf16[12,192,128]{2,1,0:T(8,128)(2,1)}, bf16[12,128,256]{2,1,0:T(8,128)(2,1)S(1)}, bf16[2304,128]{1,0:T(8,128)(2,1)}, f32[512,128]{1,0:T(8,128)...) custom-call(bf16[16,6,3,16,128]{4,3,2,1,0:T(8,128)(2,1)} %all-to-all-done.5.grads_ref, ...), custom_call_target="tpu_custom_call" | custom-call | flops 8999999488 | tf_op jit(solution)/shard_map/pallas_call | solution.py:84
  150.6 0.9 copy-done.25
  151.5 4.9 %all-to-all-start.6 = ((bf16[16,144,128]{2,1,0:T(8,128)(2,1)}), bf16[16,144,128]{2,1,0:T(8,128)(2,1)S(1)}, u32[]{:S(2)}, u32[]{:S(2)}) async-start(bf16[16,144,128]{2,1,0:T(8,128)(2,1)} %bitcast.20), calls=%async_computation.6 | async-start | bytes 1179648 | tf_op jit(solution)/shard_map/all_to_all | solution.py:555
  156.4 0.0 copy-start.36
  156.4 7.3 %shard_map.221.gleft_ref = f32[384,256]{1,0:T(8,128)S(1)} custom-call(bf16[12,128,256]{2,1,0:T(8,128)(2,1)S(1)} %copy-done.26, bf16[32,256,256]{2,1,0:T(8,128)(2,1)} %get-tuple-element.95.right_ref, bf16[1024,128]{1,0:T(8,128)(2,1)S(1)} %bitcast.32), custom_call_target="tpu_custom_call" | custom-call | flops 7000000000 | tf_op jit(solution)/shard_map/pallas_call | solution.py:84
  163.8 0.0 copy-start.31
  163.8 0.7 copy-done.31
  164.5 5.9 %shard_map.219 = bf16[2048,128]{1,0:T(8,128)(2,1)} custom-call(bf16[12,128,256]{2,1,0:T(8,128)(2,1)S(1)} %copy-done.26, bf16[12,1024,256]{2,1,0:T(8,128)(2,1)} %get-tuple-element.82.outer_ref, f32[512,128]{1,0:T(8,128)S(1)} %get-tuple-element.83.win_ref, f32[128,128]{1,0:T(8,128)S(1)} %copy-done.36, f32[128,128]{1,0:T(8,128)S(1)} %copy-done.34, ...), custom_call_target="tpu_custom_call" | custom-call | flops 6000000000 | tf_op jit(solution)/shard_map/pallas_call | solution.py:84
  170.4 5.7 %all-to-all-start.7 = ((bf16[16,128,128]{2,1,0:T(8,128)(2,1)}), bf16[16,128,128]{2,1,0:T(8,128)(2,1)S(1)}, u32[]{:S(2)}, u32[]{:S(2)}) async-start(bf16[16,128,128]{2,1,0:T(8,128)(2,1)} %bitcast.24), calls=%async_computation.7 | async-start | bytes 1048576 | tf_op jit(solution)/shard_map/all_to_all | solution.py:555
  176.2 1.0 copy-done.32
  177.2 8.5 %shard_map.222 = (bf16[6,192,128]{2,1,0:T(8,128)(2,1)S(1)}, bf16[32,128]{1,0:T(8,128)(2,1)S(1)}) custom-call(bf16[16,144,128]{2,1,0:T(8,128)(2,1)S(1)} %all-to-all-done.6.pcol_ref, bf16[32,256,256]{2,1,0:T(8,128)(2,1)} %get-tuple-element.94.left_ref, bf16[1024,128]{1,0:T(8,128)(2,1)S(1)} %copy-done, f32[384,256]{1,0:T(8,128)S(1)} %copy-done.32, ...), custom_call_target="tpu_custom_call" | custom-call | flops 8999999488 | tf_op jit(solution)/shard_map/pallas_call | solution.py:84
  185.6 1.3 all-to-all-done.7
  187.0 0.1 reduce_sum.24
  187.1 16.5 %all_to_all.52 = bf16[8,160,128]{2,1,0:T(8,128)(2,1)S(1)} all-to-all(bf16[8,160,128]{2,1,0:T(8,128)(2,1)S(1)} %broadcast_in_dim.14), channel_id=1, replica_groups=mesh['dp'=8,'dap'=16] {'dp'}, dimensions={0} | all-to-all | bytes 655360 | tf_op jit(solution)/shard_map/all_to_all | solution.py:555
  203.6 0.9 broadcast_in_dim.15
  204.6 4.4 %all-to-all-start.9 = ((bf16[16,160,128]{2,1,0:T(8,128)(2,1)}), bf16[16,160,128]{2,1,0:T(8,128)(2,1)S(1)}, u32[]{:S(2)}, u32[]{:S(2)}) async-start(bf16[16,160,128]{2,1,0:T(8,128)(2,1)} %broadcast_in_dim.15), calls=%async_computation.9 | async-start | bytes 1310720 | tf_op jit(solution)/shard_map/all_to_all | solution.py:555
  209.0 0.9 copy.42
  210.0 11.3 %all-to-all-done.9.refs_0_ = bf16[16,160,128]{2,1,0:T(8,128)(2,1)S(1)} async-done(((bf16[16,160,128]{2,1,0:T(8,128)(2,1)}), bf16[16,160,128]{2,1,0:T(8,128)(2,1)S(1)}, u32[]{:S(2)}, u32[]{:S(2)}) %all-to-all-start.9) | async-done | bytes 655392 | tf_op jit(solution)/shard_map/all_to_all | solution.py:555
  221.3 1.3 shard_map.223
  (60 shorter events, 0.2 us)
Async XLA Ops:
  1.9 0.7 copy-start.5
  2.6 0.7 copy-start.10
  6.5 22.7 %copy-start.38 = (bf16[128,512]{1,0:T(8,128)(2,1)S(1)}, bf16[128,512]{1,0:T(8,128)(2,1)}, u32[]{:S(2)}) copy-start(bf16[128,512]{1,0:T(8,128)(2,1)} %param.20) | copy-start | bytes 393220
  6.5 22.8 %copy-start = (bf16[1024,128]{1,0:T(8,128)(2,1)S(1)}, bf16[1024,128]{1,0:T(8,128)(2,1)}, u32[]{:S(2)}) copy-start(bf16[1024,128]{1,0:T(8,128)(2,1)} %w_ref.3) | copy-start | bytes 786436
  29.2 3.0 %copy-start.37 = (bf16[8,6,3,32,128]{4,3,2,1,0:T(8,128)(2,1)}, bf16[8,6,3,32,128]{4,3,2,1,0:T(8,128)(2,1)S(1)}, u32[]{:S(2)}) copy-start(bf16[8,6,3,32,128]{4,3,2,1,0:T(8,128)(2,1)S(1)} %all_to_all.50.own_ref) | copy-start | bytes 3538948
  29.2 3.0 %collective-permute-start = (bf16[8,6,3,32,128]{4,3,2,1,0:T(8,128)(2,1)S(1)}, bf16[8,6,3,32,128]{4,3,2,1,0:T(8,128)(2,1)}, u32[]{:S(2)}, u32[]{:S(2)}) collective-permute-start(bf16[8,6,3,32,128]{4,3,2,1,0:T(8,128)(2,1)S(1)} %all_to_all.50.own_ref), channel_id=1, source_target_pairs={{0,1},{1,0},{2,3},{3,2},{4,5},{5,4},{6,7},{7,6},{8,9},{9,8},{10,11... | collective-permute-start | bytes 3538952 | tf_op jit(solution)/shard_map/ppermute | solution.py:600
  32.2 3.7 %copy-start.1 = (bf16[1,12,192,128]{3,2,1,0:T(8,128)(2,1)S(1)}, bf16[1,12,192,128]{3,2,1,0:T(8,128)(2,1)}, u32[]{:S(2)}) copy-start(bf16[1,12,192,128]{3,2,1,0:T(8,128)(2,1)} %param.13) | copy-start | bytes 1769476
  32.2 3.7 %copy-start.7 = (f32[128]{0:T(128)S(1)}, f32[128]{0:T(128)}, u32[]{:S(2)}) copy-start(f32[128]{0:T(128)} %param.18) | copy-start | bytes 1540
  32.2 3.7 %copy-start.9 = (f32[128]{0:T(128)S(1)}, f32[128]{0:T(128)}, u32[]{:S(2)}) copy-start(f32[128]{0:T(128)} %param.19) | copy-start | bytes 1540
  32.2 22.8 %all-to-all-start.1 = ((bf16[8,6,3,32,128]{4,3,2,1,0:T(8,128)(2,1)}), bf16[8,6,3,32,128]{4,3,2,1,0:T(8,128)(2,1)S(1)}, u32[]{:S(2)}, u32[]{:S(2)}) async-start(bf16[8,6,3,32,128]{4,3,2,1,0:T(8,128)(2,1)} %get-tuple-element.66), calls=%async_computation.1 | async-start | bytes 2359296 | tf_op jit(solution)/shard_map/all_to_all | solution.py:555
  48.0 0.9 copy-start.17
  55.0 3.8 %copy-start.4 = (bf16[128,128]{1,0:T(8,128)(2,1)S(1)}, bf16[128,128]{1,0:T(8,128)(2,1)}, u32[]{:S(2)}) copy-start(bf16[128,128]{1,0:T(8,128)(2,1)} %wg_ref.3) | copy-start | bytes 98308
  55.0 21.7 %all-to-all-start.2 = ((bf16[16,6,3,16,128]{4,3,2,1,0:T(8,128)(2,1)}), bf16[16,6,3,16,128]{4,3,2,1,0:T(8,128)(2,1)S(1)}, u32[]{:S(2)}, u32[]{:S(2)}) async-start(bf16[16,6,3,16,128]{4,3,2,1,0:T(8,128)(2,1)} %get-tuple-element.67), calls=%async_computation.2 | async-start | bytes 2359296 | tf_op jit(solution)/shard_map/all_to_all | solution.py:555
  58.8 1.1 copy-start.2
  59.9 1.1 copy-start.18
  63.7 1.2 copy-start.12
  64.9 0.9 copy-start.14
  76.7 19.0 %copy-start.13 = (f32[12,128,256]{2,1,0:T(8,128)S(1)}, f32[12,128,256]{2,1,0:T(8,128)}, u32[]{:S(2)}) copy-start(f32[12,128,256]{2,1,0:T(8,128)} %copy-done.12) | copy-start | bytes 4718596
  79.9 0.9 copy-start.21
  80.8 14.9 %copy-start.23 = (bf16[8,192,256]{2,1,0:T(8,128)(2,1)}, bf16[8,192,256]{2,1,0:T(8,128)(2,1)S(1)}, u32[]{:S(2)}) copy-start(bf16[8,192,256]{2,1,0:T(8,128)(2,1)S(1)} %get-tuple-element.78.right_ref) | copy-start | bytes 2359300
  80.8 14.9 %copy-start.3 = (bf16[128,128]{1,0:T(8,128)(2,1)S(1)}, bf16[128,128]{1,0:T(8,128)(2,1)}, u32[]{:S(2)}) copy-start(bf16[128,128]{1,0:T(8,128)(2,1)} %wf_ref.3) | copy-start | bytes 98308
  80.8 14.9 %copy-start.8 = (f32[128]{0:T(128)S(1)}, f32[128]{0:T(128)}, u32[]{:S(2)}) copy-start(f32[128]{0:T(128)} %param.22) | copy-start | bytes 1540
  80.8 14.9 %copy-start.15 = (bf16[12,128,256]{2,1,0:T(8,128)(2,1)S(1)}, bf16[12,128,256]{2,1,0:T(8,128)(2,1)}, u32[]{:S(2)}) copy-start(bf16[12,128,256]{2,1,0:T(8,128)(2,1)} %copy-done.14) | copy-start | bytes 2359300
  97.8 15.1 %all-to-all-start.4 = ((bf16[16,3,3,16,128]{4,3,2,1,0:T(8,128)(2,1)}), bf16[16,3,3,16,128]{4,3,2,1,0:T(8,128)(2,1)S(1)}, u32[]{:S(2)}, u32[]{:S(2)}) async-start(bf16[16,3,3,16,128]{4,3,2,1,0:T(8,128)(2,1)} %shard_map.216), calls=%async_computation.4 | async-start | bytes 1179648 | tf_op jit(solution)/shard_map/all_to_all | solution.py:555
  101.4 32.5 %collective-permute-start.1 = (bf16[8,6,3,32,128]{4,3,2,1,0:T(8,128)(2,1)S(1)}, bf16[8,6,3,32,128]{4,3,2,1,0:T(8,128)(2,1)}, u32[]{:S(2)}, u32[]{:S(2)}) collective-permute-start(bf16[8,6,3,32,128]{4,3,2,1,0:T(8,128)(2,1)S(1)} %all-to-all-done.1.own_ref), channel_id=1, source_target_pairs={{0,1},{1,0},{2,3},{3,2},{4,5},{5,4},{6,7},{7,6},{8,9},{9,8},{10,11... | collective-permute-start | bytes 3538952 | tf_op jit(solution)/shard_map/ppermute | solution.py:600
  113.0 1.1 copy-start.22
  114.1 1.1 copy-start.24
  119.4 22.3 %all-to-all-start.5 = ((bf16[16,6,3,16,128]{4,3,2,1,0:T(8,128)(2,1)}), bf16[16,6,3,16,128]{4,3,2,1,0:T(8,128)(2,1)}, u32[]{:S(2)}, u32[]{:S(2)}) async-start(bf16[16,6,3,16,128]{4,3,2,1,0:T(8,128)(2,1)} %shard_map.217), calls=%async_computation.5 | async-start | bytes 2359296 | tf_op jit(solution)/shard_map/all_to_all | solution.py:555
  123.8 1.1 copy-start.16
  124.9 1.1 copy-start.19
  131.7 0.9 copy-start.27
  132.6 0.6 copy-start.33
  133.3 0.6 copy-start.35
  133.9 7.7 %copy-start.20 = (bf16[12,128,256]{2,1,0:T(8,128)(2,1)S(1)}, bf16[12,128,256]{2,1,0:T(8,128)(2,1)}, u32[]{:S(2)}) copy-start(bf16[12,128,256]{2,1,0:T(8,128)(2,1)} %copy-done.17) | copy-start | bytes 2359300
  139.9 0.9 copy-start.29
  141.6 1.1 copy-start.28
  150.6 0.9 copy-start.25
  151.5 4.9 %copy-start.26 = (bf16[12,128,256]{2,1,0:T(8,128)(2,1)S(1)}, bf16[12,128,256]{2,1,0:T(8,128)(2,1)}, u32[]{:S(2)}) copy-start(bf16[12,128,256]{2,1,0:T(8,128)(2,1)} %copy-done.25) | copy-start | bytes 2359300
  151.5 18.9 %all-to-all-start.6 = ((bf16[16,144,128]{2,1,0:T(8,128)(2,1)}), bf16[16,144,128]{2,1,0:T(8,128)(2,1)S(1)}, u32[]{:S(2)}, u32[]{:S(2)}) async-start(bf16[16,144,128]{2,1,0:T(8,128)(2,1)} %bitcast.20), calls=%async_computation.6 | async-start | bytes 1179648 | tf_op jit(solution)/shard_map/all_to_all | solution.py:555
  156.4 8.1 %copy-start.34 = (f32[128,128]{1,0:T(8,128)S(1)}, f32[128,128]{1,0:T(8,128)}, u32[]{:S(2)}) copy-start(f32[128,128]{1,0:T(8,128)} %copy-done.33) | copy-start | bytes 196612
  156.4 8.1 %copy-start.36 = (f32[128,128]{1,0:T(8,128)S(1)}, f32[128,128]{1,0:T(8,128)}, u32[]{:S(2)}) copy-start(f32[128,128]{1,0:T(8,128)} %copy-done.35) | copy-start | bytes 196612
  163.8 0.7 copy-start.31
  164.5 11.6 %copy-start.6 = (bf16[64,64]{1,0:T(8,128)(2,1)S(1)}, bf16[64,64]{1,0:T(8,128)(2,1)}, u32[]{:S(2)}) copy-start(bf16[64,64]{1,0:T(8,128)(2,1)} %refs_2_.1) | copy-start | bytes 24580
  164.5 11.6 %copy-start.11 = (f32[64]{0:T(128)S(1)}, f32[64]{0:T(128)}, u32[]{:S(2)}) copy-start(f32[64]{0:T(128)} %param.15) | copy-start | bytes 772
  164.5 11.6 %copy-start.30 = (f32[12,64,256]{2,1,0:T(8,128)S(1)}, f32[12,64,256]{2,1,0:T(8,128)}, u32[]{:S(2)}) copy-start(f32[12,64,256]{2,1,0:T(8,128)} %copy-done.29) | copy-start | bytes 2359300
  170.4 16.6 %all-to-all-start.7 = ((bf16[16,128,128]{2,1,0:T(8,128)(2,1)}), bf16[16,128,128]{2,1,0:T(8,128)(2,1)S(1)}, u32[]{:S(2)}, u32[]{:S(2)}) async-start(bf16[16,128,128]{2,1,0:T(8,128)(2,1)} %bitcast.24), calls=%async_computation.7 | async-start | bytes 1048576 | tf_op jit(solution)/shard_map/all_to_all | solution.py:555
  176.2 1.0 copy-start.32
  204.6 16.7 %all-to-all-start.9 = ((bf16[16,160,128]{2,1,0:T(8,128)(2,1)}), bf16[16,160,128]{2,1,0:T(8,128)(2,1)S(1)}, u32[]{:S(2)}, u32[]{:S(2)}) async-start(bf16[16,160,128]{2,1,0:T(8,128)(2,1)} %broadcast_in_dim.15), calls=%async_computation.9 | async-start | bytes 1310720 | tf_op jit(solution)/shard_map/all_to_all | solution.py:555

commit v4 on v3

--- a/solution.py
+++ b/solution.py
@@ -1,3 +1,5 @@
+import math
+
 import jax
 import jax.numpy as jnp
 from jax import lax
@@ -75,15 +77,56 @@
     return jnp.sum(jnp.where(a == b, column, 0.0), 0, keepdims=True)
 
 
-def call(us, kernel, outs, scratch, *operands, smem=0, away=0, sems=None):
+class Coming:
+    def __init__(self, far, buffer, sems, axis):
+        self.far, self.buffer, self.sems, self.axis = far, buffer, sems, axis
+        self.shape, self.at = buffer.shape, buffer.at
+        for k in range(sems.shape[0]):
+            self.copy(k).start()
+
+    def __getitem__(self, index):
+        return self.buffer[index]
+
+    def copy(self, k):
+        size = self.shape[self.axis] // self.sems.shape[0]
+        cut = (slice(None),) * self.axis + (pl.ds(k * size, size),)
+        return pltpu.make_async_copy(self.far.at[cut], self.buffer.at[cut], self.sems.at[k])
+
+    def wait(self, k=0):
+        self.copy(k).wait()
+
+
+def call(us, kernel, outs, scratch, *operands, smem=0, away=0, sems=None, far=None):
+    far = far or {}
+    operands = [
+        pltpu.with_memory_space_constraint(v, pltpu.HBM) if i in far else v
+        for i, v in enumerate(operands)
+    ]
     specs = [pl.BlockSpec(memory_space=pltpu.SMEM)] * smem
-    specs += [pl.BlockSpec(memory_space=pltpu.VMEM)] * (len(operands) - smem)
+    specs += [
+        pl.BlockSpec(memory_space=pltpu.HBM if i in far else pltpu.VMEM)
+        for i in range(smem, len(operands))
+    ]
     room = [pltpu.VMEM(s, t) for s, t in scratch]
     if away:
         room.append(pltpu.SemaphoreType.DMA(sems or (away,)))
+    plain = len(operands) + len(outs) + len(room)
+    for i, (pieces, _) in far.items():
+        room.append(pltpu.VMEM(operands[i].shape, operands[i].dtype))
+        room.append(pltpu.SemaphoreType.DMA((pieces,)))
+
+    def wrapped(*refs):
+        refs = list(refs)
+        for k, (i, (_, axis)) in enumerate(far.items()):
+            refs[i] = Coming(refs[i], refs[plain + 2 * k], refs[plain + 2 * k + 1], axis)
+        kernel(*refs[:plain])
+
     return pl.pallas_call(
-        kernel,
-        out_shape=[jax.ShapeDtypeStruct(s, t) for s, t in outs],
+        wrapped,
+        out_shape=[
+            pltpu.HBM(s, t) if math.prod(s) > 131072 else jax.ShapeDtypeStruct(s, t)
+            for s, t in outs
+        ],
         in_specs=specs,
         out_specs=[pl.BlockSpec(memory_space=pltpu.VMEM)] * (len(outs) - away)
         + [pl.BlockSpec(memory_space=pltpu.HBM)] * away,
@@ -158,8 +201,9 @@
     pitch = half + 1
     par = par_ref[0]
     for source, p in ((own_ref, par), (other_ref, 1 - par)):
-
-        @pl.loop(0, chips)
+        source.wait()
+
+        @pl.loop(0, chips, unroll=2)
         def _(chip):
             spread_projections(source.at[chip], (2 * chip + p) * rows, 1, pitch, head, tail)
 
@@ -183,6 +227,8 @@
     devices, _, _, sixteen, _ = send_ref.shape
     bias = as_column(bias_ref)
     gain = as_column(gain_ref)
+    for ref in (edge_ref, wt_ref, entry_ref):
+        ref.wait()
 
     @pl.loop(0, pairs, unroll=3)
     def _(m):
@@ -215,7 +261,7 @@
     devices, pairs, _, high, _ = source.shape
     many = high // half
 
-    @pl.loop(0, devices)
+    @pl.loop(0, devices, unroll=4)
     def _(d):
         for m in range(pairs):
             t = source[d, m].astype(F32)
@@ -230,7 +276,7 @@
     devices, pairs, _, high, _ = target.shape
     many = high // half
 
-    @pl.loop(0, devices)
+    @pl.loop(0, devices, unroll=4)
     def _(d):
         for m in range(pairs):
             wide = []
@@ -270,6 +316,8 @@
 def triangle_back_kernel(grads_ref, left_ref, right_ref, send_ref, head, tail, mhead, mtail):
     channels, length, _ = left_ref.shape
     spread(grads_ref, channels, mhead, mtail)
+    left_ref.wait()
+    right_ref.wait()
     for c in range(channels):
         g = pad_rows(load_wide(mhead, mtail, c, length, channels + 1), WIDE).astype(BF)
         store_wide(head, tail, c, length, 2 * channels + 1, nt(right_ref[c], g))
@@ -320,6 +368,8 @@
     wgg_ref[...] = jnp.zeros_like(wgg_ref)
     acc[...] = jnp.zeros_like(acc)
     cgain = as_column(cgain_ref)
+    for ref in (mixed_ref, mid_ref, normed_ref, gate_ref, up_ref):
+        ref.wait()
 
     @pl.loop(0, quads)
     def _(n):
@@ -353,8 +403,7 @@
     bacc[...] = jnp.zeros_like(bacc)
     gain = as_column(gain_ref)
 
-    @pl.loop(0, pairs, unroll=3)
-    def _(m):
+    def step(m):
         t = [grads_ref[:, m, k].astype(F32).reshape(devices * sixteen, 128) for k in range(3)]
         for o, (a, b) in enumerate(unpack(*t)):
             i = 2 * m + o
@@ -376,6 +425,12 @@
             pgrad_ref[i] = turned.astype(BF)
             rows[pl.ds(i, length, stride=count), :] = turned
 
+    third = pairs // 2
+    for h in range(2):
+        for ref in (grads_ref, mid_ref, normed_ref, ggate_ref, up_ref):
+            ref.wait(h)
+        pl.loop(h * third, (h + 1) * third, unroll=third)(step)
+
     send_ref[...] = rows[...].astype(BF)
     gsum_ref[...] = jnp.sum(gacc[...].T, 0, keepdims=True)
     bsum_ref[...] = jnp.sum(bacc[...].T, 0, keepdims=True)
@@ -421,7 +476,7 @@
     group = stage.shape[2] // WIDE
     total[...] = jnp.zeros_like(total)
 
-    @pl.loop(0, stage.shape[0], unroll=2)
+    @pl.loop(0, stage.shape[0], unroll=4)
     def _(k):
         r = projections[pl.ds(k * group, group)].reshape(group * WIDE, WIDE)
         total[...] += nn(stage[k], r)
@@ -436,11 +491,15 @@
     half = out_ref.shape[1] // 4
     wacc[...] = jnp.zeros_like(wacc)
 
-    @pl.loop(0, count // 2, unroll=2)
-    def _(m):
+    def step(m):
         a = jnp.concatenate([outer_ref[2 * m], outer_ref[2 * m + 1]], 1)
         b = jnp.concatenate([pgradt_ref[2 * m], pgradt_ref[2 * m + 1]], 1)
         wacc[...] += nt(a, b)
+
+    third = count // 4
+    for h in range(2):
+        outer_ref.wait(h)
+        pl.loop(h * third, (h + 1) * third, unroll=third)(step)
 
     for q in range(half):
         wout[pl.ds(q, half, stride=half + 1), :] = wacc[q * half : (q + 1) * half, :]
@@ -462,10 +521,11 @@
     count, _, _ = pgradt_ref.shape
     depth = 1.0 / (right_ref.shape[1] * 3 // 4)
 
-    @pl.loop(0, count, unroll=2)
+    @pl.loop(0, count, unroll=4)
     def _(i):
         put(stage, i, nn(w_ref[...], pgradt_ref[i]).astype(BF))
 
+    right_ref.wait()
     contract(stage, right_ref, grad_ref)
     grad_ref[...] = grad_ref[...] * depth
 
@@ -480,18 +540,21 @@
     length = devices * count
     pairs = count // 2
 
-    @pl.loop(0, devices)
+    @pl.loop(0, devices, unroll=4)
     def _(d):
         prow[pl.ds(d * (many + 1), many), :] = pcol_ref[d].astype(F32)
 
-    @pl.loop(0, count, unroll=2)
+    @pl.loop(0, count, unroll=4)
     def _(j):
         p = jnp.concatenate(
             [prow[pl.ds(j * count + i, devices, stride=many + 1), :] for i in range(count)], 0
         )
         put(stage, j, nt(w_ref[...], pad_rows(p, WIDE).astype(BF)).astype(BF))
 
+    left_ref.wait()
     contract(stage, left_ref, gright)
+    gleft_ref.wait()
+    hat_ref.wait()
     gain = as_column(mgain_ref)
     cacc[...] = jnp.zeros_like(cacc)
 
@@ -621,6 +684,7 @@
         spare + [every, outers],
         parity, own, other, left, edges, qp.T, line(tensor_final_offset),
         line(edge_scaling_factor), entry.T, smem=1, away=2,
+        far={1: (1, 0), 2: (1, 0), 4: (1, 0), 5: (1, 0), 8: (1, 0)},
     )
     edge_send, left_own = lax.optimization_barrier((edge_send, left_own))
     edge_cols = exchange(edge_send)
@@ -654,6 +718,7 @@
         [(edges.shape, BF), wide, square, square, row],
         [((channels, WIDE), F32)],
         mixed, mid, normed, gate, up, line(central_scaling_factor), trilateral_final_matrix,
+        far={i: (1, 0) for i in range(5)},
     )
     (back_send,) = call(
         4,
@@ -661,6 +726,7 @@
         [((n, pairs, 3, 2 * eight, 128), BF)],
         rooms,
         grad_cols, left_cols, right_cols,
+        far={1: (1, 0), 2: (1, 0)},
     )
     back = exchange(back_send)
     left_own, left_other, back_send = lax.optimization_barrier((left_own, left_other, back_send))
@@ -681,6 +747,7 @@
         [((channels, WIDE), F32)] * 2 + [((length * count, channels), F32)],
         back, mid, normed, grad_gate, up, line(edge_scaling_factor),
         entry.T, entry, final_sigmoid_matrix,
+        far={0: (2, 1), 1: (2, 0), 2: (2, 0), 3: (2, 0), 4: (2, 0)},
     )
     pgrad_cols = exchange(pgrad_send.reshape(n, count * count, channels))
     group = 4
@@ -696,8 +763,11 @@
         [((each * n, channels), BF)],
         [full, ((half * (half + 1), channels), F32)],
         pgradt, outer, tri_in, tri_gate, tri_out, mid_gain, tri_gain, bias,
-    )
-    (grad_left,) = call(7, outer_back_kernel, [grads], [stage], pgradt, right, qp)
+        far={1: (2, 0)},
+    )
+    (grad_left,) = call(
+        7, outer_back_kernel, [grads], [stage], pgradt, right, qp, far={1: (1, 0)}
+    )
     weights, pgrad_cols = lax.optimization_barrier((weights, pgrad_cols))
     mine = exchange(weights.reshape(n, each, channels))
     sens, cross = call(
@@ -707,6 +777,7 @@
         [((devices_rows(n, count), channels), F32), stage, grads, ((width, 128), F32)],
         pgrad_cols, lefts, tensor_final_matrix, grad_left, hat, inverse,
         msa_gain, tensor_mapping_matrix,
+        far={1: (1, 0), 3: (1, 0), 4: (1, 0)},
     )
     sensitivity = sens.transpose(1, 0, 2).reshape(depth, count, width)
     crops = lax.axis_size("dp")

time: 224 us -> 213 us (0.951)
  local copies, waits for them, and re-layouts: 22.4 us -> 9.8 us
  waiting for transfers between devices: 44.2 us -> 52.8 us
  Pallas kernels: 70 us -> 64.9 us
  starting transfers between devices: 30.8 us -> 28.5 us
    unnamed x79 -> x45, local copies, waits for them, and re-layouts: 18.9 us -> 4.79 us
    all_to_all x7, waiting for transfers between devices: 41.6 us -> 51.9 us  [exchange(): lax.all_to_all(v, axes, split_axis=0, concat_axis=0, tiled=True, axis_ind...]
    pallas_call x13, Pallas kernels: 70 us -> 64.9 us  [call(): pl.pallas_call(wrapped, out_shape=[pltpu.HBM(s, t) if math.prod(s) > 1310...]
    all_to_all x7, starting transfers between devices: 30.5 us -> 28.2 us  [exchange(): lax.all_to_all(v, axes, split_axis=0, concat_axis=0, tiled=True, axis_ind...]
  transfers between devices with their start and end apart: 9 -> 9, of which waited for: 7 -> 8; matrix products, arithmetic and copies ran while one was open for 1% -> 1% of each run, Pallas kernels for 23% -> 23%
where the time goes in v4:
time: 213 us; the launch traced here: 212 us
  Pallas kernels  64.9 us (30%)
  blocking collectives  54.5 us (26%)
  waiting for transfers between devices  52.8 us (25%)
  starting transfers between devices  28.5 us (13%)
  local copies, waits for them, and re-layouts  9.8 us (5%)
    pallas_call x13, Pallas kernels, call(): pl.pallas_call(wrapped, out_shape=[pltpu.HBM(s, t) if math.prod(s) > 1310...  64.9 us
    all_to_all x3, blocking collectives, exchange(): lax.all_to_all(v, axes, split_axis=0, concat_axis=0, tiled=True, axis_ind...  54.5 us
    all_to_all x7, waiting for transfers between devices, exchange(): lax.all_to_all(v, axes, split_axis=0, concat_axis=0, tiled=True, axis_ind...  51.9 us
    all_to_all x7, starting transfers between devices, exchange(): lax.all_to_all(v, axes, split_axis=0, concat_axis=0, tiled=True, axis_ind...  28.2 us
    unnamed x45, local copies, waits for them, and re-layouts  4.79 us
  transfers between devices with their start and end apart: 9, of which 8 were waited for; matrix products, arithmetic and copies ran while one was open for 1% of the time, Pallas kernels for 23%

profile of v4, /device:TPU:0, one launch (start us, length us, event | category | flops | bytes accessed | tf_op | source)
XLA Modules:
  0.0 211.7 jit_solution(4351084385638930692)
XLA Ops:
  0.6 1.2 copy.36
  1.9 0.0 copy-start.6
  1.9 0.7 copy-done.6
  2.6 0.7 copy-done.11
  3.2 2.6 %shard_map.211 = (bf16[12,32,256]{2,1,0:T(8,128)(2,1)S(1)}, bf16[8,6,3,32,128]{4,3,2,1,0:T(8,128)(2,1)}, bf16[8,6,3,32,128]{4,3,2,1,0:T(8,128)(2,1)}) custom-call(bf16[6,192,128]{2,1,0:T(8,128)(2,1)S(1)} %bitcast.36, f32[1,64]{1,0:T(1,128)S(1)} %bitcast.45, bf16[64,64]{1,0:T(8,128)(2,1)S(1)} %copy-done.6), custom_call_target="tpu_custom_call" | custom-call | flops 2000000000 | tf_op jit(solution)/shard_map/pallas_call | solution.py:124
  5.8 0.0 copy-start.20
  5.8 0.0 copy-start.2
  5.8 22.9 %all_to_all.50.refs_1_ = bf16[8,6,3,32,128]{4,3,2,1,0:T(8,128)(2,1)S(1)} all-to-all(bf16[8,6,3,32,128]{4,3,2,1,0:T(8,128)(2,1)} %get-tuple-element.61), channel_id=1, replica_groups={{0,2,4,6,8,10,12,14},{1,3,5,7,9,11,13,15},{16,18,20,22,24,26,28,30},{17..., dimensions={0} | all-to-all | bytes 2359296 | tf_op jit(solution)/shard_map/all_to_all | solution.py:618
  28.7 0.0 collective-permute-start
  28.7 0.0 copy-done.20
  28.7 0.1 copy.38
  28.8 0.8 copy.39
  29.7 0.1 copy.37
  29.8 0.8 copy.40.refs_5_
  30.6 0.9 collective-permute-done.refs_2_
  31.6 1.0 copy-done.21
  32.6 0.0 copy-done.18
  32.6 3.7 %all-to-all-start.1 = ((bf16[8,6,3,32,128]{4,3,2,1,0:T(8,128)(2,1)}), bf16[8,6,3,32,128]{4,3,2,1,0:T(8,128)(2,1)S(1)}, u32[]{:S(2)}, u32[]{:S(2)}) async-start(bf16[8,6,3,32,128]{4,3,2,1,0:T(8,128)(2,1)} %get-tuple-element.66), calls=%async_computation.1 | async-start | bytes 2359296 | tf_op jit(solution)/shard_map/all_to_all | solution.py:618
  36.3 11.4 %shard_map.212 = (bf16[16,6,3,16,128]{4,3,2,1,0:T(8,128)(2,1)}, f32[12,128,256]{2,1,0:T(8,128)}, bf16[12,128,256]{2,1,0:T(8,128)(2,1)}, bf16[32,256,256]{2,1,0:T(8,128)(2,1)}, bf16[12,1024,256]{2,1,0:T(8,128)(2,1)}) custom-call(s32[1]{0:T(128)} %bitcast.refs_0_, bf16[8,6,3,32,128]{4,3,2,1,0:T(8,128)(2,1)} %copy-done.18, ...), custom_call_target="tpu_custom_call" | custom-call | flops 14000000000 | tf_op jit(solution)/shard_map/pallas_call | solution.py:124
  47.7 7.7 %all-to-all-done.1.refs_1_ = bf16[8,6,3,32,128]{4,3,2,1,0:T(8,128)(2,1)S(1)} async-done(((bf16[8,6,3,32,128]{4,3,2,1,0:T(8,128)(2,1)}), bf16[8,6,3,32,128]{4,3,2,1,0:T(8,128)(2,1)S(1)}, u32[]{:S(2)}, u32[]{:S(2)}) %all-to-all-start.1) | async-done | bytes 1179680 | tf_op jit(solution)/shard_map/all_to_all | solution.py:618
  55.4 3.8 %all-to-all-start.2 = ((bf16[16,6,3,16,128]{4,3,2,1,0:T(8,128)(2,1)}), bf16[16,6,3,16,128]{4,3,2,1,0:T(8,128)(2,1)S(1)}, u32[]{:S(2)}, u32[]{:S(2)}) async-start(bf16[16,6,3,16,128]{4,3,2,1,0:T(8,128)(2,1)} %get-tuple-element.67), calls=%async_computation.2 | async-start | bytes 2359296 | tf_op jit(solution)/shard_map/all_to_all | solution.py:618
  59.2 0.0 copy-start.3
  59.2 1.1 copy-done.3
  60.3 1.1 copy-done.15
  61.4 4.0 %shard_map.214 = (f32[12,128,256]{2,1,0:T(8,128)}, bf16[12,128,256]{2,1,0:T(8,128)(2,1)}) custom-call(bf16[12,128,256]{2,1,0:T(8,128)(2,1)S(1)} %copy-done.15, bf16[12,192,128]{2,1,0:T(8,128)(2,1)S(1)} %bitcast.39, bf16[128,128]{1,0:T(8,128)(2,1)S(1)} %copy-done.5), custom_call_target="tpu_custom_call" | custom-call | flops 3000000000 | tf_op jit(solution)/shard_map/pallas_call | solution.py:124
  65.5 11.6 %all-to-all-done.2.refs_0_ = bf16[16,6,3,16,128]{4,3,2,1,0:T(8,128)(2,1)S(1)} async-done(((bf16[16,6,3,16,128]{4,3,2,1,0:T(8,128)(2,1)}), bf16[16,6,3,16,128]{4,3,2,1,0:T(8,128)(2,1)S(1)}, u32[]{:S(2)}, u32[]{:S(2)}) %all-to-all-start.2) | async-done | bytes 1179680 | tf_op jit(solution)/shard_map/all_to_all | solution.py:618
  77.1 2.8 %shard_map.213 = (bf16[16,3,3,16,128]{4,3,2,1,0:T(8,128)(2,1)}, bf16[8,192,256]{2,1,0:T(8,128)(2,1)}, bf16[8,192,256]{2,1,0:T(8,128)(2,1)}) custom-call(bf16[16,6,3,16,128]{4,3,2,1,0:T(8,128)(2,1)S(1)} %all-to-all-done.2.refs_0_), custom_call_target="tpu_custom_call" | custom-call | flops 3000000000 | tf_op jit(solution)/shard_map/pallas_call | solution.py:124
  79.9 0.0 copy-start.4
  79.9 0.0 copy-start.9
  79.9 15.2 %all_to_all.51.refs_0_ = bf16[16,3,3,16,128]{4,3,2,1,0:T(8,128)(2,1)S(1)} all-to-all(bf16[16,3,3,16,128]{4,3,2,1,0:T(8,128)(2,1)} %get-tuple-element.72), channel_id=1, replica_groups=mesh['dp'=8,'dap'=16] {'dap'}, dimensions={0} | all-to-all | bytes 1179648 | tf_op jit(solution)/shard_map/all_to_all | solution.py:618
  95.2 0.0 copy-done.9
  95.2 2.1 %shard_map.216 = bf16[16,3,3,16,128]{4,3,2,1,0:T(8,128)(2,1)} custom-call(bf16[16,3,3,16,128]{4,3,2,1,0:T(8,128)(2,1)S(1)} %all_to_all.51.refs_0_, f32[12,128,256]{2,1,0:T(8,128)S(1)} %copy-done.13, bf16[12,128,256]{2,1,0:T(8,128)(2,1)S(1)} %copy-done.14, f32[1,128]{1,0:T(1,128)S(1)} %bitcast.41, bf16[128,128]{1,0:T(8,128)(2,1)S(1)} %copy-done.4), custom_call_target="tpu_custom_call" | custom-call | flops 2000000000 | tf_op jit(solution)/shard_map/pallas_call | solution.py:124
  97.3 3.7 %all-to-all-start.4 = ((bf16[16,3,3,16,128]{4,3,2,1,0:T(8,128)(2,1)}), bf16[16,3,3,16,128]{4,3,2,1,0:T(8,128)(2,1)S(1)}, u32[]{:S(2)}, u32[]{:S(2)}) async-start(bf16[16,3,3,16,128]{4,3,2,1,0:T(8,128)(2,1)} %shard_map.216), calls=%async_computation.4 | async-start | bytes 1179648 | tf_op jit(solution)/shard_map/all_to_all | solution.py:618
  101.0 0.3 collective-permute-start.1
  101.3 0.1 copy.41.refs_7_
  101.4 11.1 %all-to-all-done.4.refs_0_ = bf16[16,3,3,16,128]{4,3,2,1,0:T(8,128)(2,1)S(1)} async-done(((bf16[16,3,3,16,128]{4,3,2,1,0:T(8,128)(2,1)}), bf16[16,3,3,16,128]{4,3,2,1,0:T(8,128)(2,1)S(1)}, u32[]{:S(2)}, u32[]{:S(2)}) %all-to-all-start.4) | async-done | bytes 589856 | tf_op jit(solution)/shard_map/all_to_all | solution.py:618
  112.5 3.5 %shard_map.217 = bf16[16,6,3,16,128]{4,3,2,1,0:T(8,128)(2,1)} custom-call(bf16[16,3,3,16,128]{4,3,2,1,0:T(8,128)(2,1)S(1)} %all-to-all-done.4.refs_0_, bf16[8,192,256]{2,1,0:T(8,128)(2,1)} %get-tuple-element.77.refs_1_, bf16[8,192,256]{2,1,0:T(8,128)(2,1)} %get-tuple-element.78.refs_2_), custom_call_target="tpu_custom_call" | custom-call | flops 4000000000 | tf_op jit(solution)/shard_map/pallas_call | solution.py:124
  116.0 4.6 %all-to-all-start.5 = ((bf16[16,6,3,16,128]{4,3,2,1,0:T(8,128)(2,1)}), bf16[16,6,3,16,128]{4,3,2,1,0:T(8,128)(2,1)}, u32[]{:S(2)}, u32[]{:S(2)}) async-start(bf16[16,6,3,16,128]{4,3,2,1,0:T(8,128)(2,1)} %shard_map.217), calls=%async_computation.5 | async-start | bytes 2359296 | tf_op jit(solution)/shard_map/all_to_all | solution.py:618
  120.6 6.6 %shard_map.215 = (bf16[12,192,128]{2,1,0:T(8,128)(2,1)}, bf16[12,128,256]{2,1,0:T(8,128)(2,1)}, f32[128,128]{1,0:T(8,128)S(1)}, f32[128,128]{1,0:T(8,128)S(1)}, f32[1,128]{1,0:T(1,128)S(1)}) custom-call(bf16[16,3,3,16,128]{4,3,2,1,0:T(8,128)(2,1)} %copy-done, f32[12,128,256]{2,1,0:T(8,128)} %get-tuple-element.73.refs_1_, ...), custom_call_target="tpu_custom_call" | custom-call | flops 6000000000 | tf_op jit(solution)/shard_map/pallas_call | solution.py:124
  127.2 0.0 collective-permute-done.1.refs_2_
  127.2 6.2 %shard_map.220 = (bf16[32,256,256]{2,1,0:T(8,128)(2,1)}, f32[12,64,256]{2,1,0:T(8,128)}, f32[12,1,256]{2,1,0:T(1,128)S(1)}) custom-call(s32[1]{0:T(128)} %bitcast.refs_0_, bf16[8,6,3,32,128]{4,3,2,1,0:T(8,128)(2,1)S(1)} %all-to-all-done.1.refs_1_, bf16[8,6,3,32,128]{4,3,2,1,0:T(8,128)(2,1)} %collective-permute-done.1.refs_2_, bf16[6,192,128]{2,1,0:T(8,128)(2,1)S(1)} %bitcast.37), custom_call_target="tpu_custom_call" | custom-call | flops 6000000000 | tf_op jit(solution)/shard_map/pallas_call | solution.py:124
  133.4 5.0 %all-to-all-done.5.refs_0_ = bf16[16,6,3,16,128]{4,3,2,1,0:T(8,128)(2,1)} async-done(((bf16[16,6,3,16,128]{4,3,2,1,0:T(8,128)(2,1)}), bf16[16,6,3,16,128]{4,3,2,1,0:T(8,128)(2,1)}, u32[]{:S(2)}, u32[]{:S(2)}) %all-to-all-start.5) | async-done | bytes 1179680 | tf_op jit(solution)/shard_map/all_to_all | solution.py:618
  138.3 7.5 %shard_map.218 = (bf16[12,192,128]{2,1,0:T(8,128)(2,1)}, bf16[12,128,256]{2,1,0:T(8,128)(2,1)}, bf16[2304,128]{1,0:T(8,128)(2,1)}, f32[512,128]{1,0:T(8,128)S(1)...) custom-call(bf16[16,6,3,16,128]{4,3,2,1,0:T(8,128)(2,1)} %all-to-all-done.5.refs_0_, ...), custom_call_target="tpu_custom_call" | custom-call | flops 8999999488 | tf_op jit(solution)/shard_map/pallas_call | solution.py:124
  145.8 3.7 %all-to-all-start.6 = ((bf16[16,144,128]{2,1,0:T(8,128)(2,1)}), bf16[16,144,128]{2,1,0:T(8,128)(2,1)S(1)}, u32[]{:S(2)}, u32[]{:S(2)}) async-start(bf16[16,144,128]{2,1,0:T(8,128)(2,1)} %bitcast.48), calls=%async_computation.6 | async-start | bytes 1179648 | tf_op jit(solution)/shard_map/all_to_all | solution.py:618
  149.6 0.0 copy-done.16
  149.6 4.4 %shard_map.221.refs_3_ = f32[384,256]{1,0:T(8,128)S(1)} custom-call(bf16[12,128,256]{2,1,0:T(8,128)(2,1)S(1)} %copy-done.16, bf16[32,256,256]{2,1,0:T(8,128)(2,1)} %get-tuple-element.95.refs_1_, bf16[1024,128]{1,0:T(8,128)(2,1)S(1)} %bitcast.32), custom_call_target="tpu_custom_call" | custom-call | flops 7000000000 | tf_op jit(solution)/shard_map/pallas_call | solution.py:124
  154.0 0.0 copy-start.17
  154.0 0.0 copy-start.7
  154.0 0.0 copy-start.12
  154.1 6.4 %shard_map.219 = bf16[2048,128]{1,0:T(8,128)(2,1)} custom-call(bf16[12,128,256]{2,1,0:T(8,128)(2,1)S(1)} %copy-done.16, bf16[12,1024,256]{2,1,0:T(8,128)(2,1)} %get-tuple-element.82.refs_1_, f32[512,128]{1,0:T(8,128)S(1)} %get-tuple-element.83.refs_2_, f32[128,128]{1,0:T(8,128)S(1)} %get-tuple-element.84.refs_3_, f32[128,128]{1,0:T(8,128)S(1)} %get-tuple-element.85.refs_4_, ...), custom_call_target="tpu_custom_call" | custom-call | flops 6000000000 | tf_op jit(solution)/shard_map/pallas_call | solution.py:124
  160.5 0.0 copy-done.17
  160.5 0.6 all-to-all-done.6.refs_0_
  161.1 5.0 %all-to-all-start.7 = ((bf16[16,128,128]{2,1,0:T(8,128)(2,1)}), bf16[16,128,128]{2,1,0:T(8,128)(2,1)S(1)}, u32[]{:S(2)}, u32[]{:S(2)}) async-start(bf16[16,128,128]{2,1,0:T(8,128)(2,1)} %bitcast.49), calls=%async_computation.7 | async-start | bytes 1048576 | tf_op jit(solution)/shard_map/all_to_all | solution.py:618
  166.1 0.0 copy-done.7
  166.2 0.0 copy-done.12
  166.2 6.2 %shard_map.222 = (bf16[6,192,128]{2,1,0:T(8,128)(2,1)}, bf16[32,128]{1,0:T(8,128)(2,1)S(1)}) custom-call(bf16[16,144,128]{2,1,0:T(8,128)(2,1)S(1)} %all-to-all-done.6.refs_0_, bf16[32,256,256]{2,1,0:T(8,128)(2,1)} %get-tuple-element.94.refs_1_, bf16[1024,128]{1,0:T(8,128)(2,1)S(1)} %copy-done.2, f32[384,256]{1,0:T(8,128)} %copy-done.17, ...), custom_call_target="tpu_custom_call" | custom-call | flops 8999999488 | tf_op jit(solution)/shard_map/pallas_call | solution.py:124
  172.4 4.6 %all-to-all-done.7 = bf16[16,128,128]{2,1,0:T(8,128)(2,1)S(1)} async-done(((bf16[16,128,128]{2,1,0:T(8,128)(2,1)}), bf16[16,128,128]{2,1,0:T(8,128)(2,1)S(1)}, u32[]{:S(2)}, u32[]{:S(2)}) %all-to-all-start.7) | async-done | bytes 524320 | tf_op jit(solution)/shard_map/all_to_all | solution.py:618
  177.0 0.1 reduce_sum.24
  177.1 16.4 %all_to_all.52 = bf16[8,160,128]{2,1,0:T(8,128)(2,1)S(1)} all-to-all(bf16[8,160,128]{2,1,0:T(8,128)(2,1)S(1)} %broadcast_in_dim.14), channel_id=1, replica_groups=mesh['dp'=8,'dap'=16] {'dp'}, dimensions={0} | all-to-all | bytes 655360 | tf_op jit(solution)/shard_map/all_to_all | solution.py:618
  193.6 0.9 broadcast_in_dim.15
  194.6 3.6 %all-to-all-start.9 = ((bf16[16,160,128]{2,1,0:T(8,128)(2,1)}), bf16[16,160,128]{2,1,0:T(8,128)(2,1)S(1)}, u32[]{:S(2)}, u32[]{:S(2)}) async-start(bf16[16,160,128]{2,1,0:T(8,128)(2,1)} %broadcast_in_dim.15), calls=%async_computation.9 | async-start | bytes 1310720 | tf_op jit(solution)/shard_map/all_to_all | solution.py:618
  198.2 0.9 copy.42
  199.1 11.3 %all-to-all-done.9.refs_0_ = bf16[16,160,128]{2,1,0:T(8,128)(2,1)S(1)} async-done(((bf16[16,160,128]{2,1,0:T(8,128)(2,1)}), bf16[16,160,128]{2,1,0:T(8,128)(2,1)S(1)}, u32[]{:S(2)}, u32[]{:S(2)}) %all-to-all-start.9) | async-done | bytes 655392 | tf_op jit(solution)/shard_map/all_to_all | solution.py:618
  210.4 1.3 shard_map.223
  (26 shorter events, 0.1 us)
Async XLA Ops:
  1.9 0.7 copy-start.6
  2.6 0.7 copy-start.11
  5.8 22.9 %copy-start.20 = (bf16[128,512]{1,0:T(8,128)(2,1)S(1)}, bf16[128,512]{1,0:T(8,128)(2,1)}, u32[]{:S(2)}) copy-start(bf16[128,512]{1,0:T(8,128)(2,1)} %param.20) | copy-start | bytes 393220
  5.8 23.8 %copy-start.2 = (bf16[1024,128]{1,0:T(8,128)(2,1)S(1)}, bf16[1024,128]{1,0:T(8,128)(2,1)}, u32[]{:S(2)}) copy-start(bf16[1024,128]{1,0:T(8,128)(2,1)} %refs_2_.6) | copy-start | bytes 786436
  28.7 3.9 %copy-start.18 = (bf16[8,6,3,32,128]{4,3,2,1,0:T(8,128)(2,1)}, bf16[8,6,3,32,128]{4,3,2,1,0:T(8,128)(2,1)S(1)}, u32[]{:S(2)}) copy-start(bf16[8,6,3,32,128]{4,3,2,1,0:T(8,128)(2,1)S(1)} %all_to_all.50.refs_1_) | copy-start | bytes 3538948
  28.7 2.8 %collective-permute-start = (bf16[8,6,3,32,128]{4,3,2,1,0:T(8,128)(2,1)S(1)}, bf16[8,6,3,32,128]{4,3,2,1,0:T(8,128)(2,1)S(1)}, u32[]{:S(2)}, u32[]{:S(2)}) collective-permute-start(bf16[8,6,3,32,128]{4,3,2,1,0:T(8,128)(2,1)S(1)} %all_to_all.50.refs_1_), channel_id=1, source_target_pairs={{0,1},{1,0},{2,3},{3,2},{4,5},{5,4},{6,7},{7,6},{8,9},{9,8},{10,11... | collective-permute-start | bytes 3538952 | tf_op jit(solution)/shard_map/ppermute | solution.py:663
  31.6 1.0 copy-start.21
  32.6 3.7 %copy-start.8 = (f32[128]{0:T(128)S(1)}, f32[128]{0:T(128)}, u32[]{:S(2)}) copy-start(f32[128]{0:T(128)} %param.18) | copy-start | bytes 1540
  32.6 3.7 %copy-start.10 = (f32[128]{0:T(128)S(1)}, f32[128]{0:T(128)}, u32[]{:S(2)}) copy-start(f32[128]{0:T(128)} %param.19) | copy-start | bytes 1540
  32.6 22.8 %all-to-all-start.1 = ((bf16[8,6,3,32,128]{4,3,2,1,0:T(8,128)(2,1)}), bf16[8,6,3,32,128]{4,3,2,1,0:T(8,128)(2,1)S(1)}, u32[]{:S(2)}, u32[]{:S(2)}) async-start(bf16[8,6,3,32,128]{4,3,2,1,0:T(8,128)(2,1)} %get-tuple-element.66), calls=%async_computation.1 | async-start | bytes 2359296 | tf_op jit(solution)/shard_map/all_to_all | solution.py:618
  55.4 3.8 %copy-start.5 = (bf16[128,128]{1,0:T(8,128)(2,1)S(1)}, bf16[128,128]{1,0:T(8,128)(2,1)}, u32[]{:S(2)}) copy-start(bf16[128,128]{1,0:T(8,128)(2,1)} %refs_8_.1) | copy-start | bytes 98308
  55.4 21.7 %all-to-all-start.2 = ((bf16[16,6,3,16,128]{4,3,2,1,0:T(8,128)(2,1)}), bf16[16,6,3,16,128]{4,3,2,1,0:T(8,128)(2,1)S(1)}, u32[]{:S(2)}, u32[]{:S(2)}) async-start(bf16[16,6,3,16,128]{4,3,2,1,0:T(8,128)(2,1)} %get-tuple-element.67), calls=%async_computation.2 | async-start | bytes 2359296 | tf_op jit(solution)/shard_map/all_to_all | solution.py:618
  59.2 1.1 copy-start.3
  60.3 1.1 copy-start.15
  77.1 18.1 %copy-start.13 = (f32[12,128,256]{2,1,0:T(8,128)S(1)}, f32[12,128,256]{2,1,0:T(8,128)}, u32[]{:S(2)}) copy-start(f32[12,128,256]{2,1,0:T(8,128)} %get-tuple-element.74.refs_3_.refs_1_) | copy-start | bytes 4718596
  79.9 15.3 %copy-start.4 = (bf16[128,128]{1,0:T(8,128)(2,1)S(1)}, bf16[128,128]{1,0:T(8,128)(2,1)}, u32[]{:S(2)}) copy-start(bf16[128,128]{1,0:T(8,128)(2,1)} %refs_4_.1) | copy-start | bytes 98308
  79.9 15.3 %copy-start.9 = (f32[128]{0:T(128)S(1)}, f32[128]{0:T(128)}, u32[]{:S(2)}) copy-start(f32[128]{0:T(128)} %param.22) | copy-start | bytes 1540
  79.9 15.3 %copy-start.14 = (bf16[12,128,256]{2,1,0:T(8,128)(2,1)S(1)}, bf16[12,128,256]{2,1,0:T(8,128)(2,1)}, u32[]{:S(2)}) copy-start(bf16[12,128,256]{2,1,0:T(8,128)(2,1)} %get-tuple-element.75.refs_4_.refs_2_) | copy-start | bytes 2359300
  95.2 2.1 %copy-start = (bf16[16,3,3,16,128]{4,3,2,1,0:T(8,128)(2,1)}, bf16[16,3,3,16,128]{4,3,2,1,0:T(8,128)(2,1)S(1)}, u32[]{:S(2)}) copy-start(bf16[16,3,3,16,128]{4,3,2,1,0:T(8,128)(2,1)S(1)} %all_to_all.51.refs_0_) | copy-start | bytes 1769476
  97.3 4.0 %copy-start.1 = (bf16[128,2,16,2,8]{0,4,3,2,1:T(8,128)(2,1)S(1)}, bf16[128,2,16,2,8]{0,4,3,2,1:T(8,128)(2,1)}, u32[]{:S(2)}) copy-start(bf16[128,2,16,2,8]{0,4,3,2,1:T(8,128)(2,1)} %copy.39) | copy-start | bytes 393220
  97.3 15.2 %all-to-all-start.4 = ((bf16[16,3,3,16,128]{4,3,2,1,0:T(8,128)(2,1)}), bf16[16,3,3,16,128]{4,3,2,1,0:T(8,128)(2,1)S(1)}, u32[]{:S(2)}, u32[]{:S(2)}) async-start(bf16[16,3,3,16,128]{4,3,2,1,0:T(8,128)(2,1)} %shard_map.216), calls=%async_computation.4 | async-start | bytes 1179648 | tf_op jit(solution)/shard_map/all_to_all | solution.py:618
  101.0 26.2 %collective-permute-start.1 = (bf16[8,6,3,32,128]{4,3,2,1,0:T(8,128)(2,1)S(1)}, bf16[8,6,3,32,128]{4,3,2,1,0:T(8,128)(2,1)}, u32[]{:S(2)}, u32[]{:S(2)}) collective-permute-start(bf16[8,6,3,32,128]{4,3,2,1,0:T(8,128)(2,1)S(1)} %all-to-all-done.1.refs_1_), channel_id=1, source_target_pairs={{0,1},{1,0},{2,3},{3,2},{4,5},{5,4},{6,7},{7,6},{8,9},{9,8},{10,11... | collective-permute-start | bytes 3538952 | tf_op jit(solution)/shard_map/ppermute | solution.py:663
  116.0 22.3 %all-to-all-start.5 = ((bf16[16,6,3,16,128]{4,3,2,1,0:T(8,128)(2,1)}), bf16[16,6,3,16,128]{4,3,2,1,0:T(8,128)(2,1)}, u32[]{:S(2)}, u32[]{:S(2)}) async-start(bf16[16,6,3,16,128]{4,3,2,1,0:T(8,128)(2,1)} %shard_map.217), calls=%async_computation.5 | async-start | bytes 2359296 | tf_op jit(solution)/shard_map/all_to_all | solution.py:618
  145.8 3.7 %copy-start.16 = (bf16[12,128,256]{2,1,0:T(8,128)(2,1)S(1)}, bf16[12,128,256]{2,1,0:T(8,128)(2,1)}, u32[]{:S(2)}) copy-start(bf16[12,128,256]{2,1,0:T(8,128)(2,1)} %get-tuple-element.81.refs_0_) | copy-start | bytes 2359300
  145.8 15.3 %all-to-all-start.6 = ((bf16[16,144,128]{2,1,0:T(8,128)(2,1)}), bf16[16,144,128]{2,1,0:T(8,128)(2,1)S(1)}, u32[]{:S(2)}, u32[]{:S(2)}) async-start(bf16[16,144,128]{2,1,0:T(8,128)(2,1)} %bitcast.48), calls=%async_computation.6 | async-start | bytes 1179648 | tf_op jit(solution)/shard_map/all_to_all | solution.py:618
  154.0 6.5 %copy-start.17 = (f32[384,256]{1,0:T(8,128)}, f32[384,256]{1,0:T(8,128)S(1)}, u32[]{:S(2)}) copy-start(f32[384,256]{1,0:T(8,128)S(1)} %shard_map.221.refs_3_) | copy-start | bytes 1179652
  154.0 12.1 %copy-start.7 = (bf16[64,64]{1,0:T(8,128)(2,1)S(1)}, bf16[64,64]{1,0:T(8,128)(2,1)}, u32[]{:S(2)}) copy-start(bf16[64,64]{1,0:T(8,128)(2,1)} %refs_2_.7) | copy-start | bytes 24580
  154.0 12.1 %copy-start.12 = (f32[64]{0:T(128)S(1)}, f32[64]{0:T(128)}, u32[]{:S(2)}) copy-start(f32[64]{0:T(128)} %param.15) | copy-start | bytes 772
  161.1 15.9 %all-to-all-start.7 = ((bf16[16,128,128]{2,1,0:T(8,128)(2,1)}), bf16[16,128,128]{2,1,0:T(8,128)(2,1)S(1)}, u32[]{:S(2)}, u32[]{:S(2)}) async-start(bf16[16,128,128]{2,1,0:T(8,128)(2,1)} %bitcast.49), calls=%async_computation.7 | async-start | bytes 1048576 | tf_op jit(solution)/shard_map/all_to_all | solution.py:618
  193.6 4.6 %copy-start.19 = (bf16[6,192,128]{2,1,0:T(8,128)(2,1)S(1)}, bf16[6,192,128]{2,1,0:T(8,128)(2,1)}, u32[]{:S(2)}) copy-start(bf16[6,192,128]{2,1,0:T(8,128)(2,1)} %get-tuple-element.98) | copy-start | bytes 884740
  194.6 15.8 %all-to-all-start.9 = ((bf16[16,160,128]{2,1,0:T(8,128)(2,1)}), bf16[16,160,128]{2,1,0:T(8,128)(2,1)S(1)}, u32[]{:S(2)}, u32[]{:S(2)}) async-start(bf16[16,160,128]{2,1,0:T(8,128)(2,1)} %broadcast_in_dim.15), calls=%async_computation.9 | async-start | bytes 1310720 | tf_op jit(solution)/shard_map/all_to_all | solution.py:618

commit v5 on v4

--- a/solution.py
+++ b/solution.py
@@ -81,8 +81,6 @@
     def __init__(self, far, buffer, sems, axis):
         self.far, self.buffer, self.sems, self.axis = far, buffer, sems, axis
         self.shape, self.at = buffer.shape, buffer.at
-        for k in range(sems.shape[0]):
-            self.copy(k).start()
 
     def __getitem__(self, index):
         return self.buffer[index]
@@ -119,6 +117,10 @@
         refs = list(refs)
         for k, (i, (_, axis)) in enumerate(far.items()):
             refs[i] = Coming(refs[i], refs[plain + 2 * k], refs[plain + 2 * k + 1], axis)
+        for k in range(max([pieces for pieces, _ in far.values()], default=0)):
+            for i, (pieces, _) in far.items():
+                if k < pieces:
+                    refs[i].copy(k).start()
         kernel(*refs[:plain])
 
     return pl.pallas_call(
@@ -191,7 +193,7 @@
 
 def outer_kernel(
     par_ref, own_ref, other_ref, left_ref, edge_ref, wt_ref, bias_ref, gain_ref, entry_ref,
-    send_ref, mid_ref, normed_ref, right_out, outer_out,
+    send_ref, mid_ref, normed_ref, sig_ref, slope_ref, right_out, outer_out,
     head, tail, right_ref, outer_ref, sems,
 ):
     chips, pairs, _, half, _ = own_ref.shape
@@ -242,7 +244,11 @@
             normed_ref[i] = normed
             raw = nn(entry_ref[...], normed)
             cut = raw.shape[0] // 2
-            both.append(sigmoid(raw[:cut]) * raw[cut:])
+            sig = sigmoid(raw[:cut])
+            edge = sig * raw[cut:]
+            both.append(edge)
+            sig_ref[i] = sig.astype(BF)
+            slope_ref[i] = (edge * (1.0 - sig)).astype(BF)
         for t, v in enumerate(pack(*both)):
             send_ref[:, m, t] = v.reshape(devices, sixteen, 128).astype(BF)
 
@@ -393,7 +399,7 @@
 
 
 def edge_back_kernel(
-    grads_ref, mid_ref, normed_ref, ggate_ref, up_ref, gain_ref, entryt_ref, entry_ref, wg_ref,
+    grads_ref, mid_ref, normed_ref, ggate_ref, up_ref, sig_ref, slope_ref, gain_ref, entry_ref, wg_ref,
     pgrad_ref, pgradt_ref, send_ref, win_ref, gsum_ref, bsum_ref, gacc, bacc, rows,
 ):
     devices, pairs, _, sixteen, _ = grads_ref.shape
@@ -402,6 +408,7 @@
     gacc[...] = jnp.zeros_like(gacc)
     bacc[...] = jnp.zeros_like(bacc)
     gain = as_column(gain_ref)
+    entry_ref.wait()
 
     def step(m):
         t = [grads_ref[:, m, k].astype(F32).reshape(devices * sixteen, 128) for k in range(3)]
@@ -409,11 +416,8 @@
             i = 2 * m + o
             grad = jnp.concatenate([a, b], 1)
             normed = normed_ref[i]
-            raw = nn(entryt_ref[...], normed)
-            cut = raw.shape[0] // 2
-            sig = sigmoid(raw[:cut])
-            gs = grad * sig
-            graw = jnp.concatenate([gs * raw[cut:] * (1.0 - sig), gs], 0).astype(BF)
+            slope, sig = slope_ref[i].astype(F32), sig_ref[i].astype(F32)
+            graw = jnp.concatenate([grad * slope, grad * sig], 0).astype(BF)
             win_ref[...] += nt(graw, normed)
             gpn = nn(entry_ref[...], graw) + nn(wg_ref[...], ggate_ref[i])
             hat, inverse = norm(mid_ref[i])
@@ -425,11 +429,12 @@
             pgrad_ref[i] = turned.astype(BF)
             rows[pl.ds(i, length, stride=count), :] = turned
 
-    third = pairs // 2
-    for h in range(2):
-        for ref in (grads_ref, mid_ref, normed_ref, ggate_ref, up_ref):
+    parts = 2
+    many = pairs // parts
+    for h in range(parts):
+        for ref in (mid_ref, normed_ref, ggate_ref, up_ref, sig_ref, slope_ref):
             ref.wait(h)
-        pl.loop(h * third, (h + 1) * third, unroll=third)(step)
+        pl.loop(h * many, (h + 1) * many, unroll=many)(step)
 
     send_ref[...] = rows[...].astype(BF)
     gsum_ref[...] = jnp.sum(gacc[...].T, 0, keepdims=True)
@@ -482,13 +487,22 @@
         total[...] += nn(stage[k], r)
 
 
-def weight_kernel(
-    pgradt_ref, outer_ref, win_ref, wgg_ref, wfg_ref, cgain_ref, pgain_ref, bias_ref,
-    out_ref, wacc, wout,
+def row_kernel(
+    pgradt_ref, right_ref, w_ref, outer_ref, win_ref, wgg_ref, wfg_ref, cgain_ref, pgain_ref,
+    bias_ref, grad_ref, out_ref, stage, wacc, wout,
 ):
     count = pgradt_ref.shape[0]
     many = wacc.shape[0]
-    half = out_ref.shape[1] // 4
+    half = right_ref.shape[0]
+    depth = 1.0 / (right_ref.shape[1] * 3 // 4)
+
+    @pl.loop(0, count, unroll=4)
+    def _(i):
+        put(stage, i, nn(w_ref[...], pgradt_ref[i]).astype(BF))
+
+    right_ref.wait()
+    contract(stage, right_ref, grad_ref)
+    grad_ref[...] = grad_ref[...] * depth
     wacc[...] = jnp.zeros_like(wacc)
 
     def step(m):
@@ -496,10 +510,8 @@
         b = jnp.concatenate([pgradt_ref[2 * m], pgradt_ref[2 * m + 1]], 1)
         wacc[...] += nt(a, b)
 
-    third = count // 4
-    for h in range(2):
-        outer_ref.wait(h)
-        pl.loop(h * third, (h + 1) * third, unroll=third)(step)
+    outer_ref.wait()
+    pl.loop(0, count // 2, unroll=3)(step)
 
     for q in range(half):
         wout[pl.ds(q, half, stride=half + 1), :] = wacc[q * half : (q + 1) * half, :]
@@ -515,19 +527,6 @@
     out_ref[at : at + 16, :] = jnp.concatenate(rest, 0).astype(BF)
     at += 16
     out_ref[at:, :] = jnp.zeros((out_ref.shape[0] - at, 128), BF)
-
-
-def outer_back_kernel(pgradt_ref, right_ref, w_ref, grad_ref, stage):
-    count, _, _ = pgradt_ref.shape
-    depth = 1.0 / (right_ref.shape[1] * 3 // 4)
-
-    @pl.loop(0, count, unroll=4)
-    def _(i):
-        put(stage, i, nn(w_ref[...], pgradt_ref[i]).astype(BF))
-
-    right_ref.wait()
-    contract(stage, right_ref, grad_ref)
-    grad_ref[...] = grad_ref[...] * depth
 
 
 def column_kernel(
@@ -663,8 +662,8 @@
         return lax.ppermute(v, "dap", [(i, i ^ 1) for i in range(n)])
 
     own = exchange(right_send, groups=groups)
+    left_send, own = lax.optimization_barrier((left_send, own))
     other = sibling(own)
-    left_send, other = lax.optimization_barrier((left_send, other))
     left_own = exchange(left_send, groups=groups)
     parity = lax.rem(lax.axis_index("dap"), 2).astype(jnp.int32).reshape(1)
 
@@ -677,10 +676,11 @@
     every = ((half, WIDE, WIDE), BF)
     outers = ((count, half * half, WIDE), BF)
     spare = [((length * (half + 1), 128), F32)] * 2
-    edge_send, mid, normed, right, outer = call(
+    sides = ((count, 2 * channels, WIDE), BF)
+    edge_send, mid, normed, sig, slope, right, outer = call(
         14,
         outer_kernel,
-        [((n, pairs, 3, 2 * eight, 128), BF), wide32, wide, every, outers],
+        [((n, pairs, 3, 2 * eight, 128), BF), wide32, wide, sides, sides, every, outers],
         spare + [every, outers],
         parity, own, other, left, edges, qp.T, line(tensor_final_offset),
         line(edge_scaling_factor), entry.T, smem=1, away=2,
@@ -745,9 +745,9 @@
             ((4 * channels, channels), F32), row, row,
         ],
         [((channels, WIDE), F32)] * 2 + [((length * count, channels), F32)],
-        back, mid, normed, grad_gate, up, line(edge_scaling_factor),
-        entry.T, entry, final_sigmoid_matrix,
-        far={0: (2, 1), 1: (2, 0), 2: (2, 0), 3: (2, 0), 4: (2, 0)},
+        back, mid, normed, grad_gate, up, sig, slope, line(edge_scaling_factor),
+        entry, final_sigmoid_matrix,
+        far={**{i: (2, 0) for i in range(1, 7)}, 8: (1, 0)},
     )
     pgrad_cols = exchange(pgrad_send.reshape(n, count * count, channels))
     group = 4
@@ -757,16 +757,13 @@
     full = ((half * half, channels), F32)
     used = half * half + 6 * channels + 3
     each = -(-used // (16 * n)) * 16
-    (weights,) = call(
-        6,
-        weight_kernel,
-        [((each * n, channels), BF)],
-        [full, ((half * (half + 1), channels), F32)],
-        pgradt, outer, tri_in, tri_gate, tri_out, mid_gain, tri_gain, bias,
-        far={1: (2, 0)},
-    )
-    (grad_left,) = call(
-        7, outer_back_kernel, [grads], [stage], pgradt, right, qp, far={1: (1, 0)}
+    grad_left, weights = call(
+        10,
+        row_kernel,
+        [grads, ((each * n, channels), BF)],
+        [stage, full, ((half * (half + 1), channels), F32)],
+        pgradt, right, qp, outer, tri_in, tri_gate, tri_out, mid_gain, tri_gain, bias,
+        far={1: (1, 0), 3: (1, 0)},
     )
     weights, pgrad_cols = lax.optimization_barrier((weights, pgrad_cols))
     mine = exchange(weights.reshape(n, each, channels))

time: 213 us -> 207 us (0.972)
  Pallas kernels: 64.9 us -> 60.8 us
  waiting for transfers between devices: 52.8 us -> 55.1 us
  starting transfers between devices: 28.5 us -> 26.3 us
    pallas_call x13 -> x12, Pallas kernels: 64.9 us -> 60.8 us  [call(): pl.pallas_call(wrapped, out_shape=[pltpu.HBM(s, t) if math.prod(s) > 1310...]
    all_to_all x7, waiting for transfers between devices: 51.9 us -> 55.1 us  [exchange(): lax.all_to_all(v, axes, split_axis=0, concat_axis=0, tiled=True, axis_ind...]
    all_to_all x7, starting transfers between devices: 28.2 us -> 26 us  [exchange(): lax.all_to_all(v, axes, split_axis=0, concat_axis=0, tiled=True, axis_ind...]
    unnamed x45 -> x47, local copies, waits for them, and re-layouts: 4.79 us -> 2.71 us
  transfers between devices with their start and end apart: 9 -> 9, of which waited for: 8 -> 7; matrix products, arithmetic and copies ran while one was open for 1% -> 2% of each run, Pallas kernels for 23% -> 22%
where the time goes in v5:
time: 207 us; the launch traced here: 206 us
  Pallas kernels  60.8 us (29%)
  waiting for transfers between devices  55.1 us (27%)
  blocking collectives  54.5 us (26%)
  starting transfers between devices  26.3 us (13%)
  local copies, waits for them, and re-layouts  8.34 us (4%)
    pallas_call x12, Pallas kernels, call(): pl.pallas_call(wrapped, out_shape=[pltpu.HBM(s, t) if math.prod(s) > 1310...  60.8 us
    all_to_all x7, waiting for transfers between devices, exchange(): lax.all_to_all(v, axes, split_axis=0, concat_axis=0, tiled=True, axis_ind...  55.1 us
    all_to_all x3, blocking collectives, exchange(): lax.all_to_all(v, axes, split_axis=0, concat_axis=0, tiled=True, axis_ind...  54.5 us
    all_to_all x7, starting transfers between devices, exchange(): lax.all_to_all(v, axes, split_axis=0, concat_axis=0, tiled=True, axis_ind...  26 us
  transfers between devices with their start and end apart: 9, of which 7 were waited for; matrix products, arithmetic and copies ran while one was open for 2% of the time, Pallas kernels for 22%

profile of v5, /device:TPU:0, one launch (start us, length us, event | category | flops | bytes accessed | tf_op | source)
XLA Modules:
  0.0 206.2 jit_solution(5194323593936159548)
XLA Ops:
  0.6 1.2 copy.35
  1.9 0.0 copy-start.7
  1.9 0.7 copy-done.7
  2.6 0.7 copy-done.12
  3.2 2.6 %shard_map.211 = (bf16[12,32,256]{2,1,0:T(8,128)(2,1)S(1)}, bf16[8,6,3,32,128]{4,3,2,1,0:T(8,128)(2,1)}, bf16[8,6,3,32,128]{4,3,2,1,0:T(8,128)(2,1)}) custom-call(bf16[6,192,128]{2,1,0:T(8,128)(2,1)S(1)} %bitcast.33, f32[1,64]{1,0:T(1,128)S(1)} %bitcast.42, bf16[64,64]{1,0:T(8,128)(2,1)S(1)} %copy-done.7), custom_call_target="tpu_custom_call" | custom-call | flops 2000000000 | tf_op jit(solution)/shard_map/pallas_call | solution.py:126
  5.8 0.0 copy-start.1
  5.8 0.0 copy-start.22
  5.8 22.9 %all_to_all.50.refs_1_ = bf16[8,6,3,32,128]{4,3,2,1,0:T(8,128)(2,1)S(1)} all-to-all(bf16[8,6,3,32,128]{4,3,2,1,0:T(8,128)(2,1)} %get-tuple-element.66), channel_id=1, replica_groups={{0,2,4,6,8,10,12,14},{1,3,5,7,9,11,13,15},{16,18,20,22,24,26,28,30},{17..., dimensions={0} | all-to-all | bytes 2359296 | tf_op jit(solution)/shard_map/all_to_all | solution.py:617
  28.7 0.0 collective-permute-start
  28.7 0.0 copy-done.1
  28.7 0.1 copy.36
  28.8 1.0 copy.39.refs_5_
  29.8 0.0 copy-done.22
  29.8 0.1 copy.37
  29.9 0.7 copy.38
  30.6 3.7 %all-to-all-start.1 = ((bf16[8,6,3,32,128]{4,3,2,1,0:T(8,128)(2,1)}), bf16[8,6,3,32,128]{4,3,2,1,0:T(8,128)(2,1)S(1)}, u32[]{:S(2)}, u32[]{:S(2)}) async-start(bf16[8,6,3,32,128]{4,3,2,1,0:T(8,128)(2,1)} %get-tuple-element.70), calls=%async_computation.1 | async-start | bytes 2359296 | tf_op jit(solution)/shard_map/all_to_all | solution.py:617
  34.3 0.0 collective-permute-done.refs_2_
  34.3 12.4 %shard_map.212 = (bf16[16,6,3,16,128]{4,3,2,1,0:T(8,128)(2,1)}, f32[12,128,256]{2,1,0:T(8,128)}, bf16[12,128,256]{2,1,0:T(8,128)(2,1)}, bf16[12,256,256]{2,1,0:T...) custom-call(s32[1]{0:T(128)} %bitcast.refs_0_, ...), custom_call_target="tpu_custom_call" | custom-call | flops 14000000000 | tf_op jit(solution)/shard_map/pallas_call | solution.py:126
  46.7 7.2 %all-to-all-done.1.refs_1_ = bf16[8,6,3,32,128]{4,3,2,1,0:T(8,128)(2,1)S(1)} async-done(((bf16[8,6,3,32,128]{4,3,2,1,0:T(8,128)(2,1)}), bf16[8,6,3,32,128]{4,3,2,1,0:T(8,128)(2,1)S(1)}, u32[]{:S(2)}, u32[]{:S(2)}) %all-to-all-start.1) | async-done | bytes 1179680 | tf_op jit(solution)/shard_map/all_to_all | solution.py:617
  53.9 3.8 %all-to-all-start.2 = ((bf16[16,6,3,16,128]{4,3,2,1,0:T(8,128)(2,1)}), bf16[16,6,3,16,128]{4,3,2,1,0:T(8,128)(2,1)S(1)}, u32[]{:S(2)}, u32[]{:S(2)}) async-start(bf16[16,6,3,16,128]{4,3,2,1,0:T(8,128)(2,1)} %get-tuple-element.71), calls=%async_computation.2 | async-start | bytes 2359296 | tf_op jit(solution)/shard_map/all_to_all | solution.py:617
  57.7 1.1 copy-done.16
  58.9 4.0 %shard_map.214 = (f32[12,128,256]{2,1,0:T(8,128)}, bf16[12,128,256]{2,1,0:T(8,128)(2,1)}) custom-call(bf16[12,128,256]{2,1,0:T(8,128)(2,1)S(1)} %copy-done.16, bf16[12,192,128]{2,1,0:T(8,128)(2,1)S(1)} %bitcast.36, bf16[128,128]{1,0:T(8,128)(2,1)S(1)} %copy-done.5), custom_call_target="tpu_custom_call" | custom-call | flops 3000000000 | tf_op jit(solution)/shard_map/pallas_call | solution.py:126
  62.9 12.6 %all-to-all-done.2.refs_0_ = bf16[16,6,3,16,128]{4,3,2,1,0:T(8,128)(2,1)S(1)} async-done(((bf16[16,6,3,16,128]{4,3,2,1,0:T(8,128)(2,1)}), bf16[16,6,3,16,128]{4,3,2,1,0:T(8,128)(2,1)S(1)}, u32[]{:S(2)}, u32[]{:S(2)}) %all-to-all-start.2) | async-done | bytes 1179680 | tf_op jit(solution)/shard_map/all_to_all | solution.py:617
  75.6 2.7 %shard_map.213 = (bf16[16,3,3,16,128]{4,3,2,1,0:T(8,128)(2,1)}, bf16[8,192,256]{2,1,0:T(8,128)(2,1)}, bf16[8,192,256]{2,1,0:T(8,128)(2,1)}) custom-call(bf16[16,6,3,16,128]{4,3,2,1,0:T(8,128)(2,1)S(1)} %all-to-all-done.2.refs_0_), custom_call_target="tpu_custom_call" | custom-call | flops 3000000000 | tf_op jit(solution)/shard_map/pallas_call | solution.py:126
  78.3 0.0 copy-start.4
  78.3 0.0 copy-start.10
  78.3 0.0 copy-start.15
  78.4 15.2 %all_to_all.51.refs_0_ = bf16[16,3,3,16,128]{4,3,2,1,0:T(8,128)(2,1)S(1)} all-to-all(bf16[16,3,3,16,128]{4,3,2,1,0:T(8,128)(2,1)} %get-tuple-element.76), channel_id=1, replica_groups=mesh['dp'=8,'dap'=16] {'dap'}, dimensions={0} | all-to-all | bytes 1179648 | tf_op jit(solution)/shard_map/all_to_all | solution.py:617
  93.6 0.0 copy-done.4
  93.6 0.0 copy-done.15
  93.6 2.1 %shard_map.216 = bf16[16,3,3,16,128]{4,3,2,1,0:T(8,128)(2,1)} custom-call(bf16[16,3,3,16,128]{4,3,2,1,0:T(8,128)(2,1)S(1)} %all_to_all.51.refs_0_, f32[12,128,256]{2,1,0:T(8,128)S(1)} %copy-done.14, bf16[12,128,256]{2,1,0:T(8,128)(2,1)S(1)} %copy-done.15, f32[1,128]{1,0:T(1,128)S(1)} %bitcast.38, bf16[128,128]{1,0:T(8,128)(2,1)S(1)} %copy-done.4), custom_call_target="tpu_custom_call" | custom-call | flops 2000000000 | tf_op jit(solution)/shard_map/pallas_call | solution.py:126
  95.7 3.7 %all-to-all-start.4 = ((bf16[16,3,3,16,128]{4,3,2,1,0:T(8,128)(2,1)}), bf16[16,3,3,16,128]{4,3,2,1,0:T(8,128)(2,1)S(1)}, u32[]{:S(2)}, u32[]{:S(2)}) async-start(bf16[16,3,3,16,128]{4,3,2,1,0:T(8,128)(2,1)} %shard_map.216), calls=%async_computation.4 | async-start | bytes 1179648 | tf_op jit(solution)/shard_map/all_to_all | solution.py:617
  99.5 0.3 collective-permute-start.1
  99.8 0.8 copy.40.refs_8_
  100.5 10.5 %all-to-all-done.4.refs_0_ = bf16[16,3,3,16,128]{4,3,2,1,0:T(8,128)(2,1)S(1)} async-done(((bf16[16,3,3,16,128]{4,3,2,1,0:T(8,128)(2,1)}), bf16[16,3,3,16,128]{4,3,2,1,0:T(8,128)(2,1)S(1)}, u32[]{:S(2)}, u32[]{:S(2)}) %all-to-all-start.4) | async-done | bytes 589856 | tf_op jit(solution)/shard_map/all_to_all | solution.py:617
  111.0 3.5 %shard_map.217 = bf16[16,6,3,16,128]{4,3,2,1,0:T(8,128)(2,1)} custom-call(bf16[16,3,3,16,128]{4,3,2,1,0:T(8,128)(2,1)S(1)} %all-to-all-done.4.refs_0_, bf16[8,192,256]{2,1,0:T(8,128)(2,1)} %get-tuple-element.81.refs_1_, bf16[8,192,256]{2,1,0:T(8,128)(2,1)} %get-tuple-element.82.refs_2_), custom_call_target="tpu_custom_call" | custom-call | flops 4000000000 | tf_op jit(solution)/shard_map/pallas_call | solution.py:126
  114.5 3.7 %all-to-all-start.5 = ((bf16[16,6,3,16,128]{4,3,2,1,0:T(8,128)(2,1)}), bf16[16,6,3,16,128]{4,3,2,1,0:T(8,128)(2,1)S(1)}, u32[]{:S(2)}, u32[]{:S(2)}) async-start(bf16[16,6,3,16,128]{4,3,2,1,0:T(8,128)(2,1)} %shard_map.217), calls=%async_computation.5 | async-start | bytes 2359296 | tf_op jit(solution)/shard_map/all_to_all | solution.py:617
  118.2 6.6 %shard_map.215 = (bf16[12,192,128]{2,1,0:T(8,128)(2,1)}, bf16[12,128,256]{2,1,0:T(8,128)(2,1)}, f32[128,128]{1,0:T(8,128)S(1)}, f32[128,128]{1,0:T(8,128)S(1)}, f32[1,128]{1,0:T(1,128)S(1)}) custom-call(bf16[16,3,3,16,128]{4,3,2,1,0:T(8,128)(2,1)} %copy-done, f32[12,128,256]{2,1,0:T(8,128)} %get-tuple-element.77.refs_1_, ...), custom_call_target="tpu_custom_call" | custom-call | flops 6000000000 | tf_op jit(solution)/shard_map/pallas_call | solution.py:126
  124.8 0.0 copy-start.6
  124.8 0.0 collective-permute-done.1.refs_2_
  124.9 6.2 %shard_map.220 = (bf16[32,256,256]{2,1,0:T(8,128)(2,1)}, f32[12,64,256]{2,1,0:T(8,128)}, f32[12,1,256]{2,1,0:T(1,128)S(1)}) custom-call(s32[1]{0:T(128)} %bitcast.refs_0_, bf16[8,6,3,32,128]{4,3,2,1,0:T(8,128)(2,1)S(1)} %all-to-all-done.1.refs_1_, bf16[8,6,3,32,128]{4,3,2,1,0:T(8,128)(2,1)} %collective-permute-done.1.refs_2_, bf16[6,192,128]{2,1,0:T(8,128)(2,1)S(1)} %bitcast.34), custom_call_target="tpu_custom_call" | custom-call | flops 6000000000 | tf_op jit(solution)/shard_map/pallas_call | solution.py:126
  131.1 4.9 %all-to-all-done.5.refs_0_ = bf16[16,6,3,16,128]{4,3,2,1,0:T(8,128)(2,1)S(1)} async-done(((bf16[16,6,3,16,128]{4,3,2,1,0:T(8,128)(2,1)}), bf16[16,6,3,16,128]{4,3,2,1,0:T(8,128)(2,1)S(1)}, u32[]{:S(2)}, u32[]{:S(2)}) %all-to-all-start.5) | async-done | bytes 1179680 | tf_op jit(solution)/shard_map/all_to_all | solution.py:617
  136.0 5.8 %shard_map.218 = (bf16[12,192,128]{2,1,0:T(8,128)(2,1)}, bf16[12,128,256]{2,1,0:T(8,128)(2,1)}, bf16[2304,128]{1,0:T(8,128)(2,1)}, f32[512,128]{1,0:T(8,128)S(1)...) custom-call(bf16[16,6,3,16,128]{4,3,2,1,0:T(8,128)(2,1)S(1)} %all-to-all-done.5.refs_0_, ...), custom_call_target="tpu_custom_call" | custom-call | flops 8999999488 | tf_op jit(solution)/shard_map/pallas_call | solution.py:126
  141.9 3.9 %all-to-all-start.6 = ((bf16[16,144,128]{2,1,0:T(8,128)(2,1)}), bf16[16,144,128]{2,1,0:T(8,128)(2,1)S(1)}, u32[]{:S(2)}, u32[]{:S(2)}) async-start(bf16[16,144,128]{2,1,0:T(8,128)(2,1)} %bitcast.45), calls=%async_computation.6 | async-start | bytes 1179648 | tf_op jit(solution)/shard_map/all_to_all | solution.py:617
  145.8 0.0 copy-start.2
  145.8 0.0 copy-start.8
  145.8 0.0 copy-start.13
  145.8 7.3 %shard_map.219 = (f32[384,256]{1,0:T(8,128)S(1)}, bf16[2048,128]{1,0:T(8,128)(2,1)}) custom-call(bf16[12,128,256]{2,1,0:T(8,128)(2,1)S(1)} %copy-done.17, bf16[32,256,256]{2,1,0:T(8,128)(2,1)} %get-tuple-element.88.refs_1_, bf16[1024,128]{1,0:T(8,128)(2,1)S(1)} %bitcast.32, bf16[12,1024,256]{2,1,0:T(8,128)(2,1)} %get-tuple-element.89.refs_3_, ...), custom_call_target="tpu_custom_call" | custom-call | flops 10000000000 | tf_op jit(solution)/shard_map/pallas_call | solution.py:126
  153.1 0.0 copy-start.18
  153.1 4.0 %all-to-all-done.6.refs_0_ = bf16[16,144,128]{2,1,0:T(8,128)(2,1)S(1)} async-done(((bf16[16,144,128]{2,1,0:T(8,128)(2,1)}), bf16[16,144,128]{2,1,0:T(8,128)(2,1)S(1)}, u32[]{:S(2)}, u32[]{:S(2)}) %all-to-all-start.6) | async-done | bytes 589856 | tf_op jit(solution)/shard_map/all_to_all | solution.py:617
  157.1 3.6 %all-to-all-start.7 = ((bf16[16,128,128]{2,1,0:T(8,128)(2,1)}), bf16[16,128,128]{2,1,0:T(8,128)(2,1)S(1)}, u32[]{:S(2)}, u32[]{:S(2)}) async-start(bf16[16,128,128]{2,1,0:T(8,128)(2,1)} %bitcast.46), calls=%async_computation.7 | async-start | bytes 1048576 | tf_op jit(solution)/shard_map/all_to_all | solution.py:617
  160.7 0.0 copy-done.18
  160.7 0.0 copy-done.2
  160.7 0.0 copy-done.8
  160.8 0.0 copy-done.13
  160.8 6.2 %shard_map.221 = (bf16[6,192,128]{2,1,0:T(8,128)(2,1)}, bf16[32,128]{1,0:T(8,128)(2,1)S(1)}) custom-call(bf16[16,144,128]{2,1,0:T(8,128)(2,1)S(1)} %all-to-all-done.6.refs_0_, bf16[32,256,256]{2,1,0:T(8,128)(2,1)} %get-tuple-element.102.refs_1_, bf16[1024,128]{1,0:T(8,128)(2,1)S(1)} %copy-done.2, f32[384,256]{1,0:T(8,128)} %copy-done.18, ...), custom_call_target="tpu_custom_call" | custom-call | flops 8999999488 | tf_op jit(solution)/shard_map/pallas_call | solution.py:126
  167.0 4.6 %all-to-all-done.7 = bf16[16,128,128]{2,1,0:T(8,128)(2,1)S(1)} async-done(((bf16[16,128,128]{2,1,0:T(8,128)(2,1)}), bf16[16,128,128]{2,1,0:T(8,128)(2,1)S(1)}, u32[]{:S(2)}, u32[]{:S(2)}) %all-to-all-start.7) | async-done | bytes 524320 | tf_op jit(solution)/shard_map/all_to_all | solution.py:617
  171.5 0.1 reduce_sum.24
  171.7 16.4 %all_to_all.52 = bf16[8,160,128]{2,1,0:T(8,128)(2,1)S(1)} all-to-all(bf16[8,160,128]{2,1,0:T(8,128)(2,1)S(1)} %broadcast_in_dim.14), channel_id=1, replica_groups=mesh['dp'=8,'dap'=16] {'dp'}, dimensions={0} | all-to-all | bytes 655360 | tf_op jit(solution)/shard_map/all_to_all | solution.py:617
  188.2 0.9 broadcast_in_dim.15
  189.1 3.6 %all-to-all-start.9 = ((bf16[16,160,128]{2,1,0:T(8,128)(2,1)}), bf16[16,160,128]{2,1,0:T(8,128)(2,1)S(1)}, u32[]{:S(2)}, u32[]{:S(2)}) async-start(bf16[16,160,128]{2,1,0:T(8,128)(2,1)} %broadcast_in_dim.15), calls=%async_computation.9 | async-start | bytes 1310720 | tf_op jit(solution)/shard_map/all_to_all | solution.py:617
  192.7 0.9 copy.41
  193.6 11.3 %all-to-all-done.9.refs_0_ = bf16[16,160,128]{2,1,0:T(8,128)(2,1)S(1)} async-done(((bf16[16,160,128]{2,1,0:T(8,128)(2,1)}), bf16[16,160,128]{2,1,0:T(8,128)(2,1)S(1)}, u32[]{:S(2)}, u32[]{:S(2)}) %all-to-all-start.9) | async-done | bytes 655392 | tf_op jit(solution)/shard_map/all_to_all | solution.py:617
  204.9 1.3 shard_map.222
  (27 shorter events, 0.1 us)
Async XLA Ops:
  1.9 0.7 copy-start.7
  2.6 0.7 copy-start.12
  5.8 22.9 %copy-start.1 = (bf16[1024,128]{1,0:T(8,128)(2,1)S(1)}, bf16[1024,128]{1,0:T(8,128)(2,1)}, u32[]{:S(2)}) copy-start(bf16[1024,128]{1,0:T(8,128)(2,1)} %refs_2_.6) | copy-start | bytes 786436
  5.8 24.0 %copy-start.22 = (bf16[128,512]{1,0:T(8,128)(2,1)S(1)}, bf16[128,512]{1,0:T(8,128)(2,1)}, u32[]{:S(2)}) copy-start(bf16[128,512]{1,0:T(8,128)(2,1)} %param.20) | copy-start | bytes 393220
  28.7 1.9 copy-start.19
  28.7 5.6 %collective-permute-start = (bf16[8,6,3,32,128]{4,3,2,1,0:T(8,128)(2,1)S(1)}, bf16[8,6,3,32,128]{4,3,2,1,0:T(8,128)(2,1)}, u32[]{:S(2)}, u32[]{:S(2)}) collective-permute-start(bf16[8,6,3,32,128]{4,3,2,1,0:T(8,128)(2,1)S(1)} %all_to_all.50.refs_1_), channel_id=1, source_target_pairs={{0,1},{1,0},{2,3},{3,2},{4,5},{5,4},{6,7},{7,6},{8,9},{9,8},{10,11... | collective-permute-start | bytes 3538952 | tf_op jit(solution)/shard_map/ppermute | solution.py:662
  30.6 3.7 %copy-start.9 = (f32[128]{0:T(128)S(1)}, f32[128]{0:T(128)}, u32[]{:S(2)}) copy-start(f32[128]{0:T(128)} %param.18) | copy-start | bytes 1540
  30.6 3.7 %copy-start.11 = (f32[128]{0:T(128)S(1)}, f32[128]{0:T(128)}, u32[]{:S(2)}) copy-start(f32[128]{0:T(128)} %param.19) | copy-start | bytes 1540
  30.6 23.3 %all-to-all-start.1 = ((bf16[8,6,3,32,128]{4,3,2,1,0:T(8,128)(2,1)}), bf16[8,6,3,32,128]{4,3,2,1,0:T(8,128)(2,1)S(1)}, u32[]{:S(2)}, u32[]{:S(2)}) async-start(bf16[8,6,3,32,128]{4,3,2,1,0:T(8,128)(2,1)} %get-tuple-element.70), calls=%async_computation.1 | async-start | bytes 2359296 | tf_op jit(solution)/shard_map/all_to_all | solution.py:617
  53.9 3.8 %copy-start.3 = (bf16[1,12,192,128]{3,2,1,0:T(8,128)(2,1)S(1)}, bf16[1,12,192,128]{3,2,1,0:T(8,128)(2,1)}, u32[]{:S(2)}) copy-start(bf16[1,12,192,128]{3,2,1,0:T(8,128)(2,1)} %param.14) | copy-start | bytes 1769476
  53.9 3.9 %copy-start.5 = (bf16[128,128]{1,0:T(8,128)(2,1)S(1)}, bf16[128,128]{1,0:T(8,128)(2,1)}, u32[]{:S(2)}) copy-start(bf16[128,128]{1,0:T(8,128)(2,1)} %refs_9_.1) | copy-start | bytes 98308
  53.9 21.7 %all-to-all-start.2 = ((bf16[16,6,3,16,128]{4,3,2,1,0:T(8,128)(2,1)}), bf16[16,6,3,16,128]{4,3,2,1,0:T(8,128)(2,1)S(1)}, u32[]{:S(2)}, u32[]{:S(2)}) async-start(bf16[16,6,3,16,128]{4,3,2,1,0:T(8,128)(2,1)} %get-tuple-element.71), calls=%async_computation.2 | async-start | bytes 2359296 | tf_op jit(solution)/shard_map/all_to_all | solution.py:617
  57.7 1.1 copy-start.16
  75.6 18.0 %copy-start.14 = (f32[12,128,256]{2,1,0:T(8,128)S(1)}, f32[12,128,256]{2,1,0:T(8,128)}, u32[]{:S(2)}) copy-start(f32[12,128,256]{2,1,0:T(8,128)} %get-tuple-element.78.refs_3_.refs_1_) | copy-start | bytes 4718596
  78.3 15.3 %copy-start.4 = (bf16[128,128]{1,0:T(8,128)(2,1)S(1)}, bf16[128,128]{1,0:T(8,128)(2,1)}, u32[]{:S(2)}) copy-start(bf16[128,128]{1,0:T(8,128)(2,1)} %refs_4_.1) | copy-start | bytes 98308
  78.3 15.3 %copy-start.10 = (f32[128]{0:T(128)S(1)}, f32[128]{0:T(128)}, u32[]{:S(2)}) copy-start(f32[128]{0:T(128)} %param.22) | copy-start | bytes 1540
  78.3 15.3 %copy-start.15 = (bf16[12,128,256]{2,1,0:T(8,128)(2,1)S(1)}, bf16[12,128,256]{2,1,0:T(8,128)(2,1)}, u32[]{:S(2)}) copy-start(bf16[12,128,256]{2,1,0:T(8,128)(2,1)} %get-tuple-element.79.refs_4_.refs_2_) | copy-start | bytes 2359300
  93.6 2.1 %copy-start = (bf16[16,3,3,16,128]{4,3,2,1,0:T(8,128)(2,1)}, bf16[16,3,3,16,128]{4,3,2,1,0:T(8,128)(2,1)S(1)}, u32[]{:S(2)}) copy-start(bf16[16,3,3,16,128]{4,3,2,1,0:T(8,128)(2,1)S(1)} %all_to_all.51.refs_0_) | copy-start | bytes 1769476
  95.7 4.0 %copy-start.20 = (bf16[128,2,16,2,8]{0,4,3,2,1:T(8,128)(2,1)S(1)}, bf16[128,2,16,2,8]{0,4,3,2,1:T(8,128)(2,1)}, u32[]{:S(2)}) copy-start(bf16[128,2,16,2,8]{0,4,3,2,1:T(8,128)(2,1)} %copy.38) | copy-start | bytes 393220
  95.7 15.2 %all-to-all-start.4 = ((bf16[16,3,3,16,128]{4,3,2,1,0:T(8,128)(2,1)}), bf16[16,3,3,16,128]{4,3,2,1,0:T(8,128)(2,1)S(1)}, u32[]{:S(2)}, u32[]{:S(2)}) async-start(bf16[16,3,3,16,128]{4,3,2,1,0:T(8,128)(2,1)} %shard_map.216), calls=%async_computation.4 | async-start | bytes 1179648 | tf_op jit(solution)/shard_map/all_to_all | solution.py:617
  99.5 25.4 %collective-permute-start.1 = (bf16[8,6,3,32,128]{4,3,2,1,0:T(8,128)(2,1)S(1)}, bf16[8,6,3,32,128]{4,3,2,1,0:T(8,128)(2,1)}, u32[]{:S(2)}, u32[]{:S(2)}) collective-permute-start(bf16[8,6,3,32,128]{4,3,2,1,0:T(8,128)(2,1)S(1)} %all-to-all-done.1.refs_1_), channel_id=1, source_target_pairs={{0,1},{1,0},{2,3},{3,2},{4,5},{5,4},{6,7},{7,6},{8,9},{9,8},{10,11... | collective-permute-start | bytes 3538952 | tf_op jit(solution)/shard_map/ppermute | solution.py:662
  114.5 21.6 %all-to-all-start.5 = ((bf16[16,6,3,16,128]{4,3,2,1,0:T(8,128)(2,1)}), bf16[16,6,3,16,128]{4,3,2,1,0:T(8,128)(2,1)S(1)}, u32[]{:S(2)}, u32[]{:S(2)}) async-start(bf16[16,6,3,16,128]{4,3,2,1,0:T(8,128)(2,1)} %shard_map.217), calls=%async_computation.5 | async-start | bytes 2359296 | tf_op jit(solution)/shard_map/all_to_all | solution.py:617
  124.8 11.2 %copy-start.6 = (bf16[128,128]{1,0:T(8,128)(2,1)S(1)}, bf16[128,128]{1,0:T(8,128)(2,1)}, u32[]{:S(2)}) copy-start(bf16[128,128]{1,0:T(8,128)(2,1)} %refs_9_.1) | copy-start | bytes 98308
  141.9 3.9 %copy-start.17 = (bf16[12,128,256]{2,1,0:T(8,128)(2,1)S(1)}, bf16[12,128,256]{2,1,0:T(8,128)(2,1)}, u32[]{:S(2)}) copy-start(bf16[12,128,256]{2,1,0:T(8,128)(2,1)} %get-tuple-element.87.refs_0_) | copy-start | bytes 2359300
  141.9 15.3 %all-to-all-start.6 = ((bf16[16,144,128]{2,1,0:T(8,128)(2,1)}), bf16[16,144,128]{2,1,0:T(8,128)(2,1)S(1)}, u32[]{:S(2)}, u32[]{:S(2)}) async-start(bf16[16,144,128]{2,1,0:T(8,128)(2,1)} %bitcast.45), calls=%async_computation.6 | async-start | bytes 1179648 | tf_op jit(solution)/shard_map/all_to_all | solution.py:617
  145.8 14.9 %copy-start.2 = (bf16[1024,128]{1,0:T(8,128)(2,1)S(1)}, bf16[1024,128]{1,0:T(8,128)(2,1)}, u32[]{:S(2)}) copy-start(bf16[1024,128]{1,0:T(8,128)(2,1)} %refs_2_.6) | copy-start | bytes 786436
  145.8 14.9 %copy-start.8 = (bf16[64,64]{1,0:T(8,128)(2,1)S(1)}, bf16[64,64]{1,0:T(8,128)(2,1)}, u32[]{:S(2)}) copy-start(bf16[64,64]{1,0:T(8,128)(2,1)} %refs_2_.7) | copy-start | bytes 24580
  145.8 14.9 %copy-start.13 = (f32[64]{0:T(128)S(1)}, f32[64]{0:T(128)}, u32[]{:S(2)}) copy-start(f32[64]{0:T(128)} %param.15) | copy-start | bytes 772
  153.1 7.6 %copy-start.18 = (f32[384,256]{1,0:T(8,128)}, f32[384,256]{1,0:T(8,128)S(1)}, u32[]{:S(2)}) copy-start(f32[384,256]{1,0:T(8,128)S(1)} %get-tuple-element.103.refs_3_) | copy-start | bytes 1179652
  157.1 14.4 %all-to-all-start.7 = ((bf16[16,128,128]{2,1,0:T(8,128)(2,1)}), bf16[16,128,128]{2,1,0:T(8,128)(2,1)S(1)}, u32[]{:S(2)}, u32[]{:S(2)}) async-start(bf16[16,128,128]{2,1,0:T(8,128)(2,1)} %bitcast.46), calls=%async_computation.7 | async-start | bytes 1048576 | tf_op jit(solution)/shard_map/all_to_all | solution.py:617
  188.1 4.6 %copy-start.21 = (bf16[6,192,128]{2,1,0:T(8,128)(2,1)S(1)}, bf16[6,192,128]{2,1,0:T(8,128)(2,1)}, u32[]{:S(2)}) copy-start(bf16[6,192,128]{2,1,0:T(8,128)(2,1)} %get-tuple-element.106) | copy-start | bytes 884740
  189.1 15.8 %all-to-all-start.9 = ((bf16[16,160,128]{2,1,0:T(8,128)(2,1)}), bf16[16,160,128]{2,1,0:T(8,128)(2,1)S(1)}, u32[]{:S(2)}, u32[]{:S(2)}) async-start(bf16[16,160,128]{2,1,0:T(8,128)(2,1)} %broadcast_in_dim.15), calls=%async_computation.9 | async-start | bytes 1310720 | tf_op jit(solution)/shard_map/all_to_all | solution.py:617

commit v6 on v5

--- a/solution.py
+++ b/solution.py
@@ -192,9 +192,9 @@
 
 
 def outer_kernel(
-    par_ref, own_ref, other_ref, left_ref, edge_ref, wt_ref, bias_ref, gain_ref, entry_ref,
-    send_ref, mid_ref, normed_ref, sig_ref, slope_ref, right_out, outer_out,
-    head, tail, right_ref, outer_ref, sems,
+    par_ref, own_ref, other_ref, left_ref, edge_ref, w_ref, bias_ref, gain_ref, entry_ref,
+    send_ref, mid_ref, normed_ref, sig_ref, slope_ref, hat_ref, inv_ref, right_out, outer_out,
+    head, tail, right_ref, outer_ref, wt_ref, sems,
 ):
     chips, pairs, _, half, _ = own_ref.shape
     rows = left_ref.shape[0]
@@ -229,8 +229,9 @@
     devices, _, _, sixteen, _ = send_ref.shape
     bias = as_column(bias_ref)
     gain = as_column(gain_ref)
-    for ref in (edge_ref, wt_ref, entry_ref):
+    for ref in (edge_ref, w_ref, entry_ref):
         ref.wait()
+    wt_ref[...] = w_ref[...].astype(F32).T.astype(BF)
 
     @pl.loop(0, pairs, unroll=3)
     def _(m):
@@ -239,7 +240,9 @@
             i = 2 * m + o
             mid = flip(edge_ref[i].astype(F32)) + (nn(wt_ref[...], outer_ref[i]) + bias)
             mid_ref[i] = mid
-            hat, _ = norm(mid)
+            hat, inverse = norm(mid)
+            hat_ref[i] = hat
+            inv_ref[i] = inverse
             normed = (hat * gain).astype(BF)
             normed_ref[i] = normed
             raw = nn(entry_ref[...], normed)
@@ -399,7 +402,7 @@
 
 
 def edge_back_kernel(
-    grads_ref, mid_ref, normed_ref, ggate_ref, up_ref, sig_ref, slope_ref, gain_ref, entry_ref, wg_ref,
+    grads_ref, hat_ref, normed_ref, ggate_ref, up_ref, sig_ref, slope_ref, gain_ref, entry_ref, wg_ref, inv_ref,
     pgrad_ref, pgradt_ref, send_ref, win_ref, gsum_ref, bsum_ref, gacc, bacc, rows,
 ):
     devices, pairs, _, sixteen, _ = grads_ref.shape
@@ -420,7 +423,7 @@
             graw = jnp.concatenate([grad * slope, grad * sig], 0).astype(BF)
             win_ref[...] += nt(graw, normed)
             gpn = nn(entry_ref[...], graw) + nn(wg_ref[...], ggate_ref[i])
-            hat, inverse = norm(mid_ref[i])
+            hat, inverse = hat_ref[i], inv_ref[i]
             gacc[...] += gpn * hat
             gmid = up_ref[i].astype(F32) + norm_back(gpn * gain, hat, inverse)
             bacc[...] += gmid
@@ -432,7 +435,7 @@
     parts = 2
     many = pairs // parts
     for h in range(parts):
-        for ref in (mid_ref, normed_ref, ggate_ref, up_ref, sig_ref, slope_ref):
+        for ref in (hat_ref, normed_ref, ggate_ref, up_ref, sig_ref, slope_ref):
             ref.wait(h)
         pl.loop(h * many, (h + 1) * many, unroll=many)(step)
 
@@ -677,12 +680,12 @@
     outers = ((count, half * half, WIDE), BF)
     spare = [((length * (half + 1), 128), F32)] * 2
     sides = ((count, 2 * channels, WIDE), BF)
-    edge_send, mid, normed, sig, slope, right, outer = call(
+    edge_send, mid, normed, sig, slope, pair_hat, pair_inv, right, outer = call(
         14,
         outer_kernel,
-        [((n, pairs, 3, 2 * eight, 128), BF), wide32, wide, sides, sides, every, outers],
-        spare + [every, outers],
-        parity, own, other, left, edges, qp.T, line(tensor_final_offset),
+        [((n, pairs, 3, 2 * eight, 128), BF), wide32, wide, sides, sides, wide32, ((count, 1, WIDE), F32), every, outers],
+        spare + [every, outers, ((channels, half * half), BF)],
+        parity, own, other, left, edges, qp, line(tensor_final_offset),
         line(edge_scaling_factor), entry.T, smem=1, away=2,
         far={1: (1, 0), 2: (1, 0), 4: (1, 0), 5: (1, 0), 8: (1, 0)},
     )
@@ -745,8 +748,8 @@
             ((4 * channels, channels), F32), row, row,
         ],
         [((channels, WIDE), F32)] * 2 + [((length * count, channels), F32)],
-        back, mid, normed, grad_gate, up, sig, slope, line(edge_scaling_factor),
-        entry, final_sigmoid_matrix,
+        back, pair_hat, normed, grad_gate, up, sig, slope, line(edge_scaling_factor),
+        entry, final_sigmoid_matrix, pair_inv,
         far={**{i: (2, 0) for i in range(1, 7)}, 8: (1, 0)},
     )
     pgrad_cols = exchange(pgrad_send.reshape(n, count * count, channels))

time: 207 us -> 207 us (level)
  waiting for transfers between devices: 55.1 us -> 52.9 us
    all_to_all x7, waiting for transfers between devices: 55.1 us -> 52.9 us  [exchange(): lax.all_to_all(v, axes, split_axis=0, concat_axis=0, tiled=True, axis_ind...]
  transfers between devices with their start and end apart: 9 -> 9, of which waited for: 7 -> 7; matrix products, arithmetic and copies ran while one was open for 2% -> 2% of each run, Pallas kernels for 22% -> 23%
where the time goes in v6:
time: 207 us; the launch traced here: 206 us
  Pallas kernels  61.6 us (30%)
  blocking collectives  54.5 us (26%)
  waiting for transfers between devices  52.9 us (26%)
  starting transfers between devices  26.3 us (13%)
  local copies, waits for them, and re-layouts  9.51 us (5%)
    pallas_call x12, Pallas kernels, call(): pl.pallas_call(wrapped, out_shape=[pltpu.HBM(s, t) if math.prod(s) > 1310...  61.6 us
    all_to_all x3, blocking collectives, exchange(): lax.all_to_all(v, axes, split_axis=0, concat_axis=0, tiled=True, axis_ind...  54.5 us
    all_to_all x7, waiting for transfers between devices, exchange(): lax.all_to_all(v, axes, split_axis=0, concat_axis=0, tiled=True, axis_ind...  52.9 us
    all_to_all x7, starting transfers between devices, exchange(): lax.all_to_all(v, axes, split_axis=0, concat_axis=0, tiled=True, axis_ind...  26 us
  transfers between devices with their start and end apart: 9, of which 7 were waited for; matrix products, arithmetic and copies ran while one was open for 2% of the time, Pallas kernels for 23%

profile of v6, /device:TPU:0, one launch (start us, length us, event | category | flops | bytes accessed | tf_op | source)
XLA Modules:
  0.0 206.0 jit_solution(3324264859557913413)
XLA Ops:
  0.6 1.2 copy.33
  1.9 0.0 copy-start.7
  1.9 0.7 copy-done.7
  2.6 0.7 copy-done.12
  3.2 2.6 %shard_map.211 = (bf16[12,32,256]{2,1,0:T(8,128)(2,1)S(1)}, bf16[8,6,3,32,128]{4,3,2,1,0:T(8,128)(2,1)}, bf16[8,6,3,32,128]{4,3,2,1,0:T(8,128)(2,1)}) custom-call(bf16[6,192,128]{2,1,0:T(8,128)(2,1)S(1)} %bitcast.29, f32[1,64]{1,0:T(1,128)S(1)} %bitcast.40, bf16[64,64]{1,0:T(8,128)(2,1)S(1)} %copy-done.7), custom_call_target="tpu_custom_call" | custom-call | flops 2000000000 | tf_op jit(solution)/shard_map/pallas_call | solution.py:126
  5.9 0.0 copy-start.1
  5.9 0.0 copy-start.24
  5.9 22.9 %all_to_all.50.refs_1_ = bf16[8,6,3,32,128]{4,3,2,1,0:T(8,128)(2,1)S(1)} all-to-all(bf16[8,6,3,32,128]{4,3,2,1,0:T(8,128)(2,1)} %get-tuple-element.68), channel_id=1, replica_groups={{0,2,4,6,8,10,12,14},{1,3,5,7,9,11,13,15},{16,18,20,22,24,26,28,30},{17..., dimensions={0} | all-to-all | bytes 2359296 | tf_op jit(solution)/shard_map/all_to_all | solution.py:620
  28.8 0.0 collective-permute-start
  28.8 0.0 copy-done.1
  28.8 0.9 copy.34
  29.7 0.0 copy-done.24
  29.7 0.1 copy.35
  29.8 0.7 copy.36
  30.5 3.7 %all-to-all-start.1 = ((bf16[8,6,3,32,128]{4,3,2,1,0:T(8,128)(2,1)}), bf16[8,6,3,32,128]{4,3,2,1,0:T(8,128)(2,1)S(1)}, u32[]{:S(2)}, u32[]{:S(2)}) async-start(bf16[8,6,3,32,128]{4,3,2,1,0:T(8,128)(2,1)} %get-tuple-element.72), calls=%async_computation.1 | async-start | bytes 2359296 | tf_op jit(solution)/shard_map/all_to_all | solution.py:620
  34.2 0.0 collective-permute-done.refs_2_
  34.2 13.4 %shard_map.212 = (bf16[16,6,3,16,128]{4,3,2,1,0:T(8,128)(2,1)}, f32[12,128,256]{2,1,0:T(8,128)}, bf16[12,128,256]{2,1,0:T(8,128)(2,1)}, bf16[12,256,256]{2,1,0:T...) custom-call(s32[1]{0:T(128)} %bitcast.refs_0_, ...), custom_call_target="tpu_custom_call" | custom-call | flops 14000000000 | tf_op jit(solution)/shard_map/pallas_call | solution.py:126
  47.6 0.0 copy-start.19
  47.7 0.6 copy-done.19
  48.2 5.6 %all-to-all-done.1.refs_1_ = bf16[8,6,3,32,128]{4,3,2,1,0:T(8,128)(2,1)S(1)} async-done(((bf16[8,6,3,32,128]{4,3,2,1,0:T(8,128)(2,1)}), bf16[8,6,3,32,128]{4,3,2,1,0:T(8,128)(2,1)S(1)}, u32[]{:S(2)}, u32[]{:S(2)}) %all-to-all-start.1) | async-done | bytes 1179680 | tf_op jit(solution)/shard_map/all_to_all | solution.py:620
  53.9 3.8 %all-to-all-start.2 = ((bf16[16,6,3,16,128]{4,3,2,1,0:T(8,128)(2,1)}), bf16[16,6,3,16,128]{4,3,2,1,0:T(8,128)(2,1)S(1)}, u32[]{:S(2)}, u32[]{:S(2)}) async-start(bf16[16,6,3,16,128]{4,3,2,1,0:T(8,128)(2,1)} %get-tuple-element.73), calls=%async_computation.2 | async-start | bytes 2359296 | tf_op jit(solution)/shard_map/all_to_all | solution.py:620
  57.7 0.0 copy-done.3
  57.7 0.0 copy-done.5
  57.7 0.0 copy-start.16
  57.8 1.1 copy-done.16
  58.9 4.0 %shard_map.214 = (f32[12,128,256]{2,1,0:T(8,128)}, bf16[12,128,256]{2,1,0:T(8,128)(2,1)}) custom-call(bf16[12,128,256]{2,1,0:T(8,128)(2,1)S(1)} %copy-done.16, bf16[12,192,128]{2,1,0:T(8,128)(2,1)S(1)} %bitcast.34, bf16[128,128]{1,0:T(8,128)(2,1)S(1)} %copy-done.5), custom_call_target="tpu_custom_call" | custom-call | flops 3000000000 | tf_op jit(solution)/shard_map/pallas_call | solution.py:126
  62.9 12.7 %all-to-all-done.2.refs_0_ = bf16[16,6,3,16,128]{4,3,2,1,0:T(8,128)(2,1)S(1)} async-done(((bf16[16,6,3,16,128]{4,3,2,1,0:T(8,128)(2,1)}), bf16[16,6,3,16,128]{4,3,2,1,0:T(8,128)(2,1)S(1)}, u32[]{:S(2)}, u32[]{:S(2)}) %all-to-all-start.2) | async-done | bytes 1179680 | tf_op jit(solution)/shard_map/all_to_all | solution.py:620
  75.6 2.8 %shard_map.213 = (bf16[16,3,3,16,128]{4,3,2,1,0:T(8,128)(2,1)}, bf16[8,192,256]{2,1,0:T(8,128)(2,1)}, bf16[8,192,256]{2,1,0:T(8,128)(2,1)}) custom-call(bf16[16,6,3,16,128]{4,3,2,1,0:T(8,128)(2,1)S(1)} %all-to-all-done.2.refs_0_), custom_call_target="tpu_custom_call" | custom-call | flops 3000000000 | tf_op jit(solution)/shard_map/pallas_call | solution.py:126
  78.3 0.0 copy-start.4
  78.3 0.0 copy-start.10
  78.4 15.2 %all_to_all.51.refs_0_ = bf16[16,3,3,16,128]{4,3,2,1,0:T(8,128)(2,1)S(1)} all-to-all(bf16[16,3,3,16,128]{4,3,2,1,0:T(8,128)(2,1)} %get-tuple-element.78), channel_id=1, replica_groups=mesh['dp'=8,'dap'=16] {'dap'}, dimensions={0} | all-to-all | bytes 1179648 | tf_op jit(solution)/shard_map/all_to_all | solution.py:620
  93.6 2.1 %shard_map.216 = bf16[16,3,3,16,128]{4,3,2,1,0:T(8,128)(2,1)} custom-call(bf16[16,3,3,16,128]{4,3,2,1,0:T(8,128)(2,1)S(1)} %all_to_all.51.refs_0_, f32[12,128,256]{2,1,0:T(8,128)S(1)} %copy-done.14, bf16[12,128,256]{2,1,0:T(8,128)(2,1)S(1)} %copy-done.15, f32[1,128]{1,0:T(1,128)S(1)} %bitcast.36, bf16[128,128]{1,0:T(8,128)(2,1)S(1)} %copy-done.4), custom_call_target="tpu_custom_call" | custom-call | flops 2000000000 | tf_op jit(solution)/shard_map/pallas_call | solution.py:126
  95.8 3.7 %all-to-all-start.4 = ((bf16[16,3,3,16,128]{4,3,2,1,0:T(8,128)(2,1)}), bf16[16,3,3,16,128]{4,3,2,1,0:T(8,128)(2,1)S(1)}, u32[]{:S(2)}, u32[]{:S(2)}) async-start(bf16[16,3,3,16,128]{4,3,2,1,0:T(8,128)(2,1)} %shard_map.216), calls=%async_computation.4 | async-start | bytes 1179648 | tf_op jit(solution)/shard_map/all_to_all | solution.py:620
  99.5 0.3 collective-permute-start.1
  99.8 0.8 copy.37.refs_8_
  100.6 10.5 %all-to-all-done.4.refs_0_ = bf16[16,3,3,16,128]{4,3,2,1,0:T(8,128)(2,1)S(1)} async-done(((bf16[16,3,3,16,128]{4,3,2,1,0:T(8,128)(2,1)}), bf16[16,3,3,16,128]{4,3,2,1,0:T(8,128)(2,1)S(1)}, u32[]{:S(2)}, u32[]{:S(2)}) %all-to-all-start.4) | async-done | bytes 589856 | tf_op jit(solution)/shard_map/all_to_all | solution.py:620
  111.0 3.5 %shard_map.217 = bf16[16,6,3,16,128]{4,3,2,1,0:T(8,128)(2,1)} custom-call(bf16[16,3,3,16,128]{4,3,2,1,0:T(8,128)(2,1)S(1)} %all-to-all-done.4.refs_0_, bf16[8,192,256]{2,1,0:T(8,128)(2,1)} %get-tuple-element.83.refs_1_, bf16[8,192,256]{2,1,0:T(8,128)(2,1)} %get-tuple-element.84.refs_2_), custom_call_target="tpu_custom_call" | custom-call | flops 4000000000 | tf_op jit(solution)/shard_map/pallas_call | solution.py:126
  114.5 3.7 %all-to-all-start.5 = ((bf16[16,6,3,16,128]{4,3,2,1,0:T(8,128)(2,1)}), bf16[16,6,3,16,128]{4,3,2,1,0:T(8,128)(2,1)S(1)}, u32[]{:S(2)}, u32[]{:S(2)}) async-start(bf16[16,6,3,16,128]{4,3,2,1,0:T(8,128)(2,1)} %shard_map.217), calls=%async_computation.5 | async-start | bytes 2359296 | tf_op jit(solution)/shard_map/all_to_all | solution.py:620
  118.2 6.6 %shard_map.215 = (bf16[12,192,128]{2,1,0:T(8,128)(2,1)}, bf16[12,128,256]{2,1,0:T(8,128)(2,1)}, f32[128,128]{1,0:T(8,128)S(1)}, f32[128,128]{1,0:T(8,128)S(1)}, f32[1,128]{1,0:T(1,128)S(1)}) custom-call(bf16[16,3,3,16,128]{4,3,2,1,0:T(8,128)(2,1)} %copy-done, f32[12,128,256]{2,1,0:T(8,128)} %get-tuple-element.79.refs_1_, ...), custom_call_target="tpu_custom_call" | custom-call | flops 6000000000 | tf_op jit(solution)/shard_map/pallas_call | solution.py:126
  124.8 0.0 copy-start.6
  124.9 0.0 copy-start.20
  124.9 0.0 collective-permute-done.1.refs_2_
  124.9 6.2 %shard_map.220 = (bf16[32,256,256]{2,1,0:T(8,128)(2,1)}, f32[12,64,256]{2,1,0:T(8,128)}, f32[12,1,256]{2,1,0:T(1,128)S(1)}) custom-call(s32[1]{0:T(128)} %bitcast.refs_0_, bf16[8,6,3,32,128]{4,3,2,1,0:T(8,128)(2,1)S(1)} %all-to-all-done.1.refs_1_, bf16[8,6,3,32,128]{4,3,2,1,0:T(8,128)(2,1)} %collective-permute-done.1.refs_2_, bf16[6,192,128]{2,1,0:T(8,128)(2,1)S(1)} %bitcast.30), custom_call_target="tpu_custom_call" | custom-call | flops 6000000000 | tf_op jit(solution)/shard_map/pallas_call | solution.py:126
  131.1 5.0 %all-to-all-done.5.refs_0_ = bf16[16,6,3,16,128]{4,3,2,1,0:T(8,128)(2,1)S(1)} async-done(((bf16[16,6,3,16,128]{4,3,2,1,0:T(8,128)(2,1)}), bf16[16,6,3,16,128]{4,3,2,1,0:T(8,128)(2,1)S(1)}, u32[]{:S(2)}, u32[]{:S(2)}) %all-to-all-start.5) | async-done | bytes 1179680 | tf_op jit(solution)/shard_map/all_to_all | solution.py:620
  136.1 0.0 copy-done.6
  136.1 5.6 %shard_map.218 = (bf16[12,192,128]{2,1,0:T(8,128)(2,1)}, bf16[12,128,256]{2,1,0:T(8,128)(2,1)}, bf16[2304,128]{1,0:T(8,128)(2,1)}, f32[512,128]{1,0:T(8,128)S(1)...) custom-call(bf16[16,6,3,16,128]{4,3,2,1,0:T(8,128)(2,1)S(1)} %all-to-all-done.5.refs_0_, ...), custom_call_target="tpu_custom_call" | custom-call | flops 8999999488 | tf_op jit(solution)/shard_map/pallas_call | solution.py:126
  141.6 0.0 copy-start.2
  141.7 3.9 %all-to-all-start.6 = ((bf16[16,144,128]{2,1,0:T(8,128)(2,1)}), bf16[16,144,128]{2,1,0:T(8,128)(2,1)S(1)}, u32[]{:S(2)}, u32[]{:S(2)}) async-start(bf16[16,144,128]{2,1,0:T(8,128)(2,1)} %bitcast.43), calls=%async_computation.6 | async-start | bytes 1179648 | tf_op jit(solution)/shard_map/all_to_all | solution.py:620
  145.6 0.0 copy-start.8
  145.6 0.0 copy-start.13
  145.6 7.3 %shard_map.219 = (f32[384,256]{1,0:T(8,128)S(1)}, bf16[2048,128]{1,0:T(8,128)(2,1)}) custom-call(bf16[12,128,256]{2,1,0:T(8,128)(2,1)S(1)} %copy-done.17, bf16[32,256,256]{2,1,0:T(8,128)(2,1)} %get-tuple-element.92.refs_1_, bf16[1024,128]{1,0:T(8,128)(2,1)S(1)} %bitcast.33, bf16[12,1024,256]{2,1,0:T(8,128)(2,1)} %get-tuple-element.93.refs_3_, ...), custom_call_target="tpu_custom_call" | custom-call | flops 10000000000 | tf_op jit(solution)/shard_map/pallas_call | solution.py:126
  152.9 0.0 copy-start.18
  152.9 0.7 copy-done.18
  153.6 3.3 %all-to-all-done.6.refs_0_ = bf16[16,144,128]{2,1,0:T(8,128)(2,1)S(1)} async-done(((bf16[16,144,128]{2,1,0:T(8,128)(2,1)}), bf16[16,144,128]{2,1,0:T(8,128)(2,1)S(1)}, u32[]{:S(2)}, u32[]{:S(2)}) %all-to-all-start.6) | async-done | bytes 589856 | tf_op jit(solution)/shard_map/all_to_all | solution.py:620
  156.9 3.6 %all-to-all-start.7 = ((bf16[16,128,128]{2,1,0:T(8,128)(2,1)}), bf16[16,128,128]{2,1,0:T(8,128)(2,1)S(1)}, u32[]{:S(2)}, u32[]{:S(2)}) async-start(bf16[16,128,128]{2,1,0:T(8,128)(2,1)} %bitcast.44), calls=%async_computation.7 | async-start | bytes 1048576 | tf_op jit(solution)/shard_map/all_to_all | solution.py:620
  160.5 6.2 %shard_map.221 = (bf16[6,192,128]{2,1,0:T(8,128)(2,1)}, bf16[32,128]{1,0:T(8,128)(2,1)S(1)}) custom-call(bf16[16,144,128]{2,1,0:T(8,128)(2,1)S(1)} %all-to-all-done.6.refs_0_, bf16[32,256,256]{2,1,0:T(8,128)(2,1)} %get-tuple-element.106.refs_1_, bf16[1024,128]{1,0:T(8,128)(2,1)S(1)} %copy-done.1, f32[384,256]{1,0:T(8,128)} %copy-done.18, ...), custom_call_target="tpu_custom_call" | custom-call | flops 8999999488 | tf_op jit(solution)/shard_map/pallas_call | solution.py:126
  166.7 4.6 %all-to-all-done.7 = bf16[16,128,128]{2,1,0:T(8,128)(2,1)S(1)} async-done(((bf16[16,128,128]{2,1,0:T(8,128)(2,1)}), bf16[16,128,128]{2,1,0:T(8,128)(2,1)S(1)}, u32[]{:S(2)}, u32[]{:S(2)}) %all-to-all-start.7) | async-done | bytes 524320 | tf_op jit(solution)/shard_map/all_to_all | solution.py:620
  171.3 0.1 reduce_sum.24
  171.5 16.4 %all_to_all.52 = bf16[8,160,128]{2,1,0:T(8,128)(2,1)S(1)} all-to-all(bf16[8,160,128]{2,1,0:T(8,128)(2,1)S(1)} %broadcast_in_dim.14), channel_id=1, replica_groups=mesh['dp'=8,'dap'=16] {'dp'}, dimensions={0} | all-to-all | bytes 655360 | tf_op jit(solution)/shard_map/all_to_all | solution.py:620
  187.9 0.9 broadcast_in_dim.15
  188.9 3.6 %all-to-all-start.9 = ((bf16[16,160,128]{2,1,0:T(8,128)(2,1)}), bf16[16,160,128]{2,1,0:T(8,128)(2,1)S(1)}, u32[]{:S(2)}, u32[]{:S(2)}) async-start(bf16[16,160,128]{2,1,0:T(8,128)(2,1)} %broadcast_in_dim.15), calls=%async_computation.9 | async-start | bytes 1310720 | tf_op jit(solution)/shard_map/all_to_all | solution.py:620
  192.5 0.9 copy.38
  193.4 11.3 %all-to-all-done.9.refs_0_ = bf16[16,160,128]{2,1,0:T(8,128)(2,1)S(1)} async-done(((bf16[16,160,128]{2,1,0:T(8,128)(2,1)}), bf16[16,160,128]{2,1,0:T(8,128)(2,1)S(1)}, u32[]{:S(2)}, u32[]{:S(2)}) %all-to-all-start.9) | async-done | bytes 655392 | tf_op jit(solution)/shard_map/all_to_all | solution.py:620
  204.7 1.3 shard_map.222
  (30 shorter events, 0.1 us)
Async XLA Ops:
  1.9 0.7 copy-start.7
  2.6 0.7 copy-start.12
  5.9 22.9 %copy-start.1 = (bf16[1024,128]{1,0:T(8,128)(2,1)S(1)}, bf16[1024,128]{1,0:T(8,128)(2,1)}, u32[]{:S(2)}) copy-start(bf16[1024,128]{1,0:T(8,128)(2,1)} %refs_2_.6) | copy-start | bytes 786436
  5.9 23.8 %copy-start.24 = (bf16[128,512]{1,0:T(8,128)(2,1)S(1)}, bf16[128,512]{1,0:T(8,128)(2,1)}, u32[]{:S(2)}) copy-start(bf16[128,512]{1,0:T(8,128)(2,1)} %param.20) | copy-start | bytes 393220
  28.8 1.7 copy-start.21
  28.8 5.4 %collective-permute-start = (bf16[8,6,3,32,128]{4,3,2,1,0:T(8,128)(2,1)S(1)}, bf16[8,6,3,32,128]{4,3,2,1,0:T(8,128)(2,1)}, u32[]{:S(2)}, u32[]{:S(2)}) collective-permute-start(bf16[8,6,3,32,128]{4,3,2,1,0:T(8,128)(2,1)S(1)} %all_to_all.50.refs_1_), channel_id=1, source_target_pairs={{0,1},{1,0},{2,3},{3,2},{4,5},{5,4},{6,7},{7,6},{8,9},{9,8},{10,11... | collective-permute-start | bytes 3538952 | tf_op jit(solution)/shard_map/ppermute | solution.py:665
  30.5 3.7 %copy-start.9 = (f32[128]{0:T(128)S(1)}, f32[128]{0:T(128)}, u32[]{:S(2)}) copy-start(f32[128]{0:T(128)} %param.18) | copy-start | bytes 1540
  30.5 3.7 %copy-start.11 = (f32[128]{0:T(128)S(1)}, f32[128]{0:T(128)}, u32[]{:S(2)}) copy-start(f32[128]{0:T(128)} %param.19) | copy-start | bytes 1540
  30.5 23.4 %all-to-all-start.1 = ((bf16[8,6,3,32,128]{4,3,2,1,0:T(8,128)(2,1)}), bf16[8,6,3,32,128]{4,3,2,1,0:T(8,128)(2,1)S(1)}, u32[]{:S(2)}, u32[]{:S(2)}) async-start(bf16[8,6,3,32,128]{4,3,2,1,0:T(8,128)(2,1)} %get-tuple-element.72), calls=%async_computation.1 | async-start | bytes 2359296 | tf_op jit(solution)/shard_map/all_to_all | solution.py:620
  47.6 0.6 copy-start.19
  53.9 3.8 %copy-start.3 = (bf16[1,12,192,128]{3,2,1,0:T(8,128)(2,1)S(1)}, bf16[1,12,192,128]{3,2,1,0:T(8,128)(2,1)}, u32[]{:S(2)}) copy-start(bf16[1,12,192,128]{3,2,1,0:T(8,128)(2,1)} %param.14) | copy-start | bytes 1769476
  53.9 3.9 %copy-start.5 = (bf16[128,128]{1,0:T(8,128)(2,1)S(1)}, bf16[128,128]{1,0:T(8,128)(2,1)}, u32[]{:S(2)}) copy-start(bf16[128,128]{1,0:T(8,128)(2,1)} %refs_9_.1) | copy-start | bytes 98308
  53.9 21.7 %all-to-all-start.2 = ((bf16[16,6,3,16,128]{4,3,2,1,0:T(8,128)(2,1)}), bf16[16,6,3,16,128]{4,3,2,1,0:T(8,128)(2,1)S(1)}, u32[]{:S(2)}, u32[]{:S(2)}) async-start(bf16[16,6,3,16,128]{4,3,2,1,0:T(8,128)(2,1)} %get-tuple-element.73), calls=%async_computation.2 | async-start | bytes 2359296 | tf_op jit(solution)/shard_map/all_to_all | solution.py:620
  57.7 1.1 copy-start.16
  75.6 18.0 %copy-start.14 = (f32[12,128,256]{2,1,0:T(8,128)S(1)}, f32[12,128,256]{2,1,0:T(8,128)}, u32[]{:S(2)}) copy-start(f32[12,128,256]{2,1,0:T(8,128)} %get-tuple-element.80.refs_3_.refs_1_) | copy-start | bytes 4718596
  78.3 15.3 %copy-start.4 = (bf16[128,128]{1,0:T(8,128)(2,1)S(1)}, bf16[128,128]{1,0:T(8,128)(2,1)}, u32[]{:S(2)}) copy-start(bf16[128,128]{1,0:T(8,128)(2,1)} %refs_4_.1) | copy-start | bytes 98308
  78.3 15.3 %copy-start.10 = (f32[128]{0:T(128)S(1)}, f32[128]{0:T(128)}, u32[]{:S(2)}) copy-start(f32[128]{0:T(128)} %param.22) | copy-start | bytes 1540
  78.4 15.3 %copy-start.15 = (bf16[12,128,256]{2,1,0:T(8,128)(2,1)S(1)}, bf16[12,128,256]{2,1,0:T(8,128)(2,1)}, u32[]{:S(2)}) copy-start(bf16[12,128,256]{2,1,0:T(8,128)(2,1)} %get-tuple-element.81.refs_4_.refs_2_) | copy-start | bytes 2359300
  93.6 2.1 %copy-start = (bf16[16,3,3,16,128]{4,3,2,1,0:T(8,128)(2,1)}, bf16[16,3,3,16,128]{4,3,2,1,0:T(8,128)(2,1)S(1)}, u32[]{:S(2)}) copy-start(bf16[16,3,3,16,128]{4,3,2,1,0:T(8,128)(2,1)S(1)} %all_to_all.51.refs_0_) | copy-start | bytes 1769476
  95.8 4.0 %copy-start.22 = (bf16[128,2,16,2,8]{0,4,3,2,1:T(8,128)(2,1)S(1)}, bf16[128,2,16,2,8]{0,4,3,2,1:T(8,128)(2,1)}, u32[]{:S(2)}) copy-start(bf16[128,2,16,2,8]{0,4,3,2,1:T(8,128)(2,1)} %copy.36) | copy-start | bytes 393220
  95.8 15.2 %all-to-all-start.4 = ((bf16[16,3,3,16,128]{4,3,2,1,0:T(8,128)(2,1)}), bf16[16,3,3,16,128]{4,3,2,1,0:T(8,128)(2,1)S(1)}, u32[]{:S(2)}, u32[]{:S(2)}) async-start(bf16[16,3,3,16,128]{4,3,2,1,0:T(8,128)(2,1)} %shard_map.216), calls=%async_computation.4 | async-start | bytes 1179648 | tf_op jit(solution)/shard_map/all_to_all | solution.py:620
  99.5 25.4 %collective-permute-start.1 = (bf16[8,6,3,32,128]{4,3,2,1,0:T(8,128)(2,1)S(1)}, bf16[8,6,3,32,128]{4,3,2,1,0:T(8,128)(2,1)}, u32[]{:S(2)}, u32[]{:S(2)}) collective-permute-start(bf16[8,6,3,32,128]{4,3,2,1,0:T(8,128)(2,1)S(1)} %all-to-all-done.1.refs_1_), channel_id=1, source_target_pairs={{0,1},{1,0},{2,3},{3,2},{4,5},{5,4},{6,7},{7,6},{8,9},{9,8},{10,11... | collective-permute-start | bytes 3538952 | tf_op jit(solution)/shard_map/ppermute | solution.py:665
  114.5 21.6 %all-to-all-start.5 = ((bf16[16,6,3,16,128]{4,3,2,1,0:T(8,128)(2,1)}), bf16[16,6,3,16,128]{4,3,2,1,0:T(8,128)(2,1)S(1)}, u32[]{:S(2)}, u32[]{:S(2)}) async-start(bf16[16,6,3,16,128]{4,3,2,1,0:T(8,128)(2,1)} %shard_map.217), calls=%async_computation.5 | async-start | bytes 2359296 | tf_op jit(solution)/shard_map/all_to_all | solution.py:620
  124.8 11.2 %copy-start.6 = (bf16[128,128]{1,0:T(8,128)(2,1)S(1)}, bf16[128,128]{1,0:T(8,128)(2,1)}, u32[]{:S(2)}) copy-start(bf16[128,128]{1,0:T(8,128)(2,1)} %refs_9_.1) | copy-start | bytes 98308
  124.9 11.2 %copy-start.20 = (f32[12,1,256]{2,1,0:T(1,128)S(1)}, f32[12,1,256]{2,1,0:T(1,128)}, u32[]{:S(2)}) copy-start(f32[12,1,256]{2,1,0:T(1,128)} %copy-done.19) | copy-start | bytes 36868
  141.6 3.9 %copy-start.2 = (bf16[32,32,128]{2,0,1:T(8,128)(2,1)S(1)}, bf16[32,32,128]{2,0,1:T(8,128)(2,1)}, u32[]{:S(2)}) copy-start(bf16[32,32,128]{2,0,1:T(8,128)(2,1)} %copy.34) | copy-start | bytes 786436
  141.6 3.9 %copy-start.17 = (bf16[12,128,256]{2,1,0:T(8,128)(2,1)S(1)}, bf16[12,128,256]{2,1,0:T(8,128)(2,1)}, u32[]{:S(2)}) copy-start(bf16[12,128,256]{2,1,0:T(8,128)(2,1)} %get-tuple-element.91.refs_0_) | copy-start | bytes 2359300
  141.7 15.3 %all-to-all-start.6 = ((bf16[16,144,128]{2,1,0:T(8,128)(2,1)}), bf16[16,144,128]{2,1,0:T(8,128)(2,1)S(1)}, u32[]{:S(2)}, u32[]{:S(2)}) async-start(bf16[16,144,128]{2,1,0:T(8,128)(2,1)} %bitcast.43), calls=%async_computation.6 | async-start | bytes 1179648 | tf_op jit(solution)/shard_map/all_to_all | solution.py:620
  145.6 14.9 %copy-start.8 = (bf16[64,64]{1,0:T(8,128)(2,1)S(1)}, bf16[64,64]{1,0:T(8,128)(2,1)}, u32[]{:S(2)}) copy-start(bf16[64,64]{1,0:T(8,128)(2,1)} %refs_2_.7) | copy-start | bytes 24580
  145.6 14.9 %copy-start.13 = (f32[64]{0:T(128)S(1)}, f32[64]{0:T(128)}, u32[]{:S(2)}) copy-start(f32[64]{0:T(128)} %param.15) | copy-start | bytes 772
  152.9 0.7 copy-start.18
  156.9 14.4 %all-to-all-start.7 = ((bf16[16,128,128]{2,1,0:T(8,128)(2,1)}), bf16[16,128,128]{2,1,0:T(8,128)(2,1)S(1)}, u32[]{:S(2)}, u32[]{:S(2)}) async-start(bf16[16,128,128]{2,1,0:T(8,128)(2,1)} %bitcast.44), calls=%async_computation.7 | async-start | bytes 1048576 | tf_op jit(solution)/shard_map/all_to_all | solution.py:620
  187.9 4.6 %copy-start.23 = (bf16[6,192,128]{2,1,0:T(8,128)(2,1)S(1)}, bf16[6,192,128]{2,1,0:T(8,128)(2,1)}, u32[]{:S(2)}) copy-start(bf16[6,192,128]{2,1,0:T(8,128)(2,1)} %get-tuple-element.110) | copy-start | bytes 884740
  188.9 15.8 %all-to-all-start.9 = ((bf16[16,160,128]{2,1,0:T(8,128)(2,1)}), bf16[16,160,128]{2,1,0:T(8,128)(2,1)S(1)}, u32[]{:S(2)}, u32[]{:S(2)}) async-start(bf16[16,160,128]{2,1,0:T(8,128)(2,1)} %broadcast_in_dim.15), calls=%async_computation.9 | async-start | bytes 1310720 | tf_op jit(solution)/shard_map/all_to_all | solution.py:620
